TPU v7x, 32 devices: a whole 2x2x4 slice. The times are simulated.
32 devices in a mesh: wide: 8 (over y, x, core), section: 4 (over z).
Axes of the slice: x: 2, y: 2, z: 4, core: 2. Of those that a mesh axis runs over, the one named last changes fastest.
Arguments:
- inputs: float32 [16, 64, 64, 512], P('wide', 'section'), may hold values from -6 to 6
- norm_gain: float32 [2, 2, 512], replicated, may hold values from 0.5 to 1.5
- norm_bias: float32 [2, 2, 512], replicated, may hold values from -2 to 2
- mix_weight: float32 [2, 2, 2, 4, 128, 128], replicated, may hold values from -0.375 to 0.375
- mix_bias: float32 [2, 2, 2, 4, 128], replicated, may hold values from -2 to 2
- up_weight: float32 [2, 512, 512], replicated, may hold values from -0.25 to 0.25
- up_bias: float32 [2, 512], replicated, may hold values from -2 to 2
- down_weight: float32 [2, 512, 512], replicated, may hold values from -0.25 to 0.25
- down_bias: float32 [2, 512], replicated, may hold values from -2 to 2
- out_grad: float32 [16, 64, 64, 512], P('wide', 'section'), may hold values from -6 to 6
Outputs:
- outputs: float32 [16, 64, 64, 512], P('wide', 'section')
- input_grad: float32 [16, 64, 64, 512], P('wide', 'section')
- gain_grad: float32 [2, 2, 512], replicated
- bias_grad: float32 [2, 2, 512], replicated
- mix_weight_grad: float32 [2, 2, 2, 4, 128, 128], replicated
- mix_bias_grad: float32 [2, 2, 2, 4, 128], replicated
- up_weight_grad: float32 [2, 512, 512], replicated
- up_bias_grad: float32 [2, 512], replicated
- down_weight_grad: float32 [2, 512, 512], replicated
- down_bias_grad: float32 [2, 512], replicated
All inputs are finite; a program needn't handle non-finite values.
Results may differ from a plain program's by a relative error of at most 0.0002.
Values sent between devices are 32-bit elements; how exact they have to be, the bound alone decides.
No kernel may reach another device: no remote copies, remote signals or barrier semaphores. Data moves between devices by JAX's collectives and lax.ppermute only.
A program may use at most 320 MiB of HBM per device.

v0:
```python
import math

import jax
import jax.numpy as jnp
from jax import lax
from jax.sharding import PartitionSpec as P

BLOCKS = 4
GRID = 64
MODES = 32


EPSILON = 1e-05
THRESHOLD = 0.05
PRECISE = lax.Precision.HIGHEST


def from_partner(shard, axis, apart):
    return lax.ppermute(shard, axis, [(i, i ^ 1 << apart) for i in range(lax.axis_size(axis))])


def shifted(shard, axis, by):
    length = lax.axis_size(axis)
    pairs = [(i, i + by) for i in range(length) if 0 <= i + by < length]
    return lax.ppermute(shard, axis, pairs)


def layer_norm(values, gains, biases):
    average = jnp.mean(values, axis=-1, keepdims=True)
    centered = values - average
    variance = jnp.mean(centered * centered, axis=-1, keepdims=True)
    return centered * lax.rsqrt(variance + EPSILON) * gains + biases


def phase_tables(frequency, places):
    product = frequency[:, None] * places[None, :] % GRID
    angles = product.astype(jnp.float32) * (2.0 * math.pi / GRID)
    return (jnp.cos(angles), jnp.sin(angles))


def row_frequencies():
    index_list = jnp.arange(MODES)
    return jnp.where(index_list < MODES // 2, index_list, index_list + GRID - MODES)


def complex_mix(real_in, imag_in, weights, offsets):
    real_out = (
        jnp.einsum("jkbi,bio->jkbo", real_in, weights[0], precision=PRECISE)
        - jnp.einsum("jkbi,bio->jkbo", imag_in, weights[1], precision=PRECISE)
        + offsets[0]
    )
    imag_out = (
        jnp.einsum("jkbi,bio->jkbo", real_in, weights[1], precision=PRECISE)
        + jnp.einsum("jkbi,bio->jkbo", imag_in, weights[0], precision=PRECISE)
        + offsets[1]
    )
    return (real_out, imag_out)


def shrink(values):
    return values - THRESHOLD * jnp.tanh(values / THRESHOLD)


def column_modes(rows_in, parameters, half_pos):
    normed = layer_norm(rows_in, parameters[0][0], parameters[1][0])
    cosine_table, sine_table = phase_tables(jnp.arange(MODES), jnp.arange(GRID))
    real_part = jnp.einsum("hwd,kw->hkd", normed, cosine_table, precision=PRECISE)
    imag_part = -jnp.einsum("hwd,kw->hkd", normed, sine_table, precision=PRECISE)
    stacked = jnp.stack([real_part, imag_part])
    half_width = MODES // 2
    held_modes = lax.dynamic_slice_in_dim(stacked, half_pos * half_width, half_width, 2)
    sent_modes = lax.dynamic_slice_in_dim(stacked, (1 - half_pos) * half_width, half_width, 2)
    return (held_modes, sent_modes)


def analyse_rows(cosine_table, sine_table, source):
    real_part = jnp.einsum("jr,rkd->jkd", cosine_table, source[0], precision=PRECISE) + jnp.einsum(
        "jr,rkd->jkd", sine_table, source[1], precision=PRECISE
    )
    imag_part = jnp.einsum("jr,rkd->jkd", cosine_table, source[1], precision=PRECISE) - jnp.einsum(
        "jr,rkd->jkd", sine_table, source[0], precision=PRECISE
    )
    return (real_part, imag_part)


def synthesise_rows(cosine_table, sine_table, real_part, imag_part):
    real_rows = jnp.einsum("jr,jkd->rkd", cosine_table, real_part, precision=PRECISE) - jnp.einsum(
        "jr,jkd->rkd", sine_table, imag_part, precision=PRECISE
    )
    imag_rows = jnp.einsum("jr,jkd->rkd", cosine_table, imag_part, precision=PRECISE) + jnp.einsum(
        "jr,jkd->rkd", sine_table, real_part, precision=PRECISE
    )
    return jnp.stack([real_rows, imag_rows])


def mode_mixing(held_modes, taken_modes, parameters, half_pos):
    row_count = held_modes.shape[1]
    own_cos, own_sin = phase_tables(row_frequencies(), half_pos * row_count + jnp.arange(row_count))
    other_cos, other_sin = phase_tables(
        row_frequencies(), (1 - half_pos) * row_count + jnp.arange(row_count)
    )
    own_real, own_imag = analyse_rows(own_cos, own_sin, held_modes)
    other_real, other_imag = analyse_rows(other_cos, other_sin, taken_modes)
    real_in = (own_real + other_real) / GRID
    imag_in = (own_imag + other_imag) / GRID
    mode_shape = real_in.shape
    block_shape = mode_shape[:2] + (BLOCKS, mode_shape[2] // BLOCKS)
    hidden_real, hidden_imag = complex_mix(
        real_in.reshape(block_shape),
        imag_in.reshape(block_shape),
        parameters[2][0],
        parameters[3][0],
    )
    hidden_real = jax.nn.gelu(hidden_real, approximate=False)
    hidden_imag = jax.nn.gelu(hidden_imag, approximate=False)
    out_real, out_imag = complex_mix(hidden_real, hidden_imag, parameters[2][1], parameters[3][1])
    out_real = shrink(out_real).reshape(mode_shape)
    out_imag = shrink(out_imag).reshape(mode_shape)
    held_rows = synthesise_rows(own_cos, own_sin, out_real, out_imag)
    sent_rows = synthesise_rows(other_cos, other_sin, out_real, out_imag)
    return (held_rows, sent_rows)


def column_synthesis(source, first_mode):
    frequency = first_mode + jnp.arange(MODES // 2)
    cosine_table, sine_table = phase_tables(frequency, jnp.arange(GRID))
    factor = jnp.where(frequency == 0, 1.0, 2.0).astype(jnp.float32)[:, None]
    real_cells = jnp.einsum("hkd,kw->hwd", source[0], cosine_table * factor, precision=PRECISE)
    imag_cells = jnp.einsum("hkd,kw->hwd", source[1], sine_table * factor, precision=PRECISE)
    return (real_cells - imag_cells) / GRID


def rows_out(held_rows, taken_rows, rows_in, parameters, half_pos):
    half_width = MODES // 2
    spatial = column_synthesis(held_rows, half_pos * half_width) + column_synthesis(
        taken_rows, (1 - half_pos) * half_width
    )
    mixed = rows_in + spatial
    second = layer_norm(mixed, parameters[0][1], parameters[1][1]).reshape(-1, mixed.shape[-1])
    hidden = jax.nn.gelu(
        jnp.dot(second, parameters[4], precision=PRECISE, preferred_element_type=jnp.float32)
        + parameters[5],
        approximate=False,
    )
    branch = (
        jnp.dot(hidden, parameters[6], precision=PRECISE, preferred_element_type=jnp.float32)
        + parameters[7]
    )
    return mixed + branch.reshape(mixed.shape)


def flip_forward(values):
    return from_partner(values, "section", 1)


def flip_backward(values):
    return from_partner(values, "section", 1)


def layer_forward(rows_in, parameters, half_pos):
    held_modes, sent_modes = column_modes(rows_in, parameters, half_pos)
    taken_modes = flip_forward(sent_modes)
    held_rows, sent_rows = mode_mixing(held_modes, taken_modes, parameters, half_pos)
    taken_rows = flip_forward(sent_rows)
    result = rows_out(held_rows, taken_rows, rows_in, parameters, half_pos)
    return (result, (held_modes, taken_modes, held_rows, taken_rows))


def add_trees(first_tree, second_tree):
    return jax.tree.map(jnp.add, first_tree, second_tree)


def layer_backward(rows_in, saved_state, parameters, half_pos, grad_out):
    held_modes, taken_modes, held_rows, taken_rows = saved_state

    def third_piece(held_part, taken_part, rows_part, param_part):
        return rows_out(held_part, taken_part, rows_part, param_part, half_pos)

    def second_piece(held_part, taken_part, param_part):
        return mode_mixing(held_part, taken_part, param_part, half_pos)

    def first_piece(rows_part, param_part):
        return column_modes(rows_part, param_part, half_pos)

    _, pull_third = jax.vjp(third_piece, held_rows, taken_rows, rows_in, parameters)
    grad_held_rows, grad_taken_rows, grad_rows_late, grad_params_late = pull_third(grad_out)
    grad_sent_rows = flip_backward(grad_taken_rows)
    _, pull_second = jax.vjp(second_piece, held_modes, taken_modes, parameters)
    grad_held_modes, grad_taken_modes, grad_params_mid = pull_second(
        (grad_held_rows, grad_sent_rows)
    )
    grad_sent_modes = flip_backward(grad_taken_modes)
    _, pull_first = jax.vjp(first_piece, rows_in, parameters)
    grad_rows_early, grad_params_early = pull_first((grad_held_modes, grad_sent_modes))
    grad_params = add_trees(add_trees(grad_params_late, grad_params_mid), grad_params_early)
    return (grad_rows_late + grad_rows_early, grad_params)


def on_device(
    inputs,
    norm_gain,
    norm_bias,
    mix_weight,
    mix_bias,
    up_weight,
    up_bias,
    down_weight,
    down_bias,
    out_grad,
):
    micro_count = inputs.shape[0]
    quarter = inputs.shape[1]
    section_pos = lax.axis_index("section")
    layer_pos = section_pos % 2
    half_pos = section_pos // 2
    weights_all = (
        norm_gain,
        norm_bias,
        mix_weight,
        mix_bias,
        up_weight,
        up_bias,
        down_weight,
        down_bias,
    )
    own_params = tuple(
        (lax.dynamic_index_in_dim(weight, layer_pos, 0, keepdims=False) for weight in weights_all)
    )
    below = shifted(inputs, "section", -1)
    first_rows = jnp.concatenate([inputs, below], axis=1)
    above = shifted(out_grad, "section", 1)
    last_rows = jnp.concatenate([above, out_grad], axis=1)

    def forward_step(carried, step_index):
        fresh_index = jnp.minimum(step_index, micro_count - 1)
        fresh_rows = lax.dynamic_index_in_dim(first_rows, fresh_index, 0, keepdims=False)
        rows_in = jnp.where(layer_pos == 0, fresh_rows, carried)
        result, saved_state = layer_forward(rows_in, own_params, half_pos)
        passed = shifted(result, "section", 1)
        return (passed, (rows_in, saved_state, result))

    initial = jnp.zeros_like(first_rows[0])
    _, (stash_rows, stash_saved, results) = lax.scan(
        forward_step, initial, jnp.arange(micro_count + 1)
    )
    finals = results[1:]
    borrowed = shifted(finals[:, :quarter], "section", -1)
    outputs = jnp.where(layer_pos == 1, finals[:, quarter:], borrowed)
    zero_grads = jax.tree.map(jnp.zeros_like, own_params)

    def backward_step(carried, step_index):
        incoming, totals = carried
        target = jnp.where(layer_pos == 1, micro_count - 1 - step_index, micro_count - step_index)
        active = (target >= 0) & (target < micro_count)
        target = jnp.clip(target, 0, micro_count - 1)
        fresh_rows = lax.dynamic_index_in_dim(last_rows, target, 0, keepdims=False)
        grad_out = jnp.where(layer_pos == 1, fresh_rows, incoming)
        slot_index = target + layer_pos
        rows_in = lax.dynamic_index_in_dim(stash_rows, slot_index, 0, keepdims=False)

        def pick_slot(stacked):
            return lax.dynamic_index_in_dim(stacked, slot_index, 0, keepdims=False)

        saved_state = jax.tree.map(pick_slot, stash_saved)
        grad_rows, grad_params = layer_backward(
            rows_in, saved_state, own_params, half_pos, grad_out
        )

        def accumulate(running, addend):
            return running + jnp.where(active, addend, jnp.zeros_like(addend))

        totals = jax.tree.map(accumulate, totals, grad_params)
        passed = shifted(grad_rows, "section", -1)
        return ((passed, totals), grad_rows)

    (_, totals), grads_rows = lax.scan(
        backward_step, (initial, zero_grads), jnp.arange(micro_count + 1)
    )
    own_grads = grads_rows[::-1][:micro_count]
    lent_rows = shifted(own_grads[:, quarter:], "section", 1)
    input_grad = jnp.where(layer_pos == 0, own_grads[:, :quarter], lent_rows)
    slots = jnp.arange(2)

    def place(running):
        slot_mask = (slots == layer_pos).reshape((2,) + (1,) * running.ndim)
        return jnp.where(slot_mask, running[None], jnp.zeros_like(running[None]))

    padded = tuple((place(running) for running in totals))
    summed = lax.psum(
        (padded[0], padded[1], padded[2], padded[3], padded[4], padded[5], padded[6], padded[7]),
        ("wide", "section"),
    )
    return (
        outputs,
        input_grad,
        summed[0],
        summed[1],
        summed[2],
        summed[3],
        summed[4],
        summed[5],
        summed[6],
        summed[7],
    )


def solution(mesh):
    return jax.shard_map(
        on_device,
        mesh=mesh,
        in_specs=(
            P("wide", "section", None, None),
            P(),
            P(),
            P(),
            P(),
            P(),
            P(),
            P(),
            P(),
            P("wide", "section", None, None),
        ),
        out_specs=(
            P("wide", "section", None, None),
            P("wide", "section", None, None),
            P(),
            P(),
            P(),
            P(),
            P(),
            P(),
            P(),
            P(),
        ),
        check_vma=False,
    )
```

profile of v0, /device:TPU:0, one launch (start us, length us, event | category | flops | bytes accessed | tf_op | source)
XLA Modules:
  0.0 2841.5 jit_solution(10924870955061290293)
XLA Ops:
  8.7 7.7 collective-permute-start.8
  22.6 80.5 %collective-permute-done.6 = f32[2,16,64,512]{3,2,1,0:T(8,128)} collective-permute-done((f32[2,16,64,512]{3,2,1,0:T(8,128)}, f32[2,16,64,512]{3,2,1,0:T(8,128)}, u32[]{:S(2)}, u32[]{:S(2)}) %collective-permute-start.6) | collective-permute-done | bytes 4194336 | tf_op jit(solution)/shard_map/ppermute | solution.py:25
  103.2 7.1 pad_maximum_fusion.1
  110.3 6.8 pad_maximum_fusion.2
  117.1 6.2 broadcast.2480.clone
  123.3 6.2 broadcast.2480.clone.1
  132.1 1150.1 %while.59 = (s32[]{:T(128)}, f32[32,64,512]{2,1,0:T(8,128)}, f32[3,32,64,512]{3,2,1,0:T(8,128)}, f32[3,2,32,16,512]{4,3,2,1,0:T(8,128)}, f32[3,2,32,16,512]{4,3,...) while((s32[]{:T(128)}, f32[32,64,512]{2,1,0:T(8,128)}, ...), condition=%wide.region_5.6_spmd, body=%wide.region_0.5_spmd.sunk | while | flops 19468214272 | bytes 394492992 | solution.py:243
  133.9 7.4 bitcast_dynamic-update-slice_fusion.12
  166.2 80.0 %collective-permute-done = f32[2,32,16,512]{3,2,1,0:T(8,128)S(1)} collective-permute-done((f32[2,32,16,512]{3,2,1,0:T(8,128)S(1)}, f32[2,32,16,512]{3,2,1,0:T(8,128)S(1)}, u32[]{:S(2)}, u32[]{:S(2)}) %collective-permute-start) | collective-permute-done | bytes 2097184 | tf_op jit(solution)/shard_map/while/body/eval_jaxpr/ppermute | solution.py:19
  304.1 79.1 %collective-permute-done.1 = f32[2,32,16,512]{3,1,2,0:T(8,128)S(1)} collective-permute-done((f32[2,32,16,512]{3,1,2,0:T(8,128)S(1)}, f32[2,32,16,512]{3,1,2,0:T(8,128)S(1)}, u32[]{:S(2)}, u32[]{:S(2)}) %collective-permute-start.1) | collective-permute-done | bytes 2097184 | tf_op jit(solution)/shard_map/while/body/eval_jaxpr/ppermute | solution.py:19
  394.9 7.5 fusion.1289
  402.5 16.8 fusion.1290
  432.7 82.0 %collective-permute-done.2 = f32[32,64,512]{2,1,0:T(8,128)} collective-permute-done((f32[32,64,512]{2,1,0:T(8,128)}, f32[32,64,512]{2,1,0:T(8,128)}, u32[]{:S(2)}, u32[]{:S(2)}) %collective-permute-start.2) | collective-permute-done | bytes 4194336 | tf_op jit(solution)/shard_map/while/body/eval_jaxpr/ppermute | solution.py:25
  516.3 7.5 bitcast_dynamic-update-slice_fusion.12
  549.1 80.0 %collective-permute-done = f32[2,32,16,512]{3,2,1,0:T(8,128)S(1)} collective-permute-done((f32[2,32,16,512]{3,2,1,0:T(8,128)S(1)}, f32[2,32,16,512]{3,2,1,0:T(8,128)S(1)}, u32[]{:S(2)}, u32[]{:S(2)}) %collective-permute-start) | collective-permute-done | bytes 2097184 | tf_op jit(solution)/shard_map/while/body/eval_jaxpr/ppermute | solution.py:19
  687.0 79.3 %collective-permute-done.1 = f32[2,32,16,512]{3,1,2,0:T(8,128)S(1)} collective-permute-done((f32[2,32,16,512]{3,1,2,0:T(8,128)S(1)}, f32[2,32,16,512]{3,1,2,0:T(8,128)S(1)}, u32[]{:S(2)}, u32[]{:S(2)}) %collective-permute-start.1) | collective-permute-done | bytes 2097184 | tf_op jit(solution)/shard_map/while/body/eval_jaxpr/ppermute | solution.py:19
  778.0 7.5 fusion.1289
  785.5 16.8 fusion.1290
  815.6 81.8 %collective-permute-done.2 = f32[32,64,512]{2,1,0:T(8,128)} collective-permute-done((f32[32,64,512]{2,1,0:T(8,128)}, f32[32,64,512]{2,1,0:T(8,128)}, u32[]{:S(2)}, u32[]{:S(2)}) %collective-permute-start.2) | collective-permute-done | bytes 4194336 | tf_op jit(solution)/shard_map/while/body/eval_jaxpr/ppermute | solution.py:25
  899.0 7.5 bitcast_dynamic-update-slice_fusion.12
  932.0 80.0 %collective-permute-done = f32[2,32,16,512]{3,2,1,0:T(8,128)S(1)} collective-permute-done((f32[2,32,16,512]{3,2,1,0:T(8,128)S(1)}, f32[2,32,16,512]{3,2,1,0:T(8,128)S(1)}, u32[]{:S(2)}, u32[]{:S(2)}) %collective-permute-start) | collective-permute-done | bytes 2097184 | tf_op jit(solution)/shard_map/while/body/eval_jaxpr/ppermute | solution.py:19
  1069.9 79.3 %collective-permute-done.1 = f32[2,32,16,512]{3,1,2,0:T(8,128)S(1)} collective-permute-done((f32[2,32,16,512]{3,1,2,0:T(8,128)S(1)}, f32[2,32,16,512]{3,1,2,0:T(8,128)S(1)}, u32[]{:S(2)}, u32[]{:S(2)}) %collective-permute-start.1) | collective-permute-done | bytes 2097184 | tf_op jit(solution)/shard_map/while/body/eval_jaxpr/ppermute | solution.py:19
  1160.9 7.5 fusion.1289
  1168.4 16.8 fusion.1290
  1198.6 81.7 %collective-permute-done.2 = f32[32,64,512]{2,1,0:T(8,128)} collective-permute-done((f32[32,64,512]{2,1,0:T(8,128)}, f32[32,64,512]{2,1,0:T(8,128)}, u32[]{:S(2)}, u32[]{:S(2)}) %collective-permute-start.2) | collective-permute-done | bytes 4194336 | tf_op jit(solution)/shard_map/while/body/eval_jaxpr/ppermute | solution.py:25
  1282.8 6.2 broadcast.2480
  1291.6 1320.2 %while.60 = (s32[]{:T(128)}, f32[32,64,512]{2,1,0:T(8,128)}, f32[2,512]{1,0:T(2,128)}, f32[2,512]{1,0:T(2,128)}, f32[2,2,4,128,128]{4,3,2,1,0:T(8,128)}, /*index...) while((s32[]{:T(128)}, f32[32,64,512]{2,1,0:T(8,128)}, ...), condition=%wide.region_25.26_spmd.clone, body=%wide.region_6.25_spmd.clone.sunk | while | flops 46963666944 | bytes 900441664 | solution.py:276
  1309.4 7.2 fusion.1397
  1318.3 7.2 fusion.1400
  1330.8 27.1 fusion.1401
  1357.9 7.4 fusion.1402
  1428.6 6.7 bitcast_multiply_fusion.27
  1444.6 24.5 collective-permute-done.3
  1531.4 11.2 fusion.1442
  1548.3 71.6 %collective-permute-done.4 = f32[2,32,16,512]{3,1,2,0:T(8,128)} collective-permute-done((f32[2,32,16,512]{3,1,2,0:T(8,128)}, f32[2,32,16,512]{3,1,2,0:T(8,128)}, u32[]{:S(2)}, u32[]{:S(2)}) %collective-permute-start.4) | collective-permute-done | bytes 2097184 | tf_op jit(solution)/shard_map/while/body/eval_jaxpr/ppermute | solution.py:19
  1629.6 7.1 multiply_reduce_fusion.18
  1647.0 7.3 fusion.1441
  1681.6 58.6 %collective-permute-done.5 = f32[32,64,512]{2,1,0:T(8,128)} collective-permute-done((f32[32,64,512]{2,1,0:T(8,128)}, f32[32,64,512]{2,1,0:T(8,128)}, u32[]{:S(2)}, u32[]{:S(2)}) %collective-permute-start.5) | collective-permute-done | bytes 4194336 | tf_op jit(solution)/shard_map/while/body/eval_jaxpr/ppermute | solution.py:25
  1758.0 7.1 fusion.1397
  1766.8 7.2 fusion.1400
  1779.3 17.8 fusion.1401
  1797.2 7.4 fusion.1402
  1864.7 6.7 bitcast_multiply_fusion.27
  1880.8 23.9 collective-permute-done.3
  1966.9 11.3 fusion.1442
  1983.9 69.1 %collective-permute-done.4 = f32[2,32,16,512]{3,1,2,0:T(8,128)} collective-permute-done((f32[2,32,16,512]{3,1,2,0:T(8,128)}, f32[2,32,16,512]{3,1,2,0:T(8,128)}, u32[]{:S(2)}, u32[]{:S(2)}) %collective-permute-start.4) | collective-permute-done | bytes 2097184 | tf_op jit(solution)/shard_map/while/body/eval_jaxpr/ppermute | solution.py:19
  2062.8 7.1 multiply_reduce_fusion.18
  2080.2 7.3 fusion.1441
  2116.0 57.4 %collective-permute-done.5 = f32[32,64,512]{2,1,0:T(8,128)} collective-permute-done((f32[32,64,512]{2,1,0:T(8,128)}, f32[32,64,512]{2,1,0:T(8,128)}, u32[]{:S(2)}, u32[]{:S(2)}) %collective-permute-start.5) | collective-permute-done | bytes 4194336 | tf_op jit(solution)/shard_map/while/body/eval_jaxpr/ppermute | solution.py:25
  2191.2 7.1 fusion.1397
  2200.0 7.2 fusion.1400
  2212.5 17.8 fusion.1401
  2230.3 7.4 fusion.1402
  2297.5 6.7 bitcast_multiply_fusion.27
  2313.5 24.4 collective-permute-done.3
  2400.1 11.3 fusion.1442
  2417.1 69.4 %collective-permute-done.4 = f32[2,32,16,512]{3,1,2,0:T(8,128)} collective-permute-done((f32[2,32,16,512]{3,1,2,0:T(8,128)}, f32[2,32,16,512]{3,1,2,0:T(8,128)}, u32[]{:S(2)}, u32[]{:S(2)}) %collective-permute-start.4) | collective-permute-done | bytes 2097184 | tf_op jit(solution)/shard_map/while/body/eval_jaxpr/ppermute | solution.py:19
  2496.3 7.1 multiply_reduce_fusion.18
  2513.7 7.3 fusion.1441
  2549.4 57.4 %collective-permute-done.5 = f32[32,64,512]{2,1,0:T(8,128)} collective-permute-done((f32[32,64,512]{2,1,0:T(8,128)}, f32[32,64,512]{2,1,0:T(8,128)}, u32[]{:S(2)}, u32[]{:S(2)}) %collective-permute-start.5) | collective-permute-done | bytes 4194336 | tf_op jit(solution)/shard_map/while/body/eval_jaxpr/ppermute | solution.py:25
  2611.8 8.7 fusion.920
  2641.8 148.8 %all-reduce.32 = (f32[2,2,512]{2,1,0:T(2,128)}, f32[2,2,512]{2,1,0:T(2,128)}, f32[2,2,2,4,128]{4,3,2,1,0:T(4,128)}, f32[2,512]{1,0:T(2,128)}, f32[2,512]{1,0:T(2,128)}) all-reduce(f32[2,2,512]{2,1,0:T(2,128)S(1)} %get-tuple-element.1541, ...), channel_id=1, replica_groups=mesh['wide'=8,'section'=4] {'wide','section'}, use_global_device_ids=true, to_apply=%region_26.27 | all-reduce | flops 10240 | bytes 81920 | tf_op jit(solution)/shard_map/psum | solution.py:289
  2796.1 7.3 slice_select_fusion
  2803.4 25.1 all-reduce.36.cloned.1.call-done
  (1126 shorter events, 996.5 us)
Async XLA Ops:
  7.2 2821.3 %all-reduce.36.cloned.1.call-start = ((), (), s32[]{:S(2)}) async-start(), calls=%async_computation | async-start | bytes 12582912 | tf_op jit(solution)/shard_map/psum | solution.py:289
  7.2 95.9 %collective-permute-start.6 = (f32[2,16,64,512]{3,2,1,0:T(8,128)}, f32[2,16,64,512]{3,2,1,0:T(8,128)}, u32[]{:S(2)}, u32[]{:S(2)}) collective-permute-start(f32[2,16,64,512]{3,2,1,0:T(8,128)} %param.14), channel_id=1, source_target_pairs={{1,0},{2,1},{3,2},{5,4},{6,5},{7,6},{9,8},{10,9},{11,10},{13,12},{... | collective-permute-start | bytes 12582920 | tf_op jit(solution)/shard_map/ppermute | solution.py:25
  8.7 101.7 %collective-permute-start.8 = (f32[2,16,64,512]{3,2,1,0:T(8,128)}, f32[2,16,64,512]{3,2,1,0:T(8,128)}, u32[]{:S(2)}, u32[]{:S(2)}) collective-permute-start(f32[2,16,64,512]{3,2,1,0:T(8,128)} %param.23), channel_id=1, source_target_pairs={{0,1},{1,2},{2,3},{4,5},{5,6},{6,7},{8,9},{9,10},{10,11},{12,13},{... | collective-permute-start | bytes 12582920 | tf_op jit(solution)/shard_map/ppermute | solution.py:25
  16.4 86.8 %copy-start.68 = (f32[2,16,64,512]{3,2,1,0:T(8,128)S(1)}, f32[2,16,64,512]{3,2,1,0:T(8,128)}, u32[]{:S(2)}) copy-start(f32[2,16,64,512]{3,2,1,0:T(8,128)} %param.14) | copy-start | bytes 12582916
  22.6 87.7 %copy-start.69 = (f32[2,16,64,512]{3,2,1,0:T(8,128)S(1)}, f32[2,16,64,512]{3,2,1,0:T(8,128)}, u32[]{:S(2)}) copy-start(f32[2,16,64,512]{3,2,1,0:T(8,128)} %param.23) | copy-start | bytes 12582916
  153.5 92.7 %collective-permute-start = (f32[2,32,16,512]{3,2,1,0:T(8,128)S(1)}, f32[2,32,16,512]{3,2,1,0:T(8,128)S(1)}, u32[]{:S(2)}, u32[]{:S(2)}) collective-permute-start(f32[2,32,16,512]{3,2,1,0:T(8,128)S(1)} %fusion.1267), channel_id=1, source_target_pairs={{0,2},{1,3},{2,0},{3,1},{4,6},{5,7},{6,4},{7,5},{8,10},{9,11},{10,... | collective-permute-start | bytes 6291464 | tf_op jit(solution)/shard_map/while/body/eval_jaxpr/ppermute | solution.py:19
  291.4 91.8 %collective-permute-start.1 = (f32[2,32,16,512]{3,1,2,0:T(8,128)S(1)}, f32[2,32,16,512]{3,1,2,0:T(8,128)S(1)}, u32[]{:S(2)}, u32[]{:S(2)}) collective-permute-start(f32[2,32,16,512]{3,1,2,0:T(8,128)S(1)} %pad_maximum_fusion.4), channel_id=1, source_target_pairs={{0,2},{1,3},{2,0},{3,1},{4,6},{5,7},{6,4},{7,5},{8,10},{9,11},{10,... | collective-permute-start | bytes 6291464 | tf_op jit(solution)/shard_map/while/body/eval_jaxpr/ppermute | solution.py:19
  304.1 83.6 %copy-start.3 = (f32[32,64,512]{2,1,0:T(8,128)S(1)}, f32[32,64,512]{2,1,0:T(8,128)}, u32[]{:S(2)}) copy-start(f32[32,64,512]{2,1,0:T(8,128)} %get-tuple-element.1953) | copy-start | bytes 12582916 | tf_op jit(solution)/shard_map/while
  423.9 90.8 %collective-permute-start.2 = (f32[32,64,512]{2,1,0:T(8,128)}, f32[32,64,512]{2,1,0:T(8,128)}, u32[]{:S(2)}, u32[]{:S(2)}) collective-permute-start(f32[32,64,512]{2,1,0:T(8,128)} %get-tuple-element.1977), channel_id=1, source_target_pairs={{0,1},{1,2},{2,3},{4,5},{5,6},{6,7},{8,9},{9,10},{10,11},{12,13},{... | collective-permute-start | bytes 12582920 | tf_op jit(solution)/shard_map/while/body/eval_jaxpr/ppermute | solution.py:25
  536.0 93.1 %collective-permute-start = (f32[2,32,16,512]{3,2,1,0:T(8,128)S(1)}, f32[2,32,16,512]{3,2,1,0:T(8,128)S(1)}, u32[]{:S(2)}, u32[]{:S(2)}) collective-permute-start(f32[2,32,16,512]{3,2,1,0:T(8,128)S(1)} %fusion.1267), channel_id=1, source_target_pairs={{0,2},{1,3},{2,0},{3,1},{4,6},{5,7},{6,4},{7,5},{8,10},{9,11},{10,... | collective-permute-start | bytes 6291464 | tf_op jit(solution)/shard_map/while/body/eval_jaxpr/ppermute | solution.py:19
  674.4 92.0 %collective-permute-start.1 = (f32[2,32,16,512]{3,1,2,0:T(8,128)S(1)}, f32[2,32,16,512]{3,1,2,0:T(8,128)S(1)}, u32[]{:S(2)}, u32[]{:S(2)}) collective-permute-start(f32[2,32,16,512]{3,1,2,0:T(8,128)S(1)} %pad_maximum_fusion.4), channel_id=1, source_target_pairs={{0,2},{1,3},{2,0},{3,1},{4,6},{5,7},{6,4},{7,5},{8,10},{9,11},{10,... | collective-permute-start | bytes 6291464 | tf_op jit(solution)/shard_map/while/body/eval_jaxpr/ppermute | solution.py:19
  687.0 83.8 %copy-start.3 = (f32[32,64,512]{2,1,0:T(8,128)S(1)}, f32[32,64,512]{2,1,0:T(8,128)}, u32[]{:S(2)}) copy-start(f32[32,64,512]{2,1,0:T(8,128)} %get-tuple-element.1953) | copy-start | bytes 12582916 | tf_op jit(solution)/shard_map/while
  806.8 90.6 %collective-permute-start.2 = (f32[32,64,512]{2,1,0:T(8,128)}, f32[32,64,512]{2,1,0:T(8,128)}, u32[]{:S(2)}, u32[]{:S(2)}) collective-permute-start(f32[32,64,512]{2,1,0:T(8,128)} %get-tuple-element.1977), channel_id=1, source_target_pairs={{0,1},{1,2},{2,3},{4,5},{5,6},{6,7},{8,9},{9,10},{10,11},{12,13},{... | collective-permute-start | bytes 12582920 | tf_op jit(solution)/shard_map/while/body/eval_jaxpr/ppermute | solution.py:25
  918.7 93.3 %collective-permute-start = (f32[2,32,16,512]{3,2,1,0:T(8,128)S(1)}, f32[2,32,16,512]{3,2,1,0:T(8,128)S(1)}, u32[]{:S(2)}, u32[]{:S(2)}) collective-permute-start(f32[2,32,16,512]{3,2,1,0:T(8,128)S(1)} %fusion.1267), channel_id=1, source_target_pairs={{0,2},{1,3},{2,0},{3,1},{4,6},{5,7},{6,4},{7,5},{8,10},{9,11},{10,... | collective-permute-start | bytes 6291464 | tf_op jit(solution)/shard_map/while/body/eval_jaxpr/ppermute | solution.py:19
  1057.2 92.0 %collective-permute-start.1 = (f32[2,32,16,512]{3,1,2,0:T(8,128)S(1)}, f32[2,32,16,512]{3,1,2,0:T(8,128)S(1)}, u32[]{:S(2)}, u32[]{:S(2)}) collective-permute-start(f32[2,32,16,512]{3,1,2,0:T(8,128)S(1)} %pad_maximum_fusion.4), channel_id=1, source_target_pairs={{0,2},{1,3},{2,0},{3,1},{4,6},{5,7},{6,4},{7,5},{8,10},{9,11},{10,... | collective-permute-start | bytes 6291464 | tf_op jit(solution)/shard_map/while/body/eval_jaxpr/ppermute | solution.py:19
  1069.9 83.8 %copy-start.3 = (f32[32,64,512]{2,1,0:T(8,128)S(1)}, f32[32,64,512]{2,1,0:T(8,128)}, u32[]{:S(2)}) copy-start(f32[32,64,512]{2,1,0:T(8,128)} %get-tuple-element.1953) | copy-start | bytes 12582916 | tf_op jit(solution)/shard_map/while
  1189.8 90.6 %collective-permute-start.2 = (f32[32,64,512]{2,1,0:T(8,128)}, f32[32,64,512]{2,1,0:T(8,128)}, u32[]{:S(2)}, u32[]{:S(2)}) collective-permute-start(f32[32,64,512]{2,1,0:T(8,128)} %get-tuple-element.1977), channel_id=1, source_target_pairs={{0,1},{1,2},{2,3},{4,5},{5,6},{6,7},{8,9},{9,10},{10,11},{12,13},{... | collective-permute-start | bytes 12582920 | tf_op jit(solution)/shard_map/while/body/eval_jaxpr/ppermute | solution.py:25
  1291.8 25.6 copy-start.74
  1291.8 25.6 copy-start.76
  1330.8 37.9 %copy-start.9 = (f32[32,64,512]{2,1,0:T(8,128)}, f32[32,64,512]{2,1,0:T(8,128)S(1)}, u32[]{:S(2)}) copy-start(f32[32,64,512]{2,1,0:T(8,128)S(1)} %get-tuple-element.2014) | copy-start | bytes 12582916 | tf_op jit(solution)/shard_map/while
  1377.1 92.0 %collective-permute-start.3 = (f32[2,32,16,512]{3,2,1,0:T(8,128)}, f32[2,32,16,512]{3,2,1,0:T(8,128)}, u32[]{:S(2)}, u32[]{:S(2)}) collective-permute-start(f32[2,32,16,512]{3,2,1,0:T(8,128)} %pad_add_fusion.5), channel_id=1, source_target_pairs={{0,2},{1,3},{2,0},{3,1},{4,6},{5,7},{6,4},{7,5},{8,10},{9,11},{10,... | collective-permute-start | bytes 6291464 | tf_op jit(solution)/shard_map/while/body/eval_jaxpr/ppermute | solution.py:19
  1407.9 13.6 copy-start.22
  1407.9 13.6 copy-start.48
  1444.6 30.6 %copy-start.45 = (f32[32,16,512]{2,0,1:T(8,128)S(1)}, f32[32,16,512]{2,0,1:T(8,128)}, u32[]{:S(2)}) copy-start(f32[32,16,512]{2,0,1:T(8,128)} %fusion.1415) | copy-start | bytes 3145732 | tf_op jit(solution)/shard_map/while
  1527.9 91.9 %collective-permute-start.4 = (f32[2,32,16,512]{3,1,2,0:T(8,128)}, f32[2,32,16,512]{3,1,2,0:T(8,128)}, u32[]{:S(2)}, u32[]{:S(2)}) collective-permute-start(f32[2,32,16,512]{3,1,2,0:T(8,128)} %pad_add_fusion.6), channel_id=1, source_target_pairs={{0,2},{1,3},{2,0},{3,1},{4,6},{5,7},{6,4},{7,5},{8,10},{9,11},{10,... | collective-permute-start | bytes 6291464 | tf_op jit(solution)/shard_map/while/body/eval_jaxpr/ppermute | solution.py:19
  1531.4 12.9 copy-start.29
  1645.2 95.0 %collective-permute-start.5 = (f32[32,64,512]{2,1,0:T(8,128)}, f32[32,64,512]{2,1,0:T(8,128)}, u32[]{:S(2)}, u32[]{:S(2)}) collective-permute-start(f32[32,64,512]{2,1,0:T(8,128)} %get-tuple-element.2054), channel_id=1, source_target_pairs={{1,0},{2,1},{3,2},{5,4},{6,5},{7,6},{9,8},{10,9},{11,10},{13,12},{... | collective-permute-start | bytes 12582920 | tf_op jit(solution)/shard_map/while/body/eval_jaxpr/ppermute | solution.py:25
  1677.7 62.5 %copy-start.75 = (f32[2,512]{1,0:T(2,128)S(1)}, f32[2,512]{1,0:T(2,128)}, u32[]{:S(2)}) copy-start(f32[2,512]{1,0:T(2,128)} %copy-done.74) | copy-start | bytes 12292 | tf_op jit(solution)/shard_map/while
  1677.7 62.5 %copy-start.77 = (f32[2,512]{1,0:T(2,128)S(1)}, f32[2,512]{1,0:T(2,128)}, u32[]{:S(2)}) copy-start(f32[2,512]{1,0:T(2,128)} %copy-done.76) | copy-start | bytes 12292 | tf_op jit(solution)/shard_map/while
  1677.8 62.4 %copy-start.79 = (f32[2,2,4,128]{3,2,1,0:T(4,128)}, f32[2,2,4,128]{3,2,1,0:T(4,128)S(1)}, u32[]{:S(2)}) copy-start(f32[2,2,4,128]{3,2,1,0:T(4,128)S(1)} %select_add_fusion.12) | copy-start | bytes 24580 | tf_op jit(solution)/shard_map/while
  1681.5 58.7 %copy-start.83 = (f32[2,512]{1,0:T(2,128)}, f32[2,512]{1,0:T(2,128)S(1)}, u32[]{:S(2)}) copy-start(f32[2,512]{1,0:T(2,128)S(1)} %get-tuple-element.2250) | copy-start | bytes 12292 | tf_op jit(solution)/shard_map/while
  1681.6 58.7 %copy-start.86 = (f32[2,512]{1,0:T(2,128)}, f32[2,512]{1,0:T(2,128)S(1)}, u32[]{:S(2)}) copy-start(f32[2,512]{1,0:T(2,128)S(1)} %get-tuple-element.2251) | copy-start | bytes 12292 | tf_op jit(solution)/shard_map/while
  1740.4 25.5 copy-start.74
  1740.4 25.5 copy-start.76
  1779.3 28.6 %copy-start.9 = (f32[32,64,512]{2,1,0:T(8,128)}, f32[32,64,512]{2,1,0:T(8,128)S(1)}, u32[]{:S(2)}) copy-start(f32[32,64,512]{2,1,0:T(8,128)S(1)} %get-tuple-element.2014) | copy-start | bytes 12582916 | tf_op jit(solution)/shard_map/while
  1816.1 88.6 %collective-permute-start.3 = (f32[2,32,16,512]{3,2,1,0:T(8,128)}, f32[2,32,16,512]{3,2,1,0:T(8,128)}, u32[]{:S(2)}, u32[]{:S(2)}) collective-permute-start(f32[2,32,16,512]{3,2,1,0:T(8,128)} %pad_add_fusion.5), channel_id=1, source_target_pairs={{0,2},{1,3},{2,0},{3,1},{4,6},{5,7},{6,4},{7,5},{8,10},{9,11},{10,... | collective-permute-start | bytes 6291464 | tf_op jit(solution)/shard_map/while/body/eval_jaxpr/ppermute | solution.py:19
  1844.0 13.7 copy-start.22
  1844.0 13.7 copy-start.48
  1880.8 29.9 %copy-start.45 = (f32[32,16,512]{2,0,1:T(8,128)S(1)}, f32[32,16,512]{2,0,1:T(8,128)}, u32[]{:S(2)}) copy-start(f32[32,16,512]{2,0,1:T(8,128)} %fusion.1415) | copy-start | bytes 3145732 | tf_op jit(solution)/shard_map/while
  1963.5 89.6 %collective-permute-start.4 = (f32[2,32,16,512]{3,1,2,0:T(8,128)}, f32[2,32,16,512]{3,1,2,0:T(8,128)}, u32[]{:S(2)}, u32[]{:S(2)}) collective-permute-start(f32[2,32,16,512]{3,1,2,0:T(8,128)} %pad_add_fusion.6), channel_id=1, source_target_pairs={{0,2},{1,3},{2,0},{3,1},{4,6},{5,7},{6,4},{7,5},{8,10},{9,11},{10,... | collective-permute-start | bytes 6291464 | tf_op jit(solution)/shard_map/while/body/eval_jaxpr/ppermute | solution.py:19
  1966.9 13.0 copy-start.29
  2078.4 95.0 %collective-permute-start.5 = (f32[32,64,512]{2,1,0:T(8,128)}, f32[32,64,512]{2,1,0:T(8,128)}, u32[]{:S(2)}, u32[]{:S(2)}) collective-permute-start(f32[32,64,512]{2,1,0:T(8,128)} %get-tuple-element.2054), channel_id=1, source_target_pairs={{1,0},{2,1},{3,2},{5,4},{6,5},{7,6},{9,8},{10,9},{11,10},{13,12},{... | collective-permute-start | bytes 12582920 | tf_op jit(solution)/shard_map/while/body/eval_jaxpr/ppermute | solution.py:25
  2110.9 62.5 %copy-start.75 = (f32[2,512]{1,0:T(2,128)S(1)}, f32[2,512]{1,0:T(2,128)}, u32[]{:S(2)}) copy-start(f32[2,512]{1,0:T(2,128)} %copy-done.74) | copy-start | bytes 12292 | tf_op jit(solution)/shard_map/while
  2110.9 62.5 %copy-start.77 = (f32[2,512]{1,0:T(2,128)S(1)}, f32[2,512]{1,0:T(2,128)}, u32[]{:S(2)}) copy-start(f32[2,512]{1,0:T(2,128)} %copy-done.76) | copy-start | bytes 12292 | tf_op jit(solution)/shard_map/while
  2110.9 62.4 %copy-start.79 = (f32[2,2,4,128]{3,2,1,0:T(4,128)}, f32[2,2,4,128]{3,2,1,0:T(4,128)S(1)}, u32[]{:S(2)}) copy-start(f32[2,2,4,128]{3,2,1,0:T(4,128)S(1)} %select_add_fusion.12) | copy-start | bytes 24580 | tf_op jit(solution)/shard_map/while
  2115.9 57.4 %copy-start.83 = (f32[2,512]{1,0:T(2,128)}, f32[2,512]{1,0:T(2,128)S(1)}, u32[]{:S(2)}) copy-start(f32[2,512]{1,0:T(2,128)S(1)} %get-tuple-element.2250) | copy-start | bytes 12292 | tf_op jit(solution)/shard_map/while
  2116.0 57.4 %copy-start.86 = (f32[2,512]{1,0:T(2,128)}, f32[2,512]{1,0:T(2,128)S(1)}, u32[]{:S(2)}) copy-start(f32[2,512]{1,0:T(2,128)S(1)} %get-tuple-element.2251) | copy-start | bytes 12292 | tf_op jit(solution)/shard_map/while
  2173.6 25.5 copy-start.74
  2173.6 25.5 copy-start.76
  2212.5 28.6 %copy-start.9 = (f32[32,64,512]{2,1,0:T(8,128)}, f32[32,64,512]{2,1,0:T(8,128)S(1)}, u32[]{:S(2)}) copy-start(f32[32,64,512]{2,1,0:T(8,128)S(1)} %get-tuple-element.2014) | copy-start | bytes 12582916 | tf_op jit(solution)/shard_map/while
  2249.3 88.6 %collective-permute-start.3 = (f32[2,32,16,512]{3,2,1,0:T(8,128)}, f32[2,32,16,512]{3,2,1,0:T(8,128)}, u32[]{:S(2)}, u32[]{:S(2)}) collective-permute-start(f32[2,32,16,512]{3,2,1,0:T(8,128)} %pad_add_fusion.5), channel_id=1, source_target_pairs={{0,2},{1,3},{2,0},{3,1},{4,6},{5,7},{6,4},{7,5},{8,10},{9,11},{10,... | collective-permute-start | bytes 6291464 | tf_op jit(solution)/shard_map/while/body/eval_jaxpr/ppermute | solution.py:19
  2276.7 13.7 copy-start.22
  2276.8 13.7 copy-start.48
  2313.5 30.4 %copy-start.45 = (f32[32,16,512]{2,0,1:T(8,128)S(1)}, f32[32,16,512]{2,0,1:T(8,128)}, u32[]{:S(2)}) copy-start(f32[32,16,512]{2,0,1:T(8,128)} %fusion.1415) | copy-start | bytes 3145732 | tf_op jit(solution)/shard_map/while
  2396.7 89.8 %collective-permute-start.4 = (f32[2,32,16,512]{3,1,2,0:T(8,128)}, f32[2,32,16,512]{3,1,2,0:T(8,128)}, u32[]{:S(2)}, u32[]{:S(2)}) collective-permute-start(f32[2,32,16,512]{3,1,2,0:T(8,128)} %pad_add_fusion.6), channel_id=1, source_target_pairs={{0,2},{1,3},{2,0},{3,1},{4,6},{5,7},{6,4},{7,5},{8,10},{9,11},{10,... | collective-permute-start | bytes 6291464 | tf_op jit(solution)/shard_map/while/body/eval_jaxpr/ppermute | solution.py:19
  2400.1 13.0 copy-start.29
  2511.9 95.0 %collective-permute-start.5 = (f32[32,64,512]{2,1,0:T(8,128)}, f32[32,64,512]{2,1,0:T(8,128)}, u32[]{:S(2)}, u32[]{:S(2)}) collective-permute-start(f32[32,64,512]{2,1,0:T(8,128)} %get-tuple-element.2054), channel_id=1, source_target_pairs={{1,0},{2,1},{3,2},{5,4},{6,5},{7,6},{9,8},{10,9},{11,10},{13,12},{... | collective-permute-start | bytes 12582920 | tf_op jit(solution)/shard_map/while/body/eval_jaxpr/ppermute | solution.py:25
  2544.4 62.5 %copy-start.75 = (f32[2,512]{1,0:T(2,128)S(1)}, f32[2,512]{1,0:T(2,128)}, u32[]{:S(2)}) copy-start(f32[2,512]{1,0:T(2,128)} %copy-done.74) | copy-start | bytes 12292 | tf_op jit(solution)/shard_map/while
  2544.4 62.5 %copy-start.77 = (f32[2,512]{1,0:T(2,128)S(1)}, f32[2,512]{1,0:T(2,128)}, u32[]{:S(2)}) copy-start(f32[2,512]{1,0:T(2,128)} %copy-done.76) | copy-start | bytes 12292 | tf_op jit(solution)/shard_map/while
  2544.4 62.4 %copy-start.79 = (f32[2,2,4,128]{3,2,1,0:T(4,128)}, f32[2,2,4,128]{3,2,1,0:T(4,128)S(1)}, u32[]{:S(2)}) copy-start(f32[2,2,4,128]{3,2,1,0:T(4,128)S(1)} %select_add_fusion.12) | copy-start | bytes 24580 | tf_op jit(solution)/shard_map/while
  2549.4 57.4 %copy-start.83 = (f32[2,512]{1,0:T(2,128)}, f32[2,512]{1,0:T(2,128)S(1)}, u32[]{:S(2)}) copy-start(f32[2,512]{1,0:T(2,128)S(1)} %get-tuple-element.2250) | copy-start | bytes 12292 | tf_op jit(solution)/shard_map/while
  2549.4 57.4 %copy-start.86 = (f32[2,512]{1,0:T(2,128)}, f32[2,512]{1,0:T(2,128)S(1)}, u32[]{:S(2)}) copy-start(f32[2,512]{1,0:T(2,128)S(1)} %get-tuple-element.2251) | copy-start | bytes 12292 | tf_op jit(solution)/shard_map/while
  2625.5 165.1 %collective-permute-start.9 = (f32[2,16,64,512]{3,2,1,0:T(8,128)}, f32[2,16,64,512]{3,2,1,0:T(8,128)}, u32[]{:S(2)}, u32[]{:S(2)}) collective-permute-start(f32[2,16,64,512]{3,2,1,0:T(8,128)} %slice.427), channel_id=1, source_target_pairs={{0,1},{1,2},{2,3},{4,5},{5,6},{6,7},{8,9},{9,10},{10,11},{12,13},{... | collective-permute-start | bytes 12582920 | tf_op jit(solution)/shard_map/ppermute | solution.py:25
  2634.0 162.2 %collective-permute-start.7 = (f32[2,16,64,512]{3,2,1,0:T(8,128)}, f32[2,16,64,512]{3,2,1,0:T(8,128)}, u32[]{:S(2)}, u32[]{:S(2)}) collective-permute-start(f32[2,16,64,512]{3,2,1,0:T(8,128)} %slice.423), channel_id=1, source_target_pairs={{1,0},{2,1},{3,2},{5,4},{6,5},{7,6},{9,8},{10,9},{11,10},{13,12},{... | collective-permute-start | bytes 12582920 | tf_op jit(solution)/shard_map/ppermute | solution.py:25
  (228 other events, 1253.8 us)
Sparse Core Ops, SparseCore 0:
  2641.0 187.4 all-reduce.35
where the time goes:
time: 2850 us; the launch traced here: 2840 us
  waiting for transfers between devices  1290 us (45%)
  matrix products  912 us (32%)
  other arithmetic  227 us (8%)
  local copies, waits for them, and re-layouts  191 us (7%)
  blocking collectives  149 us (5%)
  starting transfers between devices  42.7 us (1%)
    ppermute x12, waiting for transfers between devices, from_partner(): lax.ppermute(shard, axis, [(i, i ^ 1 << apart) for i in range(lax.axis_si...  761 us
    ppermute x10, waiting for transfers between devices, shifted(): return lax.ppermute(shard, axis, pairs)  499 us
    psum x1, blocking collectives, on_device(): lax.psum((padded[0], padded[1], padded[2], padded[3], padded[4], padded[5...  149 us
    dot_general x9, matrix products, rows_out(): jnp.dot(hidden, parameters[6], precision=PRECISE, preferred_element_type=...  147 us
    dot_general x12, matrix products, rows_out(): jnp.dot(second, parameters[4], precision=PRECISE, preferred_element_type=...  88.2 us
    dot_general x24, matrix products, complex_mix(): jnp.einsum('jkbi,bio->jkbo', imag_in, weights[1], precision=PRECISE)  78.2 us
    dot_general x18, matrix products, column_synthesis(): jnp.einsum('hkd,kw->hwd', source[1], sine_table * factor, precision=PRECISE)  71.4 us
    dot_general x24, matrix products, complex_mix(): jnp.einsum('jkbi,bio->jkbo', imag_in, weights[0], precision=PRECISE)  69.8 us
  transfers between devices with their start and end apart: 23, of which 20 were waited for; matrix products, arithmetic and copies ran while one was open for 17% of the time, Pallas kernels for 0%

commit v1 on v0

v1 whole, which is shorter than its diff:
```python
import functools
import math

import jax
import jax.numpy as jnp
import numpy as np
from jax import lax
from jax.experimental import pallas as pl
from jax.experimental.pallas import tpu as pltpu
from jax.sharding import PartitionSpec as P

BLOCKS = 4
GRID = 64
MODES = 32
EPSILON = 1e-05
THRESHOLD = 0.05
ROWS = 4
F32 = jnp.float32
BF16 = jnp.bfloat16
BOTH = ("wide", "section")


def split_table(table):
    table = table.astype(np.float32)
    high = table.astype(jnp.bfloat16)
    low = (table - high.astype(np.float32)).astype(jnp.bfloat16)
    return np.concatenate([high, high, low, low], axis=1)


def column_tables():
    columns = np.arange(MODES)
    angles = 2.0 * math.pi * (columns[:, None] * np.arange(GRID)[None, :] % GRID) / GRID
    plain = np.concatenate([np.cos(angles), np.sin(angles)], axis=0) / GRID
    factor = np.where(columns == 0, 1.0, 2.0)
    weighted = plain * np.concatenate([factor, factor])[:, None]
    return plain, weighted


def twiddle(index, length):
    angle = 2.0 * math.pi * index / length
    return math.cos(angle), math.sin(angle)


def half_spectrum(planes, pruned=False):
    length = len(planes)
    if length == 2:
        return [(planes[0] + planes[1], None), (planes[0] - planes[1], None)]
    even = half_spectrum(planes[0::2])
    odd = half_spectrum(planes[1::2])
    quarter = length // 4
    first, second = [], []
    for k in range(quarter + 1):
        (er, ei), (dr, di) = even[k], odd[k]
        if k == 0:
            first.append((er + dr, None))
            second.append((er - dr, None))
            continue
        if k == quarter:
            first.append((er, -dr))
            continue
        c, s = twiddle(k, length)
        if 2 * k == quarter:
            tr, ti = (dr + di) * c, (di - dr) * c
        else:
            tr, ti = dr * c + di * s, di * c - dr * s
        first.append((er + tr, ei + ti))
        second.append((er - tr, ti - ei))
    if pruned:
        return first
    return first + second[::-1]


def half_synthesis(spectrum, length, pruned=False):
    if length == 2:
        (a, _), (b, _) = spectrum
        return [a + b, a - b]
    quarter = length // 4
    even, odd = [], []
    for k in range(quarter + 1):
        ar, ai = spectrum[k]
        if k == quarter:
            even.append((ar, None))
            odd.append((-ai, None))
            continue
        if k == 0:
            if pruned:
                even.append((ar, None))
                odd.append((ar, None))
            else:
                br = spectrum[length // 2][0]
                even.append((ar + br, None))
                odd.append((ar - br, None))
            continue
        if pruned:
            sr, si, tr, ti = ar, ai, ar, ai
        else:
            br, bi = spectrum[length // 2 - k]
            sr, si, tr, ti = ar + br, ai - bi, ar - br, ai + bi
        even.append((sr, si))
        c, s = twiddle(k, length)
        if 2 * k == quarter:
            odd.append(((tr - ti) * c, (ti + tr) * c))
        else:
            odd.append((tr * c - ti * s, ti * c + tr * s))
    even_planes = half_synthesis(even, length // 2)
    odd_planes = half_synthesis(odd, length // 2)
    planes = []
    for e, o in zip(even_planes, odd_planes):
        planes += [e, o]
    return planes


def exact_dot(left, right, left_dim, right_dim):
    return lax.dot_general(
        left,
        right,
        (((left_dim,), (right_dim,)), ((), ())),
        precision=lax.Precision.HIGH,
        preferred_element_type=F32,
    )


def split(values):
    high = values.astype(BF16)
    low = (values - high.astype(F32)).astype(BF16)
    return high, low


def table_dot(table, values):
    high, low = split(values)
    stacked = jnp.concatenate([high, low, high, low], axis=0)
    return jnp.dot(table, stacked, preferred_element_type=F32)


def gelu(values):
    return 0.5 * values * (1.0 + lax.erf(values * math.sqrt(0.5)))


def gelu_and_slope(values):
    cumulative = 0.5 * (1.0 + lax.erf(values * math.sqrt(0.5)))
    density = jnp.exp(-0.5 * values * values) * (1.0 / math.sqrt(2.0 * math.pi))
    return values * cumulative, cumulative + values * density


def normalise(values):
    average = jnp.mean(values, axis=-1, keepdims=True)
    centered = values - average
    variance = jnp.mean(centered * centered, axis=-1, keepdims=True)
    scale = lax.rsqrt(variance + EPSILON)
    return centered * scale, scale


def norm_backward(grad, unit, scale, gains):
    inner = grad * gains
    mean_inner = jnp.mean(inner, axis=-1, keepdims=True)
    mean_unit = jnp.mean(inner * unit, axis=-1, keepdims=True)
    return scale * (inner - mean_inner - unit * mean_unit)


def column_sum(values):
    return jnp.sum(values, axis=0, keepdims=True)


def joined(core, kept, other):
    shape = (kept.shape[0] * kept.shape[1], kept.shape[2])
    kept, other = kept[...].reshape(shape), other[...].reshape(shape)
    first = jnp.where(core == 0, kept, other)
    second = jnp.where(core == 0, other, kept)
    return jnp.concatenate([first, second], axis=1)


def parted(core, values, kept, other):
    half = values.shape[1] // 2
    first, second = values[:, :half], values[:, half:]
    kept[...] = jnp.where(core == 0, first, second).reshape(kept.shape)
    other[...] = jnp.where(core == 0, second, first).reshape(other.shape)


def flat(ref):
    return ref[...].reshape(-1, ref.shape[-1])


def picked(step, steps, refs):
    if len(refs) == 1:
        return flat(refs[0])
    return jnp.where(step < steps // 2, flat(refs[0]), flat(refs[1]))


def put_pieces(step, steps, refs, values):
    if len(refs) == 1:
        refs[0][...] = values.reshape(refs[0].shape)
        return

    @pl.when(step < steps // 2)
    def _():
        refs[0][...] = values.reshape(refs[0].shape)

    @pl.when(step >= steps // 2)
    def _():
        refs[1][...] = values.reshape(refs[1].shape)


def analyse(own, recv, table, sign, planes, modes):
    def rows(index, _):
        at = pl.ds(pl.multiple_of(index * 8, 8), 8)
        loaded = [own[p, at, :] for p in range(GRID // 2)] + [recv[p, at, :] for p in range(GRID // 2)]
        for k, (re, im) in enumerate(half_spectrum(loaded, pruned=True)):
            im = jnp.zeros_like(re) if im is None else im
            if k % 2:
                re, im = re * sign, im * sign
            planes[k, at, :] = jnp.concatenate([re, im], axis=1)
        return 0

    lax.fori_loop(0, GRID // 8, rows, 0)
    for k in range(MODES // 2 + 1):
        found = table_dot(table[...], planes[k])
        lanes = found.shape[1] // 2
        cr, ci = found[:MODES, :lanes], found[:MODES, lanes:]
        sr, si = found[MODES:, :lanes], found[MODES:, lanes:]
        if k < MODES // 2:
            modes[k * MODES : (k + 1) * MODES, :] = jnp.concatenate([cr + si, ci - sr], axis=1)
        if k > 0:
            place = MODES - k
            modes[place * MODES : (place + 1) * MODES, :] = jnp.concatenate([cr - si, -ci - sr], axis=1)


def synthesise(modes, table, sign, planes, keep, send):
    lanes = modes.shape[1] // 2
    for k in range(MODES // 2 + 1):
        place = MODES - k
        if k == 0:
            above, below = modes[0:MODES, :], None
            total, apart = above, above
        elif k == MODES // 2:
            below = modes[place * MODES : (place + 1) * MODES, :]
            total, apart = below, -below
        else:
            above = modes[k * MODES : (k + 1) * MODES, :]
            below = modes[place * MODES : (place + 1) * MODES, :]
            total, apart = above + below, above - below
        upper = jnp.concatenate([total[:, :lanes], apart[:, lanes:]], axis=1)
        lower = jnp.concatenate([-total[:, lanes:], apart[:, :lanes]], axis=1)
        planes[k] = table_dot(table[...], jnp.concatenate([upper, lower], axis=0))

    def rows(index, _):
        at = pl.ds(pl.multiple_of(index * 8, 8), 8)
        spectrum = []
        for k in range(MODES // 2 + 1):
            both = planes[k, at, :]
            if k % 2:
                both = both * sign
            spectrum.append((both[:, :lanes], both[:, lanes:]))
        cells = half_synthesis(spectrum, GRID, pruned=True)
        for p in range(GRID // 2):
            keep[p, at, :] = cells[p]
            send[p, at, :] = cells[GRID // 2 + p]
        return 0

    lax.fori_loop(0, GRID // 8, rows, 0)


def place_weights(weight, stacked):
    lanes = weight.shape[-1]
    for j in range(2):
        real, imag = weight[j, 0], weight[j, 1]
        stacked[j, :lanes, :lanes] = real
        stacked[j, :lanes, lanes:] = imag
        stacked[j, lanes:, :lanes] = -imag
        stacked[j, lanes:, lanes:] = real


MIX_ROWS = 256


def mix_offsets(offset, block):
    at = pl.ds(block, 1)
    return [jnp.concatenate([offset[j, 0, at, :], offset[j, 1, at, :]], axis=1) for j in range(2)]


def spectral_forward_kernel(
    info, own, recv, weight, offset, table_in, table_out, keep, send, modes, before, after, planes, shrunk, stacked
):
    core = info[0]
    sign = jnp.where(core == 1, -1.0, 1.0).astype(F32)
    place_weights(weight, stacked)
    first_offset, second_offset = mix_offsets(offset, 2 * core + pl.program_id(0))
    analyse(own, recv, table_in, sign, planes, modes)

    def mix(index, _):
        at = pl.ds(pl.multiple_of(index * MIX_ROWS, MIX_ROWS), MIX_ROWS)
        first = exact_dot(modes[at, :], stacked[0], 1, 0) + first_offset
        before[at, :] = first
        second = exact_dot(gelu(first), stacked[1], 1, 0) + second_offset
        after[at, :] = second
        shrunk[at, :] = second - THRESHOLD * jnp.tanh(second * (1.0 / THRESHOLD))
        return 0

    lax.fori_loop(0, MODES * MODES // MIX_ROWS, mix, 0)
    synthesise(shrunk, table_out, sign, planes, keep, send)


def spectral_backward_kernel(
    info, own, recv, weight, modes, before, after, table_in, table_out, keep, send, weight_grad, offset_grad, planes, flowing, stacked, summed
):
    core = info[0]
    sign = jnp.where(core == 1, -1.0, 1.0).astype(F32)
    place_weights(weight, stacked)
    analyse(own, recv, table_in, sign, planes, flowing)
    summed[...] = jnp.zeros_like(summed)

    def mix(index, totals):
        at = pl.ds(pl.multiple_of(index * MIX_ROWS, MIX_ROWS), MIX_ROWS)
        ratio = jnp.tanh(after[at, :] * (1.0 / THRESHOLD))
        grad_second = flowing[at, :] * ratio * ratio
        hidden, slope = gelu_and_slope(before[at, :])
        summed[1] += exact_dot(hidden, grad_second, 0, 0)
        grad_first = exact_dot(grad_second, stacked[1], 1, 1) * slope
        summed[0] += exact_dot(modes[at, :], grad_first, 0, 0)
        flowing[at, :] = exact_dot(grad_first, stacked[0], 1, 1)
        return totals[0] + column_sum(grad_first), totals[1] + column_sum(grad_second)

    empty = jnp.zeros((1, flowing.shape[1]), F32)
    totals = lax.fori_loop(0, MODES * MODES // MIX_ROWS, mix, (empty, empty))
    lanes = flowing.shape[1] // 2
    for j in range(2):
        offset_grad[j, 0] = totals[j][:, :lanes]
        offset_grad[j, 1] = totals[j][:, lanes:]
        weight_grad[j, 0] = summed[j, :lanes, :lanes] + summed[j, lanes:, lanes:]
        weight_grad[j, 1] = summed[j, :lanes, lanes:] - summed[j, lanes:, :lanes]
    synthesise(flowing, table_out, sign, planes, keep, send)


def first_norm_kernel(steps, info, a, b, gains, biases, keep, send):
    unit, _ = normalise(picked(pl.program_id(0), steps, (a, b)))
    parted(info[0], unit * gains[0:1] + biases[0:1], keep, send)


def ffn_forward_kernel(steps, layer, pieces, more, info, *refs):
    step = pl.program_id(0)
    refs = list(refs)
    x_refs, refs = refs[:pieces], refs[pieces:]
    kept, taken, gains, biases, up, up_offset, down, down_offset = refs[:8]
    refs = refs[8:]
    core = info[0]
    mixed = picked(step, steps, x_refs) + joined(core, kept, taken)
    unit, _ = normalise(mixed)
    normed = unit * gains[1:2] + biases[1:2]
    before = exact_dot(normed, up[...], 1, 0) + up_offset[layer : layer + 1]
    result = mixed + exact_dot(gelu(before), down[...], 1, 0) + down_offset[layer : layer + 1]
    if more:
        next_gains, next_biases, mixed_out, before_out, result_out, keep, send = refs
        put_pieces(step, steps, (result_out,), result)
        unit, _ = normalise(result)
        parted(core, unit * next_gains[0:1] + next_biases[0:1], keep, send)
    else:
        mixed_out, before_out, first_out, second_out = refs
        put_pieces(step, steps, (first_out, second_out), result)
    mixed_out[...] = mixed.reshape(mixed_out.shape)
    before_out[...] = before.reshape(before_out.shape)


def first_norm_backward(core, x, du_kept, du_sent, dh_kept, dh_taken, gains):
    grad = joined(core, dh_kept, dh_taken)
    unit, scale = normalise(x)
    result = joined(core, du_kept, du_sent) + norm_backward(grad, unit, scale, gains[0:1])
    return result, column_sum(grad * unit), column_sum(grad)


def ffn_backward_kernel(steps, fused, info, *refs):
    step = pl.program_id(0)
    core = info[0]
    refs = list(refs)
    mixed, before, gains, biases, up, down = refs[:6]
    if fused:
        x, du_kept, du_sent, dh_kept, dh_taken, next_gains = refs[6:12]
        grad, late_gain, late_bias = first_norm_backward(core, flat(x), du_kept, du_sent, dh_kept, dh_taken, next_gains)
        refs = refs[12:]
    else:
        grad = picked(step, steps, refs[6:8])
        refs = refs[8:]
    keep, send, up_grad, down_grad, small = refs

    @pl.when(step == 0)
    def _():
        up_grad[...] = jnp.zeros_like(up_grad)
        down_grad[...] = jnp.zeros_like(down_grad)
        small[...] = jnp.zeros_like(small)

    unit, scale = normalise(flat(mixed))
    normed = unit * gains[1:2] + biases[1:2]
    hidden, slope = gelu_and_slope(flat(before))
    down_grad[...] += exact_dot(hidden, grad, 0, 0)
    inner = exact_dot(grad, down[...], 1, 1) * slope
    up_grad[...] += exact_dot(normed, inner, 0, 0)
    outer = exact_dot(inner, up[...], 1, 1)
    small[0:1] += column_sum(outer * unit)
    small[1:2] += column_sum(outer)
    small[2:3] += column_sum(inner)
    small[3:4] += column_sum(grad)
    if fused:
        small[4:5] += late_gain
        small[5:6] += late_bias
    parted(core, grad + norm_backward(outer, unit, scale, gains[1:2]), keep, send)


def input_grad_kernel(steps, info, a, b, du_kept, du_sent, dh_kept, dh_taken, gains, first_out, second_out, small):
    step = pl.program_id(0)
    x = picked(step, steps, (a, b))
    result, gain_sum, bias_sum = first_norm_backward(info[0], x, du_kept, du_sent, dh_kept, dh_taken, gains)

    @pl.when(step == 0)
    def _():
        small[...] = jnp.zeros_like(small)

    small[0:1] += gain_sum
    small[1:2] += bias_sum
    put_pieces(step, steps, (first_out, second_out), result)


def call(kernel, grid, in_specs, out_specs, out_shapes, scratch, flops, moved, name):
    return pl.pallas_call(
        kernel,
        grid_spec=pltpu.PrefetchScalarGridSpec(
            num_scalar_prefetch=1,
            grid=(grid,),
            in_specs=in_specs,
            out_specs=out_specs,
            scratch_shapes=scratch,
        ),
        out_shape=out_shapes,
        compiler_params=pltpu.CompilerParams(vmem_limit_bytes=56 * 2**20),
        cost_estimate=pl.CostEstimate(flops=int(flops), bytes_accessed=int(moved), transcendentals=0),
        name=name,
    )


class Plan:
    def __init__(self, quarter, width, hidden):
        self.quarter, self.width, self.hidden = quarter, width, hidden
        self.steps = 2 * quarter // ROWS
        per_piece = quarter // ROWS
        half = width // 2

        def local(j, s):
            return (j, 0, 0)

        def canonical(j, s):
            return (((j // per_piece) ^ s[1]) * per_piece + j % per_piece, 0, 0)

        self.row = pl.BlockSpec((ROWS, GRID, width), local)
        self.wide_row = pl.BlockSpec((ROWS, GRID, hidden), local)
        self.half_row = pl.BlockSpec((ROWS, GRID, half), canonical)
        self.first = pl.BlockSpec((ROWS, GRID, width), lambda j, s: (jnp.minimum(j, per_piece - 1), 0, 0))
        self.second = pl.BlockSpec((ROWS, GRID, width), lambda j, s: (jnp.maximum(j - per_piece, 0), 0, 0))
        self.half_shape = jax.ShapeDtypeStruct((2 * quarter, GRID, half), F32)
        self.row_shape = jax.ShapeDtypeStruct((2 * quarter, GRID, width), F32)
        self.wide_shape = jax.ShapeDtypeStruct((2 * quarter, GRID, hidden), F32)
        self.piece_shape = jax.ShapeDtypeStruct((quarter, GRID, width), F32)

    def norm(self, layer):
        return pl.BlockSpec((None, 2, self.width), lambda j, s: (layer, 0, 0))

    def matrix(self, layer, rows, columns):
        return pl.BlockSpec((None, rows, columns), lambda j, s: (layer, 0, 0))

    def whole(self, shape):
        return pl.BlockSpec(shape, lambda j, s: (0,) * len(shape))


def first_norm(plan, info, a, b, gains, biases):
    return call(
        functools.partial(first_norm_kernel, plan.steps),
        plan.steps,
        [plan.first, plan.second, plan.norm(0), plan.norm(0)],
        [plan.half_row, plan.half_row],
        [plan.half_shape, plan.half_shape],
        [],
        0,
        4 * 2**20 * 2,
        "first_norm",
    )(info, a, b, gains, biases)


def spectral_specs(layer, width):
    block = width // BLOCKS
    cells = pl.BlockSpec((GRID // 2, GRID, block), lambda b, s: (0, 0, b))
    weight = pl.BlockSpec((None, 2, 2, None, block, block), lambda b, s: (layer, 0, 0, 2 * s[0] + b, 0, 0))
    offset = pl.BlockSpec((None, 2, 2, BLOCKS, block), lambda b, s: (layer, 0, 0, 0, 0))
    table = pl.BlockSpec((GRID, 4 * GRID), lambda b, s: (0, 0))
    modes = pl.BlockSpec((None, MODES * MODES, 2 * block), lambda b, s: (b, 0, 0))
    modes_shape = jax.ShapeDtypeStruct((2, MODES * MODES, 2 * block), F32)
    planes = pltpu.VMEM((MODES // 2 + 1, GRID, 2 * block), F32)
    flowing = pltpu.VMEM((MODES * MODES, 2 * block), F32)
    stacked = pltpu.VMEM((2, 2 * block, 2 * block), F32)
    return block, cells, weight, offset, table, modes, modes_shape, planes, flowing, stacked


def spectral_forward(plan, layer, info, own, recv, weight_all, offset_all, tables):
    block, cells, weight, offset, table, modes, modes_shape, planes, flowing, stacked = spectral_specs(layer, plan.width)
    return call(
        spectral_forward_kernel,
        2,
        [cells, cells, weight, offset, table, table],
        [cells, cells, modes, modes, modes],
        [plan.half_shape, plan.half_shape, modes_shape, modes_shape, modes_shape],
        [planes, flowing, stacked],
        3 * 2e9,
        14 * 2**20,
        f"spectral_forward_{layer}",
    )(info, own, recv, weight_all, offset_all, tables[0], tables[3])


def spectral_backward(plan, layer, info, own, recv, weight_all, saved, tables):
    block, cells, weight, offset, table, modes, modes_shape, planes, flowing, stacked = spectral_specs(layer, plan.width)
    return call(
        spectral_backward_kernel,
        2,
        [cells, cells, weight, modes, modes, modes, table, table],
        [
            cells,
            cells,
            pl.BlockSpec((2, 2, None, block, block), lambda b, s: (0, 0, b, 0, 0)),
            pl.BlockSpec((2, 2, None, 1, block), lambda b, s: (0, 0, b, 0, 0)),
        ],
        [
            plan.half_shape,
            plan.half_shape,
            jax.ShapeDtypeStruct((2, 2, 2, block, block), F32),
            jax.ShapeDtypeStruct((2, 2, 2, 1, block), F32),
        ],
        [planes, flowing, stacked, pltpu.VMEM((2, 2 * block, 2 * block), F32)],
        3 * 4e9,
        14 * 2**20,
        f"spectral_backward_{layer}",
    )(info, own, recv, weight_all, *saved, tables[1], tables[2])


def ffn_forward(plan, layer, more, info, x, kept, taken, gains, biases, up, up_offset, down, down_offset):
    width, hidden = plan.width, plan.hidden
    specs = [plan.first, plan.second] if len(x) == 2 else [plan.row]
    specs += [plan.half_row, plan.half_row, plan.norm(layer), plan.norm(layer)]
    specs += [plan.matrix(layer, width, hidden), plan.whole(up_offset.shape)]
    specs += [plan.matrix(layer, hidden, width), plan.whole(down_offset.shape)]
    args = [*x, kept, taken, gains, biases, up, up_offset, down, down_offset]
    out_specs = [plan.row, plan.wide_row]
    out_shapes = [plan.row_shape, plan.wide_shape]
    if more:
        specs += [plan.norm(layer + 1), plan.norm(layer + 1)]
        args += [gains, biases]
        out_specs += [plan.row, plan.half_row, plan.half_row]
        out_shapes += [plan.row_shape, plan.half_shape, plan.half_shape]
    else:
        out_specs += [plan.first, plan.second]
        out_shapes += [plan.piece_shape, plan.piece_shape]
    return call(
        functools.partial(ffn_forward_kernel, plan.steps, layer, len(x), more),
        plan.steps,
        specs,
        out_specs,
        out_shapes,
        [],
        3 * 4 * 2048 * width * hidden,
        24 * 2**20,
        f"ffn_forward_{layer}",
    )(info, *args)


def ffn_backward(plan, layer, info, mixed, before, gains, biases, up, down, grads):
    width, hidden = plan.width, plan.hidden
    fused = len(grads) == 5
    specs = [plan.row, plan.wide_row, plan.norm(layer), plan.norm(layer)]
    specs += [plan.matrix(layer, width, hidden), plan.matrix(layer, hidden, width)]
    args = [mixed, before, gains, biases, up, down, *grads]
    if fused:
        specs += [plan.row] + [plan.half_row] * 4 + [plan.norm(layer + 1)]
        args += [gains]
    else:
        specs += [plan.first, plan.second]
    return call(
        functools.partial(ffn_backward_kernel, plan.steps, fused),
        plan.steps,
        specs,
        [
            plan.half_row,
            plan.half_row,
            plan.whole((width, hidden)),
            plan.whole((hidden, width)),
            plan.whole((8, width)),
        ],
        [
            plan.half_shape,
            plan.half_shape,
            jax.ShapeDtypeStruct((width, hidden), F32),
            jax.ShapeDtypeStruct((hidden, width), F32),
            jax.ShapeDtypeStruct((8, width), F32),
        ],
        [],
        3 * 8 * 2048 * width * hidden,
        24 * 2**20,
        f"ffn_backward_{layer}",
    )(info, *args)


def input_gradient(plan, info, a, b, du, dh, gains):
    return call(
        functools.partial(input_grad_kernel, plan.steps),
        plan.steps,
        [plan.first, plan.second] + [plan.half_row] * 4 + [plan.norm(0)],
        [plan.first, plan.second, plan.whole((8, plan.width))],
        [plan.piece_shape, plan.piece_shape, jax.ShapeDtypeStruct((8, plan.width), F32)],
        [],
        0,
        16 * 2**20,
        "input_gradient",
    )(info, a, b, *du, *dh, gains)


def item_routes(wide, section):
    routes = []
    for flip in range(2):
        pairs = []
        for w in range(wide):
            c = w % 2
            for z in range(section):
                pairs.append((w * section + z, (w - c + z // 2) * section + 2 * c + (z % 2 ^ flip)))
        routes.append(pairs)
    return routes


def gather_pieces(shard, parity, routes):
    first = lax.dynamic_index_in_dim(shard, parity, 0, keepdims=False)
    second = lax.dynamic_index_in_dim(shard, 1 - parity, 0, keepdims=False)
    return lax.ppermute(first, BOTH, routes[0]), lax.ppermute(second, BOTH, routes[1])


def scatter_pieces(first, second, parity, routes):
    first = lax.ppermute(first, BOTH, [(b, a) for a, b in routes[0]])
    second = lax.ppermute(second, BOTH, [(b, a) for a, b in routes[1]])
    low = jnp.where(parity == 0, first, second)
    high = jnp.where(parity == 0, second, first)
    return jnp.stack([low, high])


def swap(values):
    return lax.ppermute(values, "wide", [(i, i ^ 1) for i in range(lax.axis_size("wide"))])


def on_device(
    inputs,
    norm_gain,
    norm_bias,
    mix_weight,
    mix_bias,
    up_weight,
    up_bias,
    down_weight,
    down_bias,
    out_grad,
):
    width, hidden = up_weight.shape[1:]
    plan = Plan(inputs.shape[1], width, hidden)
    routes = item_routes(lax.axis_size("wide"), lax.axis_size("section"))
    core = lax.axis_index("wide") % 2
    parity = lax.axis_index("section") % 2
    info = jnp.stack([core, parity]).astype(jnp.int32)
    plain, weighted = column_tables()
    tables = [jnp.asarray(split_table(t)) for t in (plain, weighted, plain.T, weighted.T)]

    xa, xb = gather_pieces(inputs, parity, routes)
    out_grad, xa, xb = lax.optimization_barrier((out_grad, xa, xb))
    ga, gb = gather_pieces(out_grad, parity, routes)

    ffn_args = (norm_gain, norm_bias, up_weight, up_bias, down_weight, down_bias)
    keep, send = first_norm(plan, info, xa, xb, norm_gain, norm_bias)
    keep, send, *saved0 = spectral_forward(plan, 0, info, keep, swap(send), mix_weight, mix_bias, tables)
    u0, a0, x1, keep, send = ffn_forward(plan, 0, True, info, (xa, xb), keep, swap(send), *ffn_args)
    keep, send, *saved1 = spectral_forward(plan, 1, info, keep, swap(send), mix_weight, mix_bias, tables)
    u1, a1, va, vb = ffn_forward(plan, 1, False, info, (x1,), keep, swap(send), *ffn_args)

    va, vb, ga, gb = lax.optimization_barrier((va, vb, ga, gb))
    outputs = scatter_pieces(va, vb, parity, routes)

    back_args = (norm_gain, norm_bias, up_weight, down_weight)
    du1 = ffn_backward(plan, 1, info, u1, a1, *back_args, (ga, gb))
    dh1 = spectral_backward(plan, 1, info, du1[0], swap(du1[1]), mix_weight, saved1, tables)
    late = (x1, du1[0], du1[1], dh1[0], swap(dh1[1]))
    du0 = ffn_backward(plan, 0, info, u0, a0, *back_args, late)
    dh0 = spectral_backward(plan, 0, info, du0[0], swap(du0[1]), mix_weight, saved0, tables)
    dxa, dxb, small = input_gradient(plan, info, xa, xb, du0[:2], (dh0[0], swap(dh0[1])), norm_gain)
    input_grad = scatter_pieces(dxa, dxb, parity, routes)

    def placed(part):
        empty = jnp.zeros_like(part)
        return jnp.where(core == 0, jnp.concatenate([part, empty], 2), jnp.concatenate([empty, part], 2))

    mix_grads = jnp.stack([placed(dh0[2]), placed(dh1[2])])
    offset_grads = jnp.stack([placed(dh0[3]), placed(dh1[3])])[:, :, :, :, 0]
    gain_grads = jnp.stack([jnp.stack([small[0], du0[4][0]]), jnp.stack([du0[4][4], du1[4][0]])])
    bias_grads = jnp.stack([jnp.stack([small[1], du0[4][1]]), jnp.stack([du0[4][5], du1[4][1]])])
    up_grads = jnp.stack([du0[2], du1[2]])
    down_grads = jnp.stack([du0[3], du1[3]])
    up_offset_grads = jnp.stack([du0[4][2], du1[4][2]])
    down_offset_grads = jnp.stack([du0[4][3], du1[4][3]])
    summed = lax.psum(
        (gain_grads, bias_grads, mix_grads, offset_grads, up_grads, up_offset_grads, down_grads, down_offset_grads), BOTH
    )
    return (outputs, input_grad, *summed)


def solution(mesh):
    cells = P("wide", "section", None, None)
    return jax.shard_map(
        on_device,
        mesh=mesh,
        in_specs=(cells, P(), P(), P(), P(), P(), P(), P(), P(), cells),
        out_specs=(cells, cells, P(), P(), P(), P(), P(), P(), P(), P()),
        check_vma=False,
    )
```

time: 2850 us -> 662 us (0.23)
  waiting for transfers between devices: 1290 us -> 85.8 us
  matrix products: 912 us -> 0 us
  other arithmetic: 227 us -> 17.2 us
  Pallas kernels: 0 us -> 166 us
  local copies, waits for them, and re-layouts: 191 us -> 26.9 us
  starting transfers between devices: 42.7 us -> 134 us
  blocking collectives: 149 us -> 214 us
    ppermute x22 -> x16, waiting for transfers between devices: 1260 us -> 83.4 us  [the longest x2 58.3 us: gather_pieces(): lax.ppermute(second, BOTH, routes[1])]
    dot_general x285 -> x0, matrix products: 912 us -> none  [the longest x9 147 us: rows_out(): jnp.dot(hidden, parameters[6], precision=PRECISE, preferred_element_type=...]
    pallas_call x0 -> x10, Pallas kernels: none -> 166 us  [the longest x2 51 us: ffn_backward(): call(functools.partial(ffn_backward_kernel, plan.steps, fused), plan.step...]
    ppermute x22 -> x16, starting transfers between devices: 42.6 us -> 134 us  [the longest x8 90.9 us: swap(): lax.ppermute(values, 'wide', [(i, i ^ 1) for i in range(lax.axis_size('wi...]
    reduce_sum x36 -> x0, other arithmetic: 85.1 us -> none  [the longest x12 24.6 us: layer_norm(): return centered * lax.rsqrt(variance + EPSILON) * gains + biases]
    psum x1, blocking collectives: 149 us -> 214 us  [on_device(): lax.psum((gain_grads, bias_grads, mix_grads, offset_grads, up_grads, up_o...]
    dynamic_update_slice x15 -> x0, other arithmetic: 59.8 us -> none  [on_device(): lax.scan(forward_step, initial, jnp.arange(micro_count + 1))]
    reshape x30 -> x0, local copies, waits for them, and re-layouts: 53.3 us -> none  [the longest x9 17.5 us: mode_mixing(): out_imag = shrink(out_imag).reshape(mode_shape)]
  transfers between devices with their start and end apart: 23 -> 17, of which waited for: 20 -> 10; matrix products, arithmetic and copies ran while one was open for 17% -> 3% of each run, Pallas kernels for 0% -> 4%
where the time goes in v1:
time: 662 us; the launch traced here: 659 us
  blocking collectives  214 us (32%)
  Pallas kernels  166 us (25%)
  starting transfers between devices  134 us (20%)
  waiting for transfers between devices  85.8 us (13%)
  local copies, waits for them, and re-layouts  26.9 us (4%)
  other arithmetic  17.2 us (3%)
  between operations  14.3 us (2%)
    psum x1, blocking collectives, on_device(): lax.psum((gain_grads, bias_grads, mix_grads, offset_grads, up_grads, up_o...  214 us
    ppermute x8, starting transfers between devices, swap(): lax.ppermute(values, 'wide', [(i, i ^ 1) for i in range(lax.axis_size('wi...  90.9 us
    ppermute x2, waiting for transfers between devices, gather_pieces(): lax.ppermute(second, BOTH, routes[1])  58.3 us
    pallas_call x2, Pallas kernels, ffn_backward(): call(functools.partial(ffn_backward_kernel, plan.steps, fused), plan.step...  51 us
    pallas_call x2, Pallas kernels, ffn_forward(): call(functools.partial(ffn_forward_kernel, plan.steps, layer, len(x), mor...  33.2 us
    pallas_call x2, Pallas kernels, spectral_backward(): call(spectral_backward_kernel, 2, [cells, cells, weight, modes, modes, mo...  32.8 us
    pallas_call x2, Pallas kernels, spectral_forward(): call(spectral_forward_kernel, 2, [cells, cells, weight, offset, table, ta...  30.6 us
    ppermute x8, waiting for transfers between devices, swap(): lax.ppermute(values, 'wide', [(i, i ^ 1) for i in range(lax.axis_size('wi...  25.1 us
  transfers between devices with their start and end apart: 17, of which 10 were waited for; matrix products, arithmetic and copies ran while one was open for 3% of the time, Pallas kernels for 4%

profile of v1, /device:TPU:0, one launch (start us, length us, event | category | flops | bytes accessed | tf_op | source)
XLA Modules:
  0.0 658.6 jit_solution(2111103649992171450)
XLA Ops:
  7.2 0.0 all-reduce.12.cloned.1.call-start
  7.2 5.0 dynamic-slice_bitcast_fusion.2
  12.2 3.0 collective-permute-start.1
  15.2 17.2 %collective-permute-start = (f32[16,64,512]{2,1,0:T(8,128)}, f32[16,64,512]{2,1,0:T(8,128)}, u32[]{:S(2)}, u32[]{:S(2)}) collective-permute-start(f32[16,64,512]{2,1,0:T(8,128)} %get-tuple-element.123), channel_id=1, source_target_pairs={{0,0},{1,1},{2,4},{3,5},{4,2},{5,3},{6,6},{7,7},{8,8},{9,9},{10,12... | collective-permute-start | bytes 6291464 | tf_op jit(solution)/shard_map/ppermute | solution.py:633
  32.4 0.7 pad_add_fusion.info
  33.1 26.9 %collective-permute-done.1.b.refs_1_ = f32[16,64,512]{2,1,0:T(8,128)S(1)} collective-permute-done((f32[16,64,512]{2,1,0:T(8,128)}, f32[16,64,512]{2,1,0:T(8,128)S(1)}, u32[]{:S(2)}, u32[]{:S(2)}) %collective-permute-start.1) | collective-permute-done | bytes 2097184 | tf_op jit(solution)/shard_map/ppermute | solution.py:633
  60.0 1.3 copy-done
  61.4 8.2 %first_norm.1 = (f32[32,64,256]{2,1,0:T(8,128)}, f32[32,64,256]{2,1,0:T(8,128)}) custom-call(s32[2]{0:T(128)} %pad_add_fusion.info, f32[16,64,512]{2,1,0:T(8,128)} %collective-permute-done.a.refs_0_, f32[16,64,512]{2,1,0:T(8,128)} %copy-done, f32[2,2,512]{2,1,0:T(2,128)} %gains.3, f32[2,2,512]{2,1,0:T(2,128)} %refs_3_.5), custom_call_target="tpu_custom_call" | custom-call | bytes 8388608 | tf_op jit(solution)/shard_map/first_norm/pallas_call | solution.py:471
  69.5 46.4 %collective-permute-start.2 = (f32[32,64,256]{2,1,0:T(8,128)}, f32[32,64,256]{2,1,0:T(8,128)S(1)}, u32[]{:S(2)}, u32[]{:S(2)}) collective-permute-start(f32[32,64,256]{2,1,0:T(8,128)} %get-tuple-element.62), channel_id=1, source_target_pairs={{0,4},{4,0},{8,12},{12,8},{16,20},{20,16},{24,28},{28,24},{1,5},{5... | collective-permute-start | bytes 6291464 | tf_op jit(solution)/shard_map/ppermute | solution.py:645
  116.0 4.0 collective-permute-done.2.recv
  119.9 1.3 copy-done.15
  121.3 15.0 %spectral_forward_0.1 = (f32[32,64,256]{2,1,0:T(8,128)}, f32[32,64,256]{2,1,0:T(8,128)}, f32[2,1024,256]{2,1,0:T(8,128)}, f32[2,1024,256]{2,1,0:T(8,128)}, f32[2,1024,256]{2,1,0:T(8,128)}) custom-call(s32[2]{0:T(128)} %pad_add_fusion.info, f32[32,64,256]{2,1,0:T(8,128)} %get-tuple-element.61.own, f32[32,64,256]{2,1,0:T(8,128)} %copy-done.15, ...), custom_call_target="tpu_custom_call" | custom-call | flops 6000000000 | bytes 14680064 | tf_op jit(solution)/shard_map/spectral_forward_0/pallas_call | solution.py:500
  136.3 0.4 collective-permute-start.3
  136.7 4.0 collective-permute-done.3.refs_3_
  140.7 1.3 copy-done.17
  142.0 16.7 %ffn_forward_0.1 = (f32[32,64,512]{2,1,0:T(8,128)}, f32[32,64,512]{2,1,0:T(8,128)}, f32[32,64,512]{2,1,0:T(8,128)}, f32[32,64,256]{2,1,0:T(8,128)}, f32[32,64,256]{2,1,0:T(8,128)}) custom-call(s32[2]{0:T(128)} %pad_add_fusion.info, f32[16,64,512]{2,1,0:T(8,128)} %collective-permute-done.a.refs_0_, f32[16,64,512]{2,1,0:T(8,128)} %copy-done, ...), custom_call_target="tpu_custom_call" | custom-call | flops 6442450944 | bytes 25165824 | tf_op jit(solution)/shard_map/ffn_forward_0/pallas_call | solution.py:555
  158.7 0.4 collective-permute-start.4
  159.1 4.0 collective-permute-done.4.recv
  163.2 1.3 copy-done.14
  164.5 15.6 %spectral_forward_1.1 = (f32[32,64,256]{2,1,0:T(8,128)}, f32[32,64,256]{2,1,0:T(8,128)}, f32[2,1024,256]{2,1,0:T(8,128)}, f32[2,1024,256]{2,1,0:T(8,128)}, f32[2,1024,256]{2,1,0:T(8,128)}) custom-call(s32[2]{0:T(128)} %pad_add_fusion.info, f32[32,64,256]{2,1,0:T(8,128)} %get-tuple-element.66.own, f32[32,64,256]{2,1,0:T(8,128)} %copy-done.14, ...), custom_call_target="tpu_custom_call" | custom-call | flops 6000000000 | bytes 14680064 | tf_op jit(solution)/shard_map/spectral_forward_1/pallas_call | solution.py:500
  180.1 0.4 collective-permute-start.5
  180.5 2.0 dynamic-slice_bitcast_fusion
  182.5 1.0 collective-permute-start.6
  183.5 1.1 collective-permute-done.5.refs_2_
  184.6 16.5 %ffn_forward_1.1 = (f32[32,64,512]{2,1,0:T(8,128)}, f32[32,64,512]{2,1,0:T(8,128)}, f32[16,64,512]{2,1,0:T(8,128)}, f32[16,64,512]{2,1,0:T(8,128)}) custom-call(s32[2]{0:T(128)} %pad_add_fusion.info, f32[32,64,512]{2,1,0:T(8,128)} %get-tuple-element.65.refs_0_.refs_6_, f32[32,64,256]{2,1,0:T(8,128)} %get-tuple-element.68.refs_1_, ...), custom_call_target="tpu_custom_call" | custom-call | flops 6442450944 | bytes 25165824 | tf_op jit(solution)/shard_map/ffn_forward_1/pallas_call | solution.py:555
  201.1 31.3 %collective-permute-done.7.refs_7_ = f32[16,64,512]{2,1,0:T(8,128)S(1)} collective-permute-done((f32[16,64,512]{2,1,0:T(8,128)}, f32[16,64,512]{2,1,0:T(8,128)S(1)}, u32[]{:S(2)}, u32[]{:S(2)}) %collective-permute-start.7) | collective-permute-done | bytes 2097184 | tf_op jit(solution)/shard_map/ppermute | solution.py:633
  232.5 0.0 collective-permute-done.6.refs_6_
  232.5 1.3 copy-done.10
  233.8 0.7 copy-done.11
  234.5 23.8 %ffn_backward_1.1 = (f32[32,64,256]{2,1,0:T(8,128)}, f32[32,64,256]{2,1,0:T(8,128)}, f32[512,512]{1,0:T(8,128)}, f32[512,512]{1,0:T(8,128)}, f32[8,512]{1,0:T(8,128)}) custom-call(s32[2]{0:T(128)} %pad_add_fusion.info, f32[32,64,512]{2,1,0:T(8,128)} %get-tuple-element.77.refs_0_, f32[32,64,512]{2,1,0:T(8,128)} %get-tuple-element.78.refs_1_, ...), custom_call_target="tpu_custom_call" | custom-call | flops 12884901888 | bytes 25165824 | tf_op jit(solution)/shard_map/ffn_backward_1/pallas_call | solution.py:579
  258.2 41.9 %collective-permute-start.10 = (f32[32,64,256]{2,1,0:T(8,128)}, f32[32,64,256]{2,1,0:T(8,128)S(1)}, u32[]{:S(2)}, u32[]{:S(2)}) collective-permute-start(f32[32,64,256]{2,1,0:T(8,128)} %get-tuple-element.82.refs_8_), channel_id=1, source_target_pairs={{0,4},{4,0},{8,12},{12,8},{16,20},{20,16},{24,28},{28,24},{1,5},{5... | collective-permute-start | bytes 6291464 | tf_op jit(solution)/shard_map/ppermute | solution.py:645
  300.1 4.0 collective-permute-done.10.recv
  304.1 1.4 copy-done.16
  305.5 16.5 %spectral_backward_1.1 = (f32[32,64,256]{2,1,0:T(8,128)}, f32[32,64,256]{2,1,0:T(8,128)}, f32[2,2,2,128,128]{4,3,2,1,0:T(8,128)}, f32[2,2,2,1,128]{4,3,2,1,0:T(1,128)}) custom-call(s32[2]{0:T(128)} %pad_add_fusion.info, f32[32,64,256]{2,1,0:T(8,128)} %get-tuple-element.81.own.refs_7_, f32[32,64,256]{2,1,0:T(8,128)} %copy-done.16, ...), custom_call_target="tpu_custom_call" | custom-call | flops 12000000000 | bytes 14680064 | tf_op jit(solution)/shard_map/spectral_backward_1/pallas_call | solution.py:515
  322.0 0.4 collective-permute-start.11
  322.4 4.0 collective-permute-done.11.refs_10_
  326.4 1.4 copy-done.12
  327.9 27.2 %ffn_backward_0.1 = (f32[32,64,256]{2,1,0:T(8,128)}, f32[32,64,256]{2,1,0:T(8,128)}, f32[512,512]{1,0:T(8,128)}, f32[512,512]{1,0:T(8,128)}, f32[8,512]{1,0:T(8,128)}) custom-call(s32[2]{0:T(128)} %pad_add_fusion.info, f32[32,64,512]{2,1,0:T(8,128)} %get-tuple-element.75.refs_0_, f32[32,64,512]{2,1,0:T(8,128)} %get-tuple-element.76.refs_1_, ...), custom_call_target="tpu_custom_call" | custom-call | flops 12884901888 | bytes 25165824 | tf_op jit(solution)/shard_map/ffn_backward_0/pallas_call | solution.py:579
  355.0 0.4 collective-permute-start.12
  355.5 4.0 collective-permute-done.12.recv
  359.5 1.3 copy-done.13
  360.8 16.3 %spectral_backward_0.1 = (f32[32,64,256]{2,1,0:T(8,128)}, f32[32,64,256]{2,1,0:T(8,128)}, f32[2,2,2,128,128]{4,3,2,1,0:T(8,128)}, f32[2,2,2,1,128]{4,3,2,1,0:T(1,128)}) custom-call(s32[2]{0:T(128)} %pad_add_fusion.info, f32[32,64,256]{2,1,0:T(8,128)} %get-tuple-element.88.own.du_kept, f32[32,64,256]{2,1,0:T(8,128)} %copy-done.13, ...), custom_call_target="tpu_custom_call" | custom-call | flops 12000000000 | bytes 14680064 | tf_op jit(solution)/shard_map/spectral_backward_0/pallas_call | solution.py:515
  377.2 0.4 collective-permute-start.13
  377.6 2.2 collective-permute-start.8
  379.8 1.3 select_bitcast_fusion.4
  381.2 4.6 pad_maximum_fusion.3
  385.7 0.1 select_bitcast_fusion.5
  385.9 10.6 %input_gradient.1 = (f32[16,64,512]{2,1,0:T(8,128)}, f32[16,64,512]{2,1,0:T(8,128)}, f32[8,512]{1,0:T(8,128)}) custom-call(s32[2]{0:T(128)} %pad_add_fusion.info, f32[16,64,512]{2,1,0:T(8,128)} %collective-permute-done.a.refs_0_, f32[16,64,512]{2,1,0:T(8,128)} %copy-done, f32[32,64,256]{2,1,0:T(8,128)} %get-tuple-element.88.own.du_kept, ...), custom_call_target="tpu_custom_call" | custom-call | bytes 16777216 | tf_op jit(solution)/shard_map/input_gradient/pallas_call | solution.py:605
  396.5 17.2 %collective-permute-start.14 = (f32[16,64,512]{2,1,0:T(8,128)}, f32[16,64,512]{2,1,0:T(8,128)}, u32[]{:S(2)}, u32[]{:S(2)}) collective-permute-start(f32[16,64,512]{2,1,0:T(8,128)} %get-tuple-element.95), channel_id=1, source_target_pairs={{0,0},{1,1},{4,2},{5,3},{2,4},{3,5},{6,6},{7,7},{8,8},{9,9},{12,10... | collective-permute-start | bytes 6291464 | tf_op jit(solution)/shard_map/ppermute | solution.py:637
  413.7 2.0 collective-permute-start.15
  415.7 1.5 pad_maximum_fusion.2
  417.3 0.0 all-reduce.12.cloned.1.call-update
  417.3 0.7 copy-done.9
  418.0 0.0 copy-done.6
  418.1 0.8 fusion.2
  418.9 214.4 %all-reduce.8 = (f32[2,2,512]{2,1,0:T(2,128)}, f32[2,2,512]{2,1,0:T(2,128)}, f32[2,2,2,4,128]{4,3,2,1,0:T(4,128)}, f32[2,512]{1,0:T(2,128)}, f32[2,512]{1,0:T(2,128)}) all-reduce(f32[2,2,512]{2,1,0:T(2,128)S(1)} %pad_maximum_fusion.5, ...), channel_id=1, replica_groups=mesh['wide'=8,'section'=4] {'wide','section'}, use_global_device_ids=true, to_apply=%region_0.1 | all-reduce | flops 10240 | bytes 81920 | tf_op jit(solution)/shard_map/psum | solution.py:704
  633.4 4.0 select_bitcast_fusion.1
  637.4 2.5 pad_maximum_fusion.1
  639.9 2.5 pad_maximum_fusion
  642.3 2.4 all-reduce.12.cloned.1.call-done
  644.8 3.3 copy.30
  648.0 1.3 copy.31
  649.4 1.0 copy-done.2
  650.4 1.3 copy.32
  (42 shorter events, 0.2 us)
Async XLA Ops:
  7.2 637.6 %all-reduce.12.cloned.1.call-start = ((), (), s32[]{:S(2)}) async-start(), calls=%async_computation | async-start | bytes 12582912 | tf_op jit(solution)/shard_map/psum | solution.py:704
  12.2 47.8 %collective-permute-start.1 = (f32[16,64,512]{2,1,0:T(8,128)}, f32[16,64,512]{2,1,0:T(8,128)S(1)}, u32[]{:S(2)}, u32[]{:S(2)}) collective-permute-start(f32[16,64,512]{2,1,0:T(8,128)} %get-tuple-element.122), channel_id=1, source_target_pairs={{0,1},{1,0},{2,5},{3,4},{4,3},{5,2},{6,7},{7,6},{8,9},{9,8},{10,13... | collective-permute-start | bytes 6291464 | tf_op jit(solution)/shard_map/ppermute | solution.py:633
  15.2 44.8 %collective-permute-start = (f32[16,64,512]{2,1,0:T(8,128)}, f32[16,64,512]{2,1,0:T(8,128)}, u32[]{:S(2)}, u32[]{:S(2)}) collective-permute-start(f32[16,64,512]{2,1,0:T(8,128)} %get-tuple-element.123), channel_id=1, source_target_pairs={{0,0},{1,1},{2,4},{3,5},{4,2},{5,3},{6,6},{7,7},{8,8},{9,9},{10,12... | collective-permute-start | bytes 6291464 | tf_op jit(solution)/shard_map/ppermute | solution.py:633
  60.0 1.3 copy-start
  69.5 50.4 %collective-permute-start.2 = (f32[32,64,256]{2,1,0:T(8,128)}, f32[32,64,256]{2,1,0:T(8,128)S(1)}, u32[]{:S(2)}, u32[]{:S(2)}) collective-permute-start(f32[32,64,256]{2,1,0:T(8,128)} %get-tuple-element.62), channel_id=1, source_target_pairs={{0,4},{4,0},{8,12},{12,8},{16,20},{20,16},{24,28},{28,24},{1,5},{5... | collective-permute-start | bytes 6291464 | tf_op jit(solution)/shard_map/ppermute | solution.py:645
  119.9 1.3 copy-start.15
  136.3 4.4 collective-permute-start.3
  140.7 1.3 copy-start.17
  158.7 4.4 collective-permute-start.4
  163.2 1.3 copy-start.14
  164.5 16.0 %copy-start.1 = (f32[2,16,64,512]{3,2,1,0:T(8,128)S(1)}, f32[2,16,64,512]{3,2,1,0:T(8,128)}, u32[]{:S(2)}) copy-start(f32[2,16,64,512]{3,2,1,0:T(8,128)} %param.23) | copy-start | bytes 12582916
  180.1 4.5 collective-permute-start.5
  182.5 50.0 %collective-permute-start.7 = (f32[16,64,512]{2,1,0:T(8,128)}, f32[16,64,512]{2,1,0:T(8,128)S(1)}, u32[]{:S(2)}, u32[]{:S(2)}) collective-permute-start(f32[16,64,512]{2,1,0:T(8,128)} %get-tuple-element.120), channel_id=1, source_target_pairs={{0,1},{1,0},{2,5},{3,4},{4,3},{5,2},{6,7},{7,6},{8,9},{9,8},{10,13... | collective-permute-start | bytes 6291464 | tf_op jit(solution)/shard_map/ppermute | solution.py:633
  182.5 50.0 %collective-permute-start.6 = (f32[16,64,512]{2,1,0:T(8,128)S(1)}, f32[16,64,512]{2,1,0:T(8,128)S(1)}, u32[]{:S(2)}, u32[]{:S(2)}) collective-permute-start(f32[16,64,512]{2,1,0:T(8,128)S(1)} %get-tuple-element.121), channel_id=1, source_target_pairs={{0,0},{1,1},{2,4},{3,5},{4,2},{5,3},{6,6},{7,7},{8,8},{9,9},{10,12... | collective-permute-start | bytes 6291464 | tf_op jit(solution)/shard_map/ppermute | solution.py:633
  232.5 1.3 copy-start.10
  232.5 2.0 copy-start.11
  258.2 45.9 %collective-permute-start.10 = (f32[32,64,256]{2,1,0:T(8,128)}, f32[32,64,256]{2,1,0:T(8,128)S(1)}, u32[]{:S(2)}, u32[]{:S(2)}) collective-permute-start(f32[32,64,256]{2,1,0:T(8,128)} %get-tuple-element.82.refs_8_), channel_id=1, source_target_pairs={{0,4},{4,0},{8,12},{12,8},{16,20},{20,16},{24,28},{28,24},{1,5},{5... | collective-permute-start | bytes 6291464 | tf_op jit(solution)/shard_map/ppermute | solution.py:645
  304.1 1.4 copy-start.16
  322.0 4.4 collective-permute-start.11
  326.4 1.4 copy-start.12
  355.0 4.4 collective-permute-start.12
  359.5 1.3 copy-start.13
  377.2 4.0 copy-start.4
  377.2 8.7 %collective-permute-start.13 = (f32[32,64,256]{2,1,0:T(8,128)}, f32[32,64,256]{2,1,0:T(8,128)}, u32[]{:S(2)}, u32[]{:S(2)}) collective-permute-start(f32[32,64,256]{2,1,0:T(8,128)} %get-tuple-element.94), channel_id=1, source_target_pairs={{0,4},{4,0},{8,12},{12,8},{16,20},{20,16},{24,28},{28,24},{1,5},{5... | collective-permute-start | bytes 6291464 | tf_op jit(solution)/shard_map/ppermute | solution.py:645
  377.6 255.8 %collective-permute-start.8 = (f32[16,64,512]{2,1,0:T(8,128)}, f32[16,64,512]{2,1,0:T(8,128)S(1)}, u32[]{:S(2)}, u32[]{:S(2)}) collective-permute-start(f32[16,64,512]{2,1,0:T(8,128)} %get-tuple-element.73), channel_id=1, source_target_pairs={{0,0},{1,1},{4,2},{5,3},{2,4},{3,5},{6,6},{7,7},{8,8},{9,9},{12,10... | collective-permute-start | bytes 6291464 | tf_op jit(solution)/shard_map/ppermute | solution.py:637
  379.8 253.5 %collective-permute-start.9 = (f32[16,64,512]{2,1,0:T(8,128)}, f32[16,64,512]{2,1,0:T(8,128)}, u32[]{:S(2)}, u32[]{:S(2)}) collective-permute-start(f32[16,64,512]{2,1,0:T(8,128)} %get-tuple-element.74), channel_id=1, source_target_pairs={{1,0},{0,1},{5,2},{4,3},{3,4},{2,5},{7,6},{6,7},{9,8},{8,9},{13,10... | collective-permute-start | bytes 6291464 | tf_op jit(solution)/shard_map/ppermute | solution.py:638
  381.2 4.6 copy-start.5
  396.5 236.9 %collective-permute-start.14 = (f32[16,64,512]{2,1,0:T(8,128)}, f32[16,64,512]{2,1,0:T(8,128)}, u32[]{:S(2)}, u32[]{:S(2)}) collective-permute-start(f32[16,64,512]{2,1,0:T(8,128)} %get-tuple-element.95), channel_id=1, source_target_pairs={{0,0},{1,1},{4,2},{5,3},{2,4},{3,5},{6,6},{7,7},{8,8},{9,9},{12,10... | collective-permute-start | bytes 6291464 | tf_op jit(solution)/shard_map/ppermute | solution.py:637
  413.7 219.7 %collective-permute-start.15 = (f32[16,64,512]{2,1,0:T(8,128)}, f32[16,64,512]{2,1,0:T(8,128)}, u32[]{:S(2)}, u32[]{:S(2)}) collective-permute-start(f32[16,64,512]{2,1,0:T(8,128)} %get-tuple-element.96), channel_id=1, source_target_pairs={{1,0},{0,1},{5,2},{4,3},{3,4},{2,5},{7,6},{6,7},{9,8},{8,9},{13,10... | collective-permute-start | bytes 6291464 | tf_op jit(solution)/shard_map/ppermute | solution.py:638
  417.2 0.7 copy-start.9
  417.2 0.7 copy-start.7
  417.2 0.7 copy-start.6
  417.3 0.8 copy-start.8
  644.8 3.3 copy-start.3
  648.0 2.3 copy-start.2
Sparse Core Ops, SparseCore 0:
  417.4 227.3 all-reduce.11

commit v2 on v1

--- a/solution.py
+++ b/solution.py
@@ -366,7 +366,11 @@
     return result, column_sum(grad * unit), column_sum(grad)
 
 
-def ffn_backward_kernel(steps, fused, info, *refs):
+def lanes_first(values):
+    return [values[:, at : at + 128] for at in range(0, values.shape[1], 128)]
+
+
+def ffn_backward_kernel(steps, fused, by_member, info, *refs):
     step = pl.program_id(0)
     core = info[0]
     refs = list(refs)
@@ -378,7 +382,8 @@
     else:
         grad = picked(step, steps, refs[6:8])
         refs = refs[8:]
-    keep, send, up_grad, down_grad, small = refs
+    keep, send, *packed, up_grad, down_grad, small = refs
+    kept_grads, sent_grads = packed if by_member else (packed[0].at[0], packed[0].at[1])
 
     @pl.when(step == 0)
     def _():
@@ -402,6 +407,16 @@
         small[5:6] += late_bias
     parted(core, grad + norm_backward(outer, unit, scale, gains[1:2]), keep, send)
 
+    @pl.when(step == steps - 1)
+    def _():
+        width = up_grad.shape[0]
+        parts = zip(lanes_first(up_grad[...]), lanes_first(down_grad[...]), lanes_first(small[...]))
+        for index, (a, b, c) in enumerate(parts):
+            kept_grads[index, :width] = jnp.where(core == 0, a, b) if by_member else a
+            sent_grads[index, :width] = jnp.where(core == 0, b, a) if by_member else b
+            kept_grads[index, width:] = c
+            sent_grads[index, width:] = c
+
 
 def input_grad_kernel(steps, info, a, b, du_kept, du_sent, dh_kept, dh_taken, gains, first_out, second_out, small):
     step = pl.program_id(0)
@@ -417,7 +432,7 @@
     put_pieces(step, steps, (first_out, second_out), result)
 
 
-def call(kernel, grid, in_specs, out_specs, out_shapes, scratch, flops, moved, name):
+def call(kernel, grid, in_specs, out_specs, out_shapes, scratch, flops, moved, name, vmem=56):
     return pl.pallas_call(
         kernel,
         grid_spec=pltpu.PrefetchScalarGridSpec(
@@ -428,7 +443,7 @@
             scratch_shapes=scratch,
         ),
         out_shape=out_shapes,
-        compiler_params=pltpu.CompilerParams(vmem_limit_bytes=56 * 2**20),
+        compiler_params=pltpu.CompilerParams(vmem_limit_bytes=vmem * 2**20),
         cost_estimate=pl.CostEstimate(flops=int(flops), bytes_accessed=int(moved), transcendentals=0),
         name=name,
     )
@@ -568,6 +583,8 @@
 def ffn_backward(plan, layer, info, mixed, before, gains, biases, up, down, grads):
     width, hidden = plan.width, plan.hidden
     fused = len(grads) == 5
+    packed = (width // 128, hidden + 8, 128)
+    packed = [packed, packed] if layer == 0 else [(2, *packed)]
     specs = [plan.row, plan.wide_row, plan.norm(layer), plan.norm(layer)]
     specs += [plan.matrix(layer, width, hidden), plan.matrix(layer, hidden, width)]
     args = [mixed, before, gains, biases, up, down, *grads]
@@ -577,24 +594,20 @@
     else:
         specs += [plan.first, plan.second]
     return call(
-        functools.partial(ffn_backward_kernel, plan.steps, fused),
+        functools.partial(ffn_backward_kernel, plan.steps, fused, layer == 0),
         plan.steps,
         specs,
         [
             plan.half_row,
             plan.half_row,
-            plan.whole((width, hidden)),
-            plan.whole((hidden, width)),
-            plan.whole((8, width)),
+            *[plan.whole(shape) for shape in packed],
         ],
         [
             plan.half_shape,
             plan.half_shape,
-            jax.ShapeDtypeStruct((width, hidden), F32),
-            jax.ShapeDtypeStruct((hidden, width), F32),
-            jax.ShapeDtypeStruct((8, width), F32),
+            *[jax.ShapeDtypeStruct(shape, F32) for shape in packed],
         ],
-        [],
+        [pltpu.VMEM(shape, F32) for shape in ((width, hidden), (hidden, width), (8, width))],
         3 * 8 * 2048 * width * hidden,
         24 * 2**20,
         f"ffn_backward_{layer}",
@@ -627,22 +640,210 @@
     return routes
 
 
-def gather_pieces(shard, parity, routes):
-    first = lax.dynamic_index_in_dim(shard, parity, 0, keepdims=False)
-    second = lax.dynamic_index_in_dim(shard, 1 - parity, 0, keepdims=False)
-    return lax.ppermute(first, BOTH, routes[0]), lax.ppermute(second, BOTH, routes[1])
-
-
-def scatter_pieces(first, second, parity, routes):
-    first = lax.ppermute(first, BOTH, [(b, a) for a, b in routes[0]])
-    second = lax.ppermute(second, BOTH, [(b, a) for a, b in routes[1]])
-    low = jnp.where(parity == 0, first, second)
-    high = jnp.where(parity == 0, second, first)
-    return jnp.stack([low, high])
+def copy_kernel(info, source, *refs):
+    refs[-1][...] = source[...]
+
+
+def pick(info, shard, flip, after=()):
+    items, rows, *cell = shard.shape
+    anywhere = pl.BlockSpec(memory_space=pl.ANY)
+    return call(
+        copy_kernel,
+        rows // ROWS,
+        [pl.BlockSpec((None, ROWS, *cell), lambda j, s: (s[1] ^ flip, j, 0, 0))] + [anywhere] * len(after),
+        pl.BlockSpec((ROWS, *cell), lambda j, s: (j, 0, 0)),
+        jax.ShapeDtypeStruct((rows, *cell), F32),
+        [],
+        0,
+        0,
+        "pick",
+        16,
+    )(info, shard, *after)
+
+
+def pass_kernel(count, *refs):
+    pass
+
+
+def passed(values, after):
+    anywhere = pl.BlockSpec(memory_space=pl.ANY)
+    return pl.pallas_call(
+        functools.partial(pass_kernel, len(values)),
+        in_specs=[anywhere] * (len(values) + len(after)),
+        out_specs=[anywhere] * len(values),
+        out_shape=[jax.ShapeDtypeStruct(v.shape, v.dtype) for v in values],
+        input_output_aliases={i: i for i in range(len(values))},
+        name="passed",
+    )(*values, *after)
+
+
+def send_piece(piece, route):
+    return lax.ppermute(piece, BOTH, route)
+
+
+def join_kernel(steps, info, first, second, *refs):
+    step = pl.program_id(0)
+    from_first = (step // steps) == info[1]
+    refs[-1][...] = jnp.where(from_first, first[...], second[...])
+
+
+def join(info, first, second, after=()):
+    rows, *cell = first.shape
+    steps = rows // ROWS
+    anywhere = pl.BlockSpec(memory_space=pl.ANY)
+
+    def piece(flip):
+        def place(j, s):
+            return (jnp.where(j // steps == s[1] ^ flip, j % steps, (1 - j // steps) * (steps - 1)), 0, 0)
+
+        return pl.BlockSpec((ROWS, *cell), place)
+
+    return call(
+        functools.partial(join_kernel, steps),
+        2 * steps,
+        [piece(0), piece(1)] + [anywhere] * len(after),
+        pl.BlockSpec((None, ROWS, *cell), lambda j, s: (j // steps, j % steps, 0, 0)),
+        jax.ShapeDtypeStruct((2, rows, *cell), F32),
+        [],
+        0,
+        0,
+        "join",
+        16,
+    )(info, first, second, *after)
+
+
+def as_one(function, *args):
+    def empty(*args):
+        return jax.tree.map(lambda leaf: jnp.zeros(leaf.shape, leaf.dtype), jax.eval_shape(function, *args))
+
+    return lax.cond(lax.axis_index("wide") < lax.axis_size("wide"), function, empty, *args)
 
 
 def swap(values):
     return lax.ppermute(values, "wide", [(i, i ^ 1) for i in range(lax.axis_size("wide"))])
+
+
+def digits(size, low, most):
+    found = []
+    while 1 << low < size:
+        radix = most if most << low <= size else 2
+        found.append((low, radix))
+        low += radix.bit_length() - 1
+    return found
+
+
+def partners(axis, bit, offset):
+    return [(i, i ^ offset << bit) for i in range(lax.axis_size(axis))]
+
+
+def sum_spread(values, axis, bit, radix):
+    me = (lax.axis_index(axis) >> bit) % radix
+    parts = values.reshape((radix, -1) + values.shape[1:])
+    total = lax.dynamic_index_in_dim(parts, me, 0, keepdims=False)
+    for offset in range(1, radix):
+        part = lax.dynamic_index_in_dim(parts, me ^ offset, 0, keepdims=False)
+        total = total + lax.ppermute(part, axis, partners(axis, bit, offset))
+    return total
+
+
+def collect(values, axis, bit, radix):
+    me = (lax.axis_index(axis) >> bit) % radix
+    out = jnp.zeros((radix,) + values.shape, F32)
+    for offset in range(radix):
+        got = lax.ppermute(values, axis, partners(axis, bit, offset)) if offset else values
+        out = lax.dynamic_update_index_in_dim(out, got, me ^ offset, 0)
+    return out.reshape((-1,) + values.shape[1:])
+
+
+def spread_steps(axis, low, most):
+    return [(axis, *digit) for digit in digits(lax.axis_size(axis), low, most)]
+
+
+def sum_spread_all(values, steps):
+    for step in steps:
+        values = sum_spread(values, *step)
+    return values
+
+
+def collect_all(values, steps):
+    for step in steps[::-1]:
+        values = collect(values, *step)
+    return values
+
+
+def packed_rows(parts, unit):
+    rows = [part.reshape(-1, 128) for part in parts]
+    missing = -sum(row.shape[0] for row in rows) % unit
+    return jnp.concatenate(rows + [jnp.zeros((missing, 128), F32)])
+
+
+def unpack_kernel(cuts, info, mine, other, second, *outs):
+    gain_out, bias_out, mix_out, offset_out, up_out, up_offset_out, down_out, down_offset_out = outs
+    core = info[0]
+    low = jnp.where(core == 0, mine[...], other[...])
+    high = jnp.where(core == 0, other[...], mine[...])
+    width = up_out.shape[1]
+    rows, lanes = width + 8, width // 128
+    down_at, mix_at = lanes * rows, 2 * lanes * rows
+    for index in range(lanes):
+        at = pl.ds(index * 128, 128)
+        begin = index * rows
+        up_out[0, :, at] = low[begin : begin + width]
+        down_out[0, :, at] = high[begin : begin + width]
+        up_out[1, :, at] = second[begin : begin + width]
+        down_out[1, :, at] = second[down_at + begin : down_at + begin + width]
+        small = low[begin + width : begin + rows]
+        late = second[begin + width : begin + rows]
+        inner = [low[row : row + 1] + high[row : row + 1] for row in (cuts[3] + index, cuts[3] + lanes + index)]
+        gain_out[0, 0:1, at] = inner[0]
+        bias_out[0, 0:1, at] = inner[1]
+        gain_out[0, 1:2, at] = small[0:1]
+        bias_out[0, 1:2, at] = small[1:2]
+        gain_out[1, 0:1, at] = small[4:5]
+        bias_out[1, 0:1, at] = small[5:6]
+        gain_out[1, 1:2, at] = late[0:1]
+        bias_out[1, 1:2, at] = late[1:2]
+        up_offset_out[0:1, at] = small[2:3]
+        up_offset_out[1:2, at] = late[2:3]
+        down_offset_out[0:1, at] = small[3:4]
+        down_offset_out[1:2, at] = late[3:4]
+    mix_rows = mix_out[1].size // 128
+    mix_out[1] = second[mix_at : mix_at + mix_rows].reshape(mix_out.shape[1:])
+    for j in range(2):
+        for part in range(2):
+            begin = mix_at + mix_rows + (2 * j + part) * BLOCKS
+            offset_out[1, j, part] = second[begin : begin + BLOCKS]
+            for block in range(2):
+                index = (2 * j + part) * 2 + block
+                begin = cuts[1] + index * 128
+                mix_out[0, j, part, block] = low[begin : begin + 128]
+                mix_out[0, j, part, 2 + block] = high[begin : begin + 128]
+                begin = cuts[2] + index
+                offset_out[0, j, part, block : block + 1] = low[begin : begin + 1]
+                offset_out[0, j, part, 2 + block : 3 + block] = high[begin : begin + 1]
+
+
+def unpack(info, cuts, args, shapes):
+    def whole(shape):
+        return pl.BlockSpec(shape, lambda j, s: (0,) * len(shape))
+
+    return call(
+        functools.partial(unpack_kernel, cuts),
+        1,
+        [whole(arg.shape) for arg in args],
+        [whole(shape) for shape in shapes],
+        [jax.ShapeDtypeStruct(shape, F32) for shape in shapes],
+        [],
+        0,
+        0,
+        "unpack",
+        40,
+    )(info, *args)
+
+
+def whole_blocks(core, part):
+    empty = jnp.zeros_like(part)
+    return jnp.where(core == 0, jnp.concatenate([part, empty], 2), jnp.concatenate([empty, part], 2))
 
 
 def on_device(
@@ -666,45 +867,74 @@
     plain, weighted = column_tables()
     tables = [jnp.asarray(split_table(t)) for t in (plain, weighted, plain.T, weighted.T)]
 
-    xa, xb = gather_pieces(inputs, parity, routes)
-    out_grad, xa, xb = lax.optimization_barrier((out_grad, xa, xb))
-    ga, gb = gather_pieces(out_grad, parity, routes)
-
+    back_routes = [[(b, a) for a, b in route] for route in routes]
     ffn_args = (norm_gain, norm_bias, up_weight, up_bias, down_weight, down_bias)
-    keep, send = first_norm(plan, info, xa, xb, norm_gain, norm_bias)
-    keep, send, *saved0 = spectral_forward(plan, 0, info, keep, swap(send), mix_weight, mix_bias, tables)
-    u0, a0, x1, keep, send = ffn_forward(plan, 0, True, info, (xa, xb), keep, swap(send), *ffn_args)
-    keep, send, *saved1 = spectral_forward(plan, 1, info, keep, swap(send), mix_weight, mix_bias, tables)
-    u1, a1, va, vb = ffn_forward(plan, 1, False, info, (x1,), keep, swap(send), *ffn_args)
-
-    va, vb, ga, gb = lax.optimization_barrier((va, vb, ga, gb))
-    outputs = scatter_pieces(va, vb, parity, routes)
-
     back_args = (norm_gain, norm_bias, up_weight, down_weight)
-    du1 = ffn_backward(plan, 1, info, u1, a1, *back_args, (ga, gb))
-    dh1 = spectral_backward(plan, 1, info, du1[0], swap(du1[1]), mix_weight, saved1, tables)
-    late = (x1, du1[0], du1[1], dh1[0], swap(dh1[1]))
-    du0 = ffn_backward(plan, 0, info, u0, a0, *back_args, late)
-    dh0 = spectral_backward(plan, 0, info, du0[0], swap(du0[1]), mix_weight, saved0, tables)
-    dxa, dxb, small = input_gradient(plan, info, xa, xb, du0[:2], (dh0[0], swap(dh0[1])), norm_gain)
-    input_grad = scatter_pieces(dxa, dxb, parity, routes)
-
-    def placed(part):
-        empty = jnp.zeros_like(part)
-        return jnp.where(core == 0, jnp.concatenate([part, empty], 2), jnp.concatenate([empty, part], 2))
-
-    mix_grads = jnp.stack([placed(dh0[2]), placed(dh1[2])])
-    offset_grads = jnp.stack([placed(dh0[3]), placed(dh1[3])])[:, :, :, :, 0]
-    gain_grads = jnp.stack([jnp.stack([small[0], du0[4][0]]), jnp.stack([du0[4][4], du1[4][0]])])
-    bias_grads = jnp.stack([jnp.stack([small[1], du0[4][1]]), jnp.stack([du0[4][5], du1[4][1]])])
-    up_grads = jnp.stack([du0[2], du1[2]])
-    down_grads = jnp.stack([du0[3], du1[3]])
-    up_offset_grads = jnp.stack([du0[4][2], du1[4][2]])
-    down_offset_grads = jnp.stack([du0[4][3], du1[4][3]])
-    summed = lax.psum(
-        (gain_grads, bias_grads, mix_grads, offset_grads, up_grads, up_offset_grads, down_grads, down_offset_grads), BOTH
-    )
-    return (outputs, input_grad, *summed)
+
+    def forward(xa, xb):
+        keep, send = first_norm(plan, info, xa, xb, norm_gain, norm_bias)
+        keep, send, *saved0 = spectral_forward(plan, 0, info, keep, swap(send), mix_weight, mix_bias, tables)
+        u0, a0, x1, keep, send = ffn_forward(plan, 0, True, info, (xa, xb), keep, swap(send), *ffn_args)
+        keep, send, *saved1 = spectral_forward(plan, 1, info, keep, swap(send), mix_weight, mix_bias, tables)
+        u1, a1, va, vb = ffn_forward(plan, 1, False, info, (x1,), keep, swap(send), *ffn_args)
+        return (va, vb), (saved0, u0, a0, x1, saved1, u1, a1)
+
+    def backward(xa, xb, ga, gb, saved):
+        saved0, u0, a0, x1, saved1, u1, a1 = saved
+        keep, send, matrices = ffn_backward(plan, 1, info, u1, a1, *back_args, (ga, gb))
+        dh_keep, dh_send, mix, offsets = spectral_backward(plan, 1, info, keep, swap(send), mix_weight, saved1, tables)
+        late = (x1, keep, send, dh_keep, swap(dh_send))
+        mixing = [whole_blocks(core, part).reshape(-1, 128) for part in (mix, offsets)]
+        second = packed_rows([matrices, *mixing], lax.axis_size("wide") * lax.axis_size("section") * 8)
+        second = lax.psum_scatter(second, "wide", scatter_dimension=0, tiled=True)
+        return *as_one(backward_first, xa, xb, late, (saved0, u0, a0)), second
+
+    def backward_first(xa, xb, late, saved):
+        saved0, u0, a0 = saved
+        keep, send, *matrices = ffn_backward(plan, 0, info, u0, a0, *back_args, late)
+        dh_keep, dh_send, mix, offsets = spectral_backward(plan, 0, info, keep, swap(send), mix_weight, saved0, tables)
+        last = ((keep, send), (dh_keep, swap(dh_send)))
+        dxa, dxb, inner = input_gradient(plan, info, xa, xb, *last, norm_gain)
+        return (dxa, dxb), (matrices, mix, offsets, inner)
+
+    members = spread_steps("wide", 1, 4)
+    sections = spread_steps("section", 0, 2)
+
+    def reduce_gradients(matrices, mix, offsets, inner, second):
+        mine = matrices[0] + swap(matrices[1])
+        parts = [mine, mix, offsets, inner.reshape(8, -1, 128)]
+        unit = lax.axis_size("wide") // 2 * lax.axis_size("section") * 8
+        first = sum_spread_all(packed_rows(parts, unit), members)
+        both = sum_spread_all(jnp.stack([first, second], axis=1).reshape(-1, 2, 128), sections)
+        both = collect_all(both, sections)
+        return both[:, 0], both[:, 1]
+
+    def share_first(first, outputs):
+        summed = collect_all(first, members)
+        return join(info, *outputs), summed, swap(summed)
+
+    def share_gradients(first, second, outputs):
+        second = lax.all_gather(second, "wide", axis=0, tiled=True)
+        return *as_one(share_first, first, outputs), second
+
+    xa = send_piece(pick(info, inputs, 0), routes[0])
+    xb = send_piece(pick(info, inputs, 1), routes[1])
+    picked_grads = pick(info, out_grad, 0), pick(info, out_grad, 1)
+    ga, gb = [send_piece(piece, route) for piece, route in zip(passed(picked_grads, (xa, xb)), routes)]
+    results, saved = as_one(forward, xa, xb)
+    outputs = [send_piece(piece, route) for piece, route in zip(passed(results, (ga, gb)), back_routes)]
+    (dxa, dxb), local, second = as_one(backward, xa, xb, ga, gb, saved)
+    dxa = send_piece(*passed([dxa], outputs), back_routes[0])
+    first, second = as_one(reduce_gradients, *local, second)
+    dxb = send_piece(*passed([dxb], [dxa, first]), back_routes[1])
+    outputs, mine, other, second = as_one(share_gradients, first, second, outputs)
+
+    sizes = [part.size // 128 for part in (local[0][0], local[1], local[2])]
+    cuts = [0, sizes[0], sizes[0] + sizes[1], sum(sizes)]
+    args = [mine, other, second]
+    shapes = [a.shape for a in (norm_gain, norm_bias, mix_weight, mix_bias, up_weight, up_bias, down_weight, down_bias)]
+    gradients = unpack(info, cuts, args, shapes)
+    return (outputs, join(info, dxa, dxb, gradients[:1]), *gradients)
 
 
 def solution(mesh):

time: 662 us -> 508 us (0.77)
  blocking collectives: 214 us -> 0 us
  waiting for transfers between devices: 85.8 us -> 179 us
  starting transfers between devices: 134 us -> 89.2 us
  Pallas kernels: 166 us -> 186 us
    psum x1 -> x0, blocking collectives: 214 us -> none  [on_device(): lax.psum((gain_grads, bias_grads, mix_grads, offset_grads, up_grads, up_o...]
    ppermute x8 -> x18, waiting for transfers between devices: 58.3 us -> 136 us  [the longest x5 53.5 us: sum_spread(): total = total + lax.ppermute(part, axis, partners(axis, bit, offset))]
    ppermute x8 -> x10, starting transfers between devices: 90.9 us -> 38.5 us  [swap(): lax.ppermute(values, 'wide', [(i, i ^ 1) for i in range(lax.axis_size('wi...]
    pallas_call x2 -> x13, Pallas kernels: 51 us -> 74.3 us  [the longest x2 52.6 us: ffn_backward(): call(functools.partial(ffn_backward_kernel, plan.steps, fused, layer == 0...]
    another operation x13 -> x0, other arithmetic: 16.5 us -> none  [the longest x3 8.95 us: scatter_pieces(): return jnp.stack([low, high])]
    unnamed x39 -> x24, local copies, waits for them, and re-layouts: 19.1 us -> 6.05 us
    ppermute x8 -> x10, waiting for transfers between devices: 25.1 us -> 35.3 us  [swap(): lax.ppermute(values, 'wide', [(i, i ^ 1) for i in range(lax.axis_size('wi...]
    cond x0 -> x28, local copies, waits for them, and re-layouts: none -> 9.15 us
  transfers between devices with their start and end apart: 17 -> 30, of which waited for: 10 -> 20; matrix products, arithmetic and copies ran while one was open for 3% -> 4% of each run, Pallas kernels for 4% -> 36%
where the time goes in v2:
time: 508 us; the launch traced here: 504 us
  Pallas kernels  186 us (37%)
  waiting for transfers between devices  179 us (35%)
  starting transfers between devices  89.2 us (18%)
  local copies, waits for them, and re-layouts  21.8 us (4%)
  between operations  14.2 us (3%)
  other arithmetic  13.8 us (3%)
    ppermute x5, waiting for transfers between devices, sum_spread(): total = total + lax.ppermute(part, axis, partners(axis, bit, offset))  53.5 us
    pallas_call x2, Pallas kernels, ffn_backward(): call(functools.partial(ffn_backward_kernel, plan.steps, fused, layer == 0...  52.6 us
    ppermute x8, starting transfers between devices, send_piece(): return lax.ppermute(piece, BOTH, route)  42.7 us
    ppermute x8, waiting for transfers between devices, send_piece(): return lax.ppermute(piece, BOTH, route)  42.7 us
    ppermute x5, waiting for transfers between devices, collect(): lax.ppermute(values, axis, partners(axis, bit, offset))  39.9 us
    ppermute x10, starting transfers between devices, swap(): lax.ppermute(values, 'wide', [(i, i ^ 1) for i in range(lax.axis_size('wi...  38.5 us
    ppermute x10, waiting for transfers between devices, swap(): lax.ppermute(values, 'wide', [(i, i ^ 1) for i in range(lax.axis_size('wi...  35.3 us
    pallas_call x2, Pallas kernels, spectral_backward(): call(spectral_backward_kernel, 2, [cells, cells, weight, modes, modes, mo...  33.1 us
  transfers between devices with their start and end apart: 30, of which 20 were waited for; matrix products, arithmetic and copies ran while one was open for 4% of the time, Pallas kernels for 36%

profile of v2, /device:TPU:0, one launch (start us, length us, event | category | flops | bytes accessed | tf_op | source)
XLA Modules:
  0.0 504.5 jit_solution(8553225981769926852)
XLA Ops:
  7.3 2.2 copy-done
  11.9 3.1 collective-permute-start.21
  17.1 1.3 copy-done.5
  18.4 42.7 %collective-permute-done.21.refs_3_ = f32[16,64,512]{2,1,0:T(8,128)} collective-permute-done((f32[16,64,512]{2,1,0:T(8,128)S(1)}, f32[16,64,512]{2,1,0:T(8,128)}, u32[]{:S(2)}, u32[]{:S(2)}) %collective-permute-start.21) | collective-permute-done | bytes 2097184 | tf_op jit(solution)/shard_map/ppermute | solution.py:681
  61.1 17.1 %collective-permute-start.22 = (f32[16,64,512]{2,1,0:T(8,128)}, f32[16,64,512]{2,1,0:T(8,128)}, u32[]{:S(2)}, u32[]{:S(2)}) collective-permute-start(f32[16,64,512]{2,1,0:T(8,128)} %get-tuple-element.316), channel_id=1, source_target_pairs={{0,0},{1,1},{2,4},{3,5},{4,2},{5,3},{6,6},{7,7},{8,8},{9,9},{10,12... | collective-permute-start | bytes 6291464 | tf_op jit(solution)/shard_map/ppermute | solution.py:681
  78.2 1.7 collective-permute-start.23
  80.0 121.8 %conditional.6 = (f32[16,64,512]{2,1,0:T(8,128)}, f32[16,64,512]{2,1,0:T(8,128)}, f32[2,1024,256]{2,1,0:T(8,128)}, f32[2,1024,256]{2,1,0:T(8,128)}, f32[2,1024,2...) conditional(s32[]{:T(128)} %convert_element_type.12, () %tuple.57, ...), branch_computations={%region_0.1_spmd, %region_1.2_spmd} | conditional | flops 24884901888 | bytes 155189600 | solution.py:719
  80.0 7.4 %first_norm.1 = (f32[32,64,256]{2,1,0:T(8,128)}, f32[32,64,256]{2,1,0:T(8,128)}) custom-call(s32[2]{0:T(128)S(1)} %get-tuple-element.144.info, f32[16,64,512]{2,1,0:T(8,128)S(1)} %get-tuple-element.145.a.refs_0_, f32[16,64,512]{2,1,0:T(8,128)} %get-tuple-element.146.b.refs_1_, f32[2,2,512]{2,1,0:T(2,128)S(1)} %get-tuple-element.147.gains.refs_4_.refs_10_.refs_3_, ...), custom_call_target="tpu_custom_call" | custom-call | bytes 8388608 | tf_op jit(solution)/shard_map/cond/branch_1_fun/first_norm/pallas_call | solution.py:486
  87.4 32.8 %collective-permute-start = (f32[32,64,256]{2,1,0:T(8,128)}, f32[32,64,256]{2,1,0:T(8,128)S(1)}, u32[]{:S(2)}, u32[]{:S(2)}) collective-permute-start(f32[32,64,256]{2,1,0:T(8,128)} %get-tuple-element.150), channel_id=1, source_target_pairs={{0,4},{4,0},{8,12},{12,8},{16,20},{20,16},{24,28},{28,24},{1,5},{5... | collective-permute-start | bytes 6291464 | tf_op jit(solution)/shard_map/cond/branch_1_fun/ppermute | solution.py:723
  120.2 4.0 collective-permute-done.recv
  124.2 1.3 copy-done.16
  125.5 14.9 %spectral_forward_0.1 = (f32[32,64,256]{2,1,0:T(8,128)}, f32[32,64,256]{2,1,0:T(8,128)}, f32[2,1024,256]{2,1,0:T(8,128)}, f32[2,1024,256]{2,1,0:T(8,128)}, f32[2,1024,256]{2,1,0:T(8,128)}) custom-call(s32[2]{0:T(128)S(1)} %get-tuple-element.144.info, f32[32,64,256]{2,1,0:T(8,128)} %get-tuple-element.149.own, f32[32,64,256]{2,1,0:T(8,128)} %copy-done.16, ...), custom_call_target="tpu_custom_call" | custom-call | flops 6000000000 | bytes 14680064 | tf_op jit(solution)/shard_map/cond/branch_1_fun/spectral_forward_0/pallas_call | solution.py:515
  140.7 4.1 collective-permute-done.1.refs_3_
  144.9 15.8 %ffn_forward_0.1 = (f32[32,64,512]{2,1,0:T(8,128)}, f32[32,64,512]{2,1,0:T(8,128)}, f32[32,64,512]{2,1,0:T(8,128)}, f32[32,64,256]{2,1,0:T(8,128)}, f32[32,64,256]{2,1,0:T(8,128)}) custom-call(s32[2]{0:T(128)S(1)} %get-tuple-element.144.info, f32[16,64,512]{2,1,0:T(8,128)S(1)} %get-tuple-element.145.a.refs_0_, f32[16,64,512]{2,1,0:T(8,128)} %get-tuple-element.146.b.refs_1_, ...), custom_call_target="tpu_custom_call" | custom-call | flops 6442450944 | bytes 25165824 | tf_op jit(solution)/shard_map/cond/branch_1_fun/ffn_forward_0/pallas_call | solution.py:570
  161.0 4.1 collective-permute-done.2.recv
  165.2 14.8 %spectral_forward_1.1 = (f32[32,64,256]{2,1,0:T(8,128)}, f32[32,64,256]{2,1,0:T(8,128)}, f32[2,1024,256]{2,1,0:T(8,128)}, f32[2,1024,256]{2,1,0:T(8,128)}, f32[2,1024,256]{2,1,0:T(8,128)}) custom-call(s32[2]{0:T(128)S(1)} %get-tuple-element.144.info, f32[32,64,256]{2,1,0:T(8,128)} %get-tuple-element.162.own, f32[32,64,256]{2,1,0:T(8,128)} %collective-permute-done.2.recv, ...), custom_call_target="tpu_custom_call" | custom-call | flops 6000000000 | bytes 14680064 | tf_op jit(solution)/shard_map/cond/branch_1_fun/spectral_forward_1/pallas_call | solution.py:515
  180.3 4.0 collective-permute-done.3.refs_2_
  184.3 1.3 copy-done.17
  185.7 16.1 %ffn_forward_1.1 = (f32[32,64,512]{2,1,0:T(8,128)}, f32[32,64,512]{2,1,0:T(8,128)}, f32[16,64,512]{2,1,0:T(8,128)}, f32[16,64,512]{2,1,0:T(8,128)}) custom-call(s32[2]{0:T(128)S(1)} %get-tuple-element.144.info, f32[32,64,512]{2,1,0:T(8,128)} %get-tuple-element.426.refs_0_, f32[32,64,256]{2,1,0:T(8,128)} %get-tuple-element.164.refs_1_, ...), custom_call_target="tpu_custom_call" | custom-call | flops 6442450944 | bytes 25165824 | tf_op jit(solution)/shard_map/cond/branch_1_fun/ffn_forward_1/pallas_call | solution.py:570
  201.7 17.1 %collective-permute-start.24 = (f32[16,64,512]{2,1,0:T(8,128)}, f32[16,64,512]{2,1,0:T(8,128)}, u32[]{:S(2)}, u32[]{:S(2)}) collective-permute-start(f32[16,64,512]{2,1,0:T(8,128)} %get-tuple-element.318), channel_id=1, source_target_pairs={{0,0},{1,1},{4,2},{5,3},{2,4},{3,5},{6,6},{7,7},{8,8},{9,9},{12,10... | collective-permute-start | bytes 6291464 | tf_op jit(solution)/shard_map/ppermute | solution.py:681
  219.2 125.5 %conditional.7 = (f32[16,64,512]{2,1,0:T(8,128)}, f32[16,64,512]{2,1,0:T(8,128)}, f32[4,520,128]{2,1,0:T(8,128)}, f32[4,520,128]{2,1,0:T(8,128)}, f32[2,2,2,128,...) conditional(s32[]{:T(128)} %convert_element_type.12, () %tuple.60, ...), branch_computations={%region_2.3_spmd, %region_3.7_spmd} | conditional | flops 49772527616 | bytes 183132240 | solution.py:719
  219.2 24.3 %ffn_backward_1.1 = (f32[32,64,256]{2,1,0:T(8,128)}, f32[32,64,256]{2,1,0:T(8,128)}, f32[2,4,520,128]{3,2,1,0:T(8,128)}) custom-call(s32[2]{0:T(128)S(1)} %get-tuple-element.209.info, f32[32,64,512]{2,1,0:T(8,128)} %get-tuple-element.217.refs_0_, f32[32,64,512]{2,1,0:T(8,128)} %get-tuple-element.218.refs_1_, f32[2,2,512]{2,1,0:T(2,128)S(1)} %get-tuple-element.212.refs_2_, ...), custom_call_target="tpu_custom_call" | custom-call | flops 12884901888 | bytes 25165824 | tf_op jit(solution)/shard_map/cond/branch_1_fun/ffn_backward_1/pallas_call | solution.py:596
  243.6 4.4 collective-permute-done.6.recv
  248.1 16.4 %spectral_backward_1.1 = (f32[32,64,256]{2,1,0:T(8,128)}, f32[32,64,256]{2,1,0:T(8,128)}, f32[2,2,2,128,128]{4,3,2,1,0:T(8,128)}, f32[2,2,2,1,128]{4,3,2,1,0:T(1,128)}) custom-call(s32[2]{0:T(128)S(1)} %get-tuple-element.209.info, f32[32,64,256]{2,1,0:T(8,128)} %get-tuple-element.221.own, f32[32,64,256]{2,1,0:T(8,128)} %collective-permute-done.6.recv, ...), custom_call_target="tpu_custom_call" | custom-call | flops 12000000000 | bytes 14680064 | tf_op jit(solution)/shard_map/cond/branch_1_fun/spectral_backward_1/pallas_call | solution.py:530
  264.5 1.3 pad_select_fusion
  266.5 6.9 %maximum_maximum_fusion = f32[6400,128]{1,0:T(8,128)} fusion(f32[16,128]{1,0:T(8,128)S(1)} %bitcast.75, f32[2048,128]{1,0:T(8,128)S(1)} %bitcast.66, f32[4160,128]{1,0:T(8,128)S(1)} %bitcast.70, f32[6400]{0:T(1024)S(1)} %pad.7.clone), kind=kLoop, calls=%fused_computation | loop fusion | flops 2457600 | bytes 6489088 | tf_op jit(solution)/shard_map/cond/branch_1_fun/concatenate | solution.py:777
  273.7 4.4 collective-permute-done.7
  278.1 66.6 %conditional = (f32[16,64,512]{2,1,0:T(8,128)}, f32[16,64,512]{2,1,0:T(8,128)}, f32[4,520,128]{2,1,0:T(8,128)}, f32[4,520,128]{2,1,0:T(8,128)}, f32[2,2,2,128,12...) conditional(s32[]{:T(128)} %convert_element_type.0, () %tuple.35, (s32[2]{0:T(128)S(1)}, ...), branch_computations={%region_4.4_spmd, %region_5.5_spmd} | conditional | flops 24884901888 | bytes 98566368 | solution.py:719
  278.1 28.3 %ffn_backward_0.1 = (f32[32,64,256]{2,1,0:T(8,128)}, f32[32,64,256]{2,1,0:T(8,128)}, f32[4,520,128]{2,1,0:T(8,128)}, f32[4,520,128]{2,1,0:T(8,128)}) custom-call(s32[2]{0:T(128)S(1)} %get-tuple-element.178.info, f32[32,64,512]{2,1,0:T(8,128)} %get-tuple-element.181.refs_0_, f32[32,64,512]{2,1,0:T(8,128)} %get-tuple-element.182.refs_1_, ...), custom_call_target="tpu_custom_call" | custom-call | flops 12884901888 | bytes 25165824 | tf_op jit(solution)/shard_map/cond/branch_1_fun/cond/branch_1_fun/ffn_backward_0/pallas_call | solution.py:596
  306.6 4.2 collective-permute-done.4.recv
  310.8 1.4 copy-done.18
  312.2 16.7 %spectral_backward_0.1 = (f32[32,64,256]{2,1,0:T(8,128)}, f32[32,64,256]{2,1,0:T(8,128)}, f32[2,2,2,128,128]{4,3,2,1,0:T(8,128)}, f32[2,2,2,1,128]{4,3,2,1,0:T(1,128)}) custom-call(s32[2]{0:T(128)S(1)} %get-tuple-element.178.info, f32[32,64,256]{2,1,0:T(8,128)} %get-tuple-element.192.own.du_kept, f32[32,64,256]{2,1,0:T(8,128)} %copy-done.18, ...), custom_call_target="tpu_custom_call" | custom-call | flops 12000000000 | bytes 14680064 | tf_op jit(solution)/shard_map/cond/branch_1_fun/cond/branch_1_fun/spectral_backward_0/pallas_call | solution.py:530
  329.0 4.2 collective-permute-done.5.dh_taken
  333.2 1.4 copy-done.9
  334.6 10.0 %input_gradient.1 = (f32[16,64,512]{2,1,0:T(8,128)}, f32[16,64,512]{2,1,0:T(8,128)}, f32[8,512]{1,0:T(8,128)}) custom-call(s32[2]{0:T(128)S(1)} %get-tuple-element.178.info, f32[16,64,512]{2,1,0:T(8,128)S(1)} %get-tuple-element.179.a, f32[16,64,512]{2,1,0:T(8,128)} %get-tuple-element.180.b, f32[32,64,256]{2,1,0:T(8,128)} %get-tuple-element.192.own.du_kept, ...), custom_call_target="tpu_custom_call" | custom-call | bytes 16777216 | tf_op jit(solution)/shard_map/cond/branch_1_fun/cond/branch_1_fun/input_gradient/pallas_call | solution.py:618
  344.7 2.2 collective-permute-start.26
  346.9 94.2 %conditional.8 = (f32[800,128]{1,0:T(8,128)S(1)}, f32[800,128]{1,0:T(8,128)S(1)}) conditional(s32[]{:T(128)} %convert_element_type.12, () %tuple.59, (f32[4,520,128]{2,1,0:T(8,128)}, f32[4,520,128]{2,1,0:T(8,128)}, f32[2,2,2,128,128]{4,3,2,1,0:T(8,128)}, f32[2,2,2,1,128]{4,3,2,1,0:T(1,128)}, f32[8,512]{1,0:T(8,128)}, ...), branch_computations={%region_7.8_spmd, %region_8.9_spmd} | conditional | flops 931910 | bytes 41456776 | solution.py:719
  346.9 3.1 collective-permute-start.12
  350.7 1.8 collective-permute-done.12
  352.5 1.3 add.71
  355.7 1.2 copy-done.7
  357.0 1.6 collective-permute-start.13
  358.5 1.5 collective-permute-start.14
  360.5 8.9 %collective-permute-done.13 = f32[800,128]{1,0:T(8,128)} collective-permute-done((f32[800,128]{1,0:T(8,128)S(1)}, f32[800,128]{1,0:T(8,128)}, u32[]{:S(2)}, u32[]{:S(2)}) %collective-permute-start.13) | collective-permute-done | bytes 409632 | tf_op jit(solution)/shard_map/cond/branch_1_fun/ppermute | solution.py:745
  369.4 9.5 %collective-permute-done.14 = f32[800,128]{1,0:T(8,128)} collective-permute-done((f32[800,128]{1,0:T(8,128)S(1)}, f32[800,128]{1,0:T(8,128)}, u32[]{:S(2)}, u32[]{:S(2)}) %collective-permute-start.14) | collective-permute-done | bytes 409632 | tf_op jit(solution)/shard_map/cond/branch_1_fun/ppermute | solution.py:745
  378.9 1.4 fusion.6
  381.7 23.5 %collective-permute-done.16 = f32[400,2,128]{2,0,1:T(8,128)S(1)} collective-permute-done((f32[400,2,128]{2,0,1:T(8,128)S(1)}, f32[400,2,128]{2,0,1:T(8,128)S(1)}, u32[]{:S(2)}, u32[]{:S(2)}) %collective-permute-start.16) | collective-permute-done | bytes 409632 | tf_op jit(solution)/shard_map/cond/branch_1_fun/ppermute | solution.py:745
  406.6 11.6 %collective-permute-done.17 = f32[200,2,128]{2,0,1:T(8,128)S(1)} collective-permute-done((f32[200,2,128]{2,0,1:T(8,128)S(1)}, f32[200,2,128]{2,0,1:T(8,128)S(1)}, u32[]{:S(2)}, u32[]{:S(2)}) %collective-permute-start.17) | collective-permute-done | bytes 204832 | tf_op jit(solution)/shard_map/cond/branch_1_fun/ppermute | solution.py:745
  418.3 11.2 %collective-permute-done.18 = f32[200,2,128]{2,0,1:T(8,128)S(1)} collective-permute-done((f32[200,2,128]{2,0,1:T(8,128)S(1)}, f32[200,2,128]{2,0,1:T(8,128)S(1)}, u32[]{:S(2)}, u32[]{:S(2)}) %collective-permute-start.18) | collective-permute-done | bytes 204832 | tf_op jit(solution)/shard_map/cond/branch_1_fun/ppermute | solution.py:753
  429.8 11.3 %collective-permute-done.19 = f32[400,2,128]{2,0,1:T(8,128)S(1)} collective-permute-done((f32[400,2,128]{2,0,1:T(8,128)S(1)}, f32[400,2,128]{2,0,1:T(8,128)S(1)}, u32[]{:S(2)}, u32[]{:S(2)}) %collective-permute-start.19) | collective-permute-done | bytes 409632 | tf_op jit(solution)/shard_map/cond/branch_1_fun/ppermute | solution.py:753
  441.2 1.3 copy-done.2
  442.8 43.3 %conditional.9 = (f32[2,16,64,512]{3,2,1,0:T(8,128)}, f32[3200,128]{1,0:T(8,128)}, f32[3200,128]{1,0:T(8,128)}, f32[6400,128]{1,0:T(8,128)}) conditional(s32[]{:T(128)} %convert_element_type.12, () %tuple.56, (s32[2]{0:T(128)S(1)}, f32[16,64,512]{2,1,0:T(8,128)}, f32[16,64,512]{2,1,0:T(8,128)}, f32[800,128]{1,0:T(8,128)S(1)}, ...), branch_computations={%region_9.10_spmd, %region_10.13_spmd} | conditional | flops 35 | bytes 29082308 | solution.py:719
  443.6 34.9 %conditional.1 = (f32[2,16,64,512]{3,2,1,0:T(8,128)}, f32[3200,128]{1,0:T(8,128)}, f32[3200,128]{1,0:T(8,128)}) conditional(s32[]{:T(128)} %convert_element_type.1, () %tuple.43, (s32[2]{0:T(128)S(1)}, f32[16,64,512]{2,1,0:T(8,128)}, f32[16,64,512]{2,1,0:T(8,128)}, f32[800,128]{1,0:T(8,128)S(1)}) %tuple.44), branch_computations={%region_11.11_spmd, %region_12.12_spmd} | conditional | flops 30 | bytes 16384529 | solution.py:719
  443.6 1.6 collective-permute-start.8
  445.2 1.5 collective-permute-start.9
  447.1 1.3 broadcast.90
  449.2 5.8 %collective-permute-done.8 = f32[800,128]{1,0:T(8,128)} collective-permute-done((f32[800,128]{1,0:T(8,128)S(1)}, f32[800,128]{1,0:T(8,128)}, u32[]{:S(2)}, u32[]{:S(2)}) %collective-permute-start.8) | collective-permute-done | bytes 409632 | tf_op jit(solution)/shard_map/cond/branch_1_fun/cond/branch_1_fun/ppermute | solution.py:753
  455.0 1.8 bitcast_dynamic-update-slice_fusion.6
  456.8 2.3 collective-permute-done.9
  459.9 9.3 %collective-permute-done.10 = f32[800,128]{1,0:T(8,128)S(1)} collective-permute-done((f32[800,128]{1,0:T(8,128)S(1)}, f32[800,128]{1,0:T(8,128)S(1)}, u32[]{:S(2)}, u32[]{:S(2)}) %collective-permute-start.10) | collective-permute-done | bytes 409632 | tf_op jit(solution)/shard_map/cond/branch_1_fun/cond/branch_1_fun/ppermute | solution.py:753
  470.8 7.7 %join.2 = f32[2,16,64,512]{3,2,1,0:T(8,128)} custom-call(s32[2]{0:T(128)S(1)} %get-tuple-element.253.info, f32[16,64,512]{2,1,0:T(8,128)} %get-tuple-element.254.first, f32[16,64,512]{2,1,0:T(8,128)} %get-tuple-element.255.second), custom_call_target="tpu_custom_call" | custom-call | tf_op jit(solution)/shard_map/cond/branch_1_fun/cond/branch_1_fun/join/pallas_call | solution.py:701
  478.5 7.5 %all-gather.2.cloned.1.call-done = f32[6400,128]{1,0:T(8,128)} async-done(((f32[800,128]{1,0:T(8,128)}), f32[6400,128]{1,0:T(8,128)}) %all-gather.2.cloned.1.call-update) | async-done | bytes 3276816 | tf_op jit(solution)/shard_map/cond/branch_1_fun/all_gather | solution.py:917
  486.0 6.7 %unpack.1 = (f32[2,2,512]{2,1,0:T(2,128)}, f32[2,2,512]{2,1,0:T(2,128)}, f32[2,2,2,4,128,128]{5,4,3,2,1,0:T(8,128)}, f32[2,2,2,4,128]{4,3,2,1,0:T(4,128)}, f32[2...) custom-call(s32[2]{0:T(128)S(1)} %pad_add_fusion.info, ...), custom_call_target="tpu_custom_call" | custom-call | tf_op jit(solution)/shard_map/unpack/pallas_call | solution.py:830
  493.5 4.2 join.3
  (104 shorter events, 19.3 us)
Async XLA Ops:
  7.3 2.2 copy-start
  10.2 4.8 copy-start.1
  10.2 8.2 %collective-permute-start.20 = (f32[16,64,512]{2,1,0:T(8,128)S(1)}, f32[16,64,512]{2,1,0:T(8,128)S(1)}, u32[]{:S(2)}, u32[]{:S(2)}) collective-permute-start(f32[16,64,512]{2,1,0:T(8,128)S(1)} %pick.4), channel_id=1, source_target_pairs={{0,0},{1,1},{2,4},{3,5},{4,2},{5,3},{6,6},{7,7},{8,8},{9,9},{10,12... | collective-permute-start | bytes 6291464 | tf_op jit(solution)/shard_map/ppermute | solution.py:681
  11.9 49.2 %collective-permute-start.21 = (f32[16,64,512]{2,1,0:T(8,128)S(1)}, f32[16,64,512]{2,1,0:T(8,128)}, u32[]{:S(2)}, u32[]{:S(2)}) collective-permute-start(f32[16,64,512]{2,1,0:T(8,128)S(1)} %pick.5), channel_id=1, source_target_pairs={{0,1},{1,0},{2,5},{3,4},{4,3},{5,2},{6,7},{7,6},{8,9},{9,8},{10,13... | collective-permute-start | bytes 6291464 | tf_op jit(solution)/shard_map/ppermute | solution.py:681
  15.8 1.3 copy-start.4
  17.1 1.3 copy-start.5
  18.4 61.5 %copy-start.11 = (f32[2,2,512]{2,1,0:T(2,128)S(1)}, f32[2,2,512]{2,1,0:T(2,128)}, u32[]{:S(2)}) copy-start(f32[2,2,512]{2,1,0:T(2,128)} %param.27) | copy-start | bytes 24580
  18.4 61.5 %copy-start.12 = (f32[2,2,512]{2,1,0:T(2,128)S(1)}, f32[2,2,512]{2,1,0:T(2,128)}, u32[]{:S(2)}) copy-start(f32[2,2,512]{2,1,0:T(2,128)} %param.28) | copy-start | bytes 24580
  18.4 61.5 %copy-start.19 = (f32[2,2,2,4,128]{4,3,2,1,0:T(4,128)S(1)}, f32[2,2,2,4,128]{4,3,2,1,0:T(4,128)}, u32[]{:S(2)}) copy-start(f32[2,2,2,4,128]{4,3,2,1,0:T(4,128)} %param.30) | copy-start | bytes 49156
  18.4 61.5 %copy-start.20 = (f32[2,512]{1,0:T(2,128)S(1)}, f32[2,512]{1,0:T(2,128)}, u32[]{:S(2)}) copy-start(f32[2,512]{1,0:T(2,128)} %param.32) | copy-start | bytes 12292
  18.4 61.5 %copy-start.21 = (f32[2,512]{1,0:T(2,128)S(1)}, f32[2,512]{1,0:T(2,128)}, u32[]{:S(2)}) copy-start(f32[2,512]{1,0:T(2,128)} %param.34) | copy-start | bytes 12292
  61.1 140.6 %collective-permute-start.22 = (f32[16,64,512]{2,1,0:T(8,128)}, f32[16,64,512]{2,1,0:T(8,128)}, u32[]{:S(2)}, u32[]{:S(2)}) collective-permute-start(f32[16,64,512]{2,1,0:T(8,128)} %get-tuple-element.316), channel_id=1, source_target_pairs={{0,0},{1,1},{2,4},{3,5},{4,2},{5,3},{6,6},{7,7},{8,8},{9,9},{10,12... | collective-permute-start | bytes 6291464 | tf_op jit(solution)/shard_map/ppermute | solution.py:681
  78.2 123.5 %collective-permute-start.23 = (f32[16,64,512]{2,1,0:T(8,128)}, f32[16,64,512]{2,1,0:T(8,128)}, u32[]{:S(2)}, u32[]{:S(2)}) collective-permute-start(f32[16,64,512]{2,1,0:T(8,128)} %get-tuple-element.317), channel_id=1, source_target_pairs={{0,1},{1,0},{2,5},{3,4},{4,3},{5,2},{6,7},{7,6},{8,9},{9,8},{10,13... | collective-permute-start | bytes 6291464 | tf_op jit(solution)/shard_map/ppermute | solution.py:681
  80.0 45.5 %copy-start.13 = (f32[2,2,2,4,128,128]{5,4,3,2,1,0:T(8,128)S(1)}, f32[2,2,2,4,128,128]{5,4,3,2,1,0:T(8,128)}, u32[]{:S(2)}) copy-start(f32[2,2,2,4,128,128]{5,4,3,2,1,0:T(8,128)} %get-tuple-element.151.weight) | copy-start | bytes 6291460 | tf_op jit(solution)/shard_map/cond
  87.4 36.8 %collective-permute-start = (f32[32,64,256]{2,1,0:T(8,128)}, f32[32,64,256]{2,1,0:T(8,128)S(1)}, u32[]{:S(2)}, u32[]{:S(2)}) collective-permute-start(f32[32,64,256]{2,1,0:T(8,128)} %get-tuple-element.150), channel_id=1, source_target_pairs={{0,4},{4,0},{8,12},{12,8},{16,20},{20,16},{24,28},{28,24},{1,5},{5... | collective-permute-start | bytes 6291464 | tf_op jit(solution)/shard_map/cond/branch_1_fun/ppermute | solution.py:723
  124.2 1.3 copy-start.16
  125.5 19.4 %copy-start.15 = (f32[2,512,512]{2,1,0:T(8,128)S(1)}, f32[2,512,512]{2,1,0:T(8,128)}, u32[]{:S(2)}) copy-start(f32[2,512,512]{2,1,0:T(8,128)} %get-tuple-element.157.refs_6_.refs_5_) | copy-start | bytes 6291460 | tf_op jit(solution)/shard_map/cond
  140.4 4.5 collective-permute-start.1
  160.7 4.5 collective-permute-start.2
  180.0 4.4 collective-permute-start.3
  184.3 1.3 copy-start.17
  201.7 142.9 %collective-permute-start.24 = (f32[16,64,512]{2,1,0:T(8,128)}, f32[16,64,512]{2,1,0:T(8,128)}, u32[]{:S(2)}, u32[]{:S(2)}) collective-permute-start(f32[16,64,512]{2,1,0:T(8,128)} %get-tuple-element.318), channel_id=1, source_target_pairs={{0,0},{1,1},{4,2},{5,3},{2,4},{3,5},{6,6},{7,7},{8,8},{9,9},{12,10... | collective-permute-start | bytes 6291464 | tf_op jit(solution)/shard_map/ppermute | solution.py:681
  218.8 125.8 %collective-permute-start.25 = (f32[16,64,512]{2,1,0:T(8,128)}, f32[16,64,512]{2,1,0:T(8,128)}, u32[]{:S(2)}, u32[]{:S(2)}) collective-permute-start(f32[16,64,512]{2,1,0:T(8,128)} %get-tuple-element.319), channel_id=1, source_target_pairs={{1,0},{0,1},{5,2},{4,3},{3,4},{2,5},{7,6},{6,7},{9,8},{8,9},{13,10... | collective-permute-start | bytes 6291464 | tf_op jit(solution)/shard_map/ppermute | solution.py:681
  219.2 125.5 %reduce-scatter.2.cloned.1.call-start = ((), (), s32[]{:S(2)}) async-start(), calls=%async_computation.1 | async-start | bytes 3686400 | tf_op jit(solution)/shard_map/cond/branch_1_fun/reduce_scatter | solution.py:889
  219.2 28.9 %copy-start.22 = (bf16[64,256]{1,0:T(8,128)(2,1)S(1)}, bf16[64,256]{1,0:T(8,128)(2,1)}, u32[]{:S(2)}) copy-start(bf16[64,256]{1,0:T(8,128)(2,1)} %constant.198.clone.1.table_in) | copy-start | bytes 98308 | tf_op jit(solution)/shard_map/cond
  219.2 28.9 %copy-start.23 = (bf16[64,256]{1,0:T(8,128)(2,1)S(1)}, bf16[64,256]{1,0:T(8,128)(2,1)}, u32[]{:S(2)}) copy-start(bf16[64,256]{1,0:T(8,128)(2,1)} %constant.199.clone.1.table_out) | copy-start | bytes 98308 | tf_op jit(solution)/shard_map/cond
  243.5 4.6 collective-permute-start.6
  248.0 18.5 %copy-start.8 = (f32[2,4,520,128]{3,2,1,0:T(8,128)S(1)}, f32[2,4,520,128]{3,2,1,0:T(8,128)}, u32[]{:S(2)}) copy-start(f32[2,4,520,128]{3,2,1,0:T(8,128)} %get-tuple-element.243) | copy-start | bytes 6389764 | tf_op jit(solution)/shard_map/cond
  273.5 4.6 collective-permute-start.7
  278.1 34.1 %copy-start.14 = (f32[2,2,2,4,128,128]{5,4,3,2,1,0:T(8,128)S(1)}, f32[2,2,2,4,128,128]{5,4,3,2,1,0:T(8,128)}, u32[]{:S(2)}) copy-start(f32[2,2,2,4,128,128]{5,4,3,2,1,0:T(8,128)} %get-tuple-element.194.weight) | copy-start | bytes 6291460 | tf_op jit(solution)/shard_map/cond/branch_1_fun/cond
  306.4 4.4 collective-permute-start.4
  310.8 1.4 copy-start.18
  328.9 4.4 collective-permute-start.5
  333.2 1.4 copy-start.9
  344.7 96.5 %collective-permute-start.26 = (f32[16,64,512]{2,1,0:T(8,128)}, f32[16,64,512]{2,1,0:T(8,128)S(1)}, u32[]{:S(2)}, u32[]{:S(2)}) collective-permute-start(f32[16,64,512]{2,1,0:T(8,128)} %passed.6), channel_id=1, source_target_pairs={{0,0},{1,1},{4,2},{5,3},{2,4},{3,5},{6,6},{7,7},{8,8},{9,9},{12,10... | collective-permute-start | bytes 6291464 | tf_op jit(solution)/shard_map/ppermute | solution.py:681
  346.9 5.6 %collective-permute-start.12 = (f32[4,520,128]{2,1,0:T(8,128)}, f32[4,520,128]{2,1,0:T(8,128)S(1)}, u32[]{:S(2)}, u32[]{:S(2)}) collective-permute-start(f32[4,520,128]{2,1,0:T(8,128)} %get-tuple-element.248), channel_id=1, source_target_pairs={{0,4},{4,0},{8,12},{12,8},{16,20},{20,16},{24,28},{28,24},{1,5},{5... | collective-permute-start | bytes 3194888 | tf_op jit(solution)/shard_map/cond/branch_1_fun/ppermute | solution.py:723
  355.7 1.2 copy-start.7
  357.0 12.5 %collective-permute-start.13 = (f32[800,128]{1,0:T(8,128)S(1)}, f32[800,128]{1,0:T(8,128)}, u32[]{:S(2)}, u32[]{:S(2)}) collective-permute-start(f32[800,128]{1,0:T(8,128)S(1)} %get-tuple-element.381), channel_id=1, source_target_pairs={{0,8},{4,12},{8,0},{12,4},{16,24},{20,28},{24,16},{28,20},{1,9},{5... | collective-permute-start | bytes 1228808 | tf_op jit(solution)/shard_map/cond/branch_1_fun/ppermute | solution.py:745
  358.5 20.3 %collective-permute-start.14 = (f32[800,128]{1,0:T(8,128)S(1)}, f32[800,128]{1,0:T(8,128)}, u32[]{:S(2)}, u32[]{:S(2)}) collective-permute-start(f32[800,128]{1,0:T(8,128)S(1)} %get-tuple-element.383), channel_id=1, source_target_pairs={{0,16},{4,20},{8,24},{12,28},{16,0},{20,4},{24,8},{28,12},{1,17},{... | collective-permute-start | bytes 1228808 | tf_op jit(solution)/shard_map/cond/branch_1_fun/ppermute | solution.py:745
  360.1 18.8 %collective-permute-start.15 = (f32[800,128]{1,0:T(8,128)S(1)}, f32[800,128]{1,0:T(8,128)}, u32[]{:S(2)}, u32[]{:S(2)}) collective-permute-start(f32[800,128]{1,0:T(8,128)S(1)} %get-tuple-element.382), channel_id=1, source_target_pairs={{0,24},{4,28},{8,16},{12,20},{16,8},{20,12},{24,0},{28,4},{1,25},{... | collective-permute-start | bytes 1228808 | tf_op jit(solution)/shard_map/cond/branch_1_fun/ppermute | solution.py:745
  381.3 24.0 %collective-permute-start.16 = (f32[400,2,128]{2,0,1:T(8,128)S(1)}, f32[400,2,128]{2,0,1:T(8,128)S(1)}, u32[]{:S(2)}, u32[]{:S(2)}) collective-permute-start(f32[400,2,128]{2,0,1:T(8,128)S(1)} %fusion.1), channel_id=1, source_target_pairs={{0,1},{1,0},{2,3},{3,2},{4,5},{5,4},{6,7},{7,6},{8,9},{9,8},{10,11... | collective-permute-start | bytes 1228808 | tf_op jit(solution)/shard_map/cond/branch_1_fun/ppermute | solution.py:745
  406.3 11.9 %collective-permute-start.17 = (f32[200,2,128]{2,0,1:T(8,128)S(1)}, f32[200,2,128]{2,0,1:T(8,128)S(1)}, u32[]{:S(2)}, u32[]{:S(2)}) collective-permute-start(f32[200,2,128]{2,0,1:T(8,128)S(1)} %dynamic-slice_bitcast_fusion.3), channel_id=1, source_target_pairs={{0,2},{1,3},{2,0},{3,1},{4,6},{5,7},{6,4},{7,5},{8,10},{9,11},{10,... | collective-permute-start | bytes 614408 | tf_op jit(solution)/shard_map/cond/branch_1_fun/ppermute | solution.py:745
  418.2 11.4 %collective-permute-start.18 = (f32[200,2,128]{2,0,1:T(8,128)S(1)}, f32[200,2,128]{2,0,1:T(8,128)S(1)}, u32[]{:S(2)}, u32[]{:S(2)}) collective-permute-start(f32[200,2,128]{2,0,1:T(8,128)S(1)} %get-tuple-element.380), channel_id=1, source_target_pairs={{0,2},{1,3},{2,0},{3,1},{4,6},{5,7},{6,4},{7,5},{8,10},{9,11},{10,... | collective-permute-start | bytes 614408 | tf_op jit(solution)/shard_map/cond/branch_1_fun/ppermute | solution.py:753
  429.6 11.5 %collective-permute-start.19 = (f32[400,2,128]{2,0,1:T(8,128)S(1)}, f32[400,2,128]{2,0,1:T(8,128)S(1)}, u32[]{:S(2)}, u32[]{:S(2)}) collective-permute-start(f32[400,2,128]{2,0,1:T(8,128)S(1)} %bitcast.73), channel_id=1, source_target_pairs={{0,1},{1,0},{2,3},{3,2},{4,5},{5,4},{6,7},{7,6},{8,9},{9,8},{10,11... | collective-permute-start | bytes 1228808 | tf_op jit(solution)/shard_map/cond/branch_1_fun/ppermute | solution.py:753
  441.2 1.3 copy-start.2
  442.5 50.2 %collective-permute-start.27 = (f32[16,64,512]{2,1,0:T(8,128)}, f32[16,64,512]{2,1,0:T(8,128)S(1)}, u32[]{:S(2)}, u32[]{:S(2)}) collective-permute-start(f32[16,64,512]{2,1,0:T(8,128)} %passed.7), channel_id=1, source_target_pairs={{1,0},{0,1},{5,2},{4,3},{3,4},{2,5},{7,6},{6,7},{9,8},{8,9},{13,10... | collective-permute-start | bytes 6291464 | tf_op jit(solution)/shard_map/ppermute | solution.py:681
  442.8 0.8 copy-start.10
  442.8 43.3 %all-gather.2.cloned.1.call-start = ((), (), s32[]{:S(2)}) async-start(), calls=%async_computation.2 | async-start | bytes 3686400 | tf_op jit(solution)/shard_map/cond/branch_1_fun/all_gather | solution.py:917
  443.6 11.5 %collective-permute-start.8 = (f32[800,128]{1,0:T(8,128)S(1)}, f32[800,128]{1,0:T(8,128)}, u32[]{:S(2)}, u32[]{:S(2)}) collective-permute-start(f32[800,128]{1,0:T(8,128)S(1)} %get-tuple-element.256), channel_id=1, source_target_pairs={{0,8},{4,12},{8,0},{12,4},{16,24},{20,28},{24,16},{28,20},{1,9},{5... | collective-permute-start | bytes 1228808 | tf_op jit(solution)/shard_map/cond/branch_1_fun/cond/branch_1_fun/ppermute | solution.py:753
  445.2 13.9 %collective-permute-start.9 = (f32[800,128]{1,0:T(8,128)S(1)}, f32[800,128]{1,0:T(8,128)S(1)}, u32[]{:S(2)}, u32[]{:S(2)}) collective-permute-start(f32[800,128]{1,0:T(8,128)S(1)} %get-tuple-element.256), channel_id=1, source_target_pairs={{0,16},{4,20},{8,24},{12,28},{16,0},{20,4},{24,8},{28,12},{1,17},{... | collective-permute-start | bytes 1228808 | tf_op jit(solution)/shard_map/cond/branch_1_fun/cond/branch_1_fun/ppermute | solution.py:753
  446.7 22.5 %collective-permute-start.10 = (f32[800,128]{1,0:T(8,128)S(1)}, f32[800,128]{1,0:T(8,128)S(1)}, u32[]{:S(2)}, u32[]{:S(2)}) collective-permute-start(f32[800,128]{1,0:T(8,128)S(1)} %get-tuple-element.256), channel_id=1, source_target_pairs={{0,24},{4,28},{8,16},{12,20},{16,8},{20,12},{24,0},{28,4},{1,25},{... | collective-permute-start | bytes 1228808 | tf_op jit(solution)/shard_map/cond/branch_1_fun/cond/branch_1_fun/ppermute | solution.py:753
  469.9 8.6 %collective-permute-start.11 = (f32[3200,128]{1,0:T(8,128)}, f32[3200,128]{1,0:T(8,128)}, u32[]{:S(2)}, u32[]{:S(2)}) collective-permute-start(f32[3200,128]{1,0:T(8,128)} %bitcast.34), channel_id=1, source_target_pairs={{0,4},{4,0},{8,12},{12,8},{16,20},{20,16},{24,28},{28,24},{1,5},{5... | collective-permute-start | bytes 4915208 | tf_op jit(solution)/shard_map/cond/branch_1_fun/cond/branch_1_fun/ppermute | solution.py:723
  486.0 6.7 %copy-start.3 = (f32[16,64,512]{2,1,0:T(8,128)S(1)}, f32[16,64,512]{2,1,0:T(8,128)}, u32[]{:S(2)}) copy-start(f32[16,64,512]{2,1,0:T(8,128)} %copy-done.2) | copy-start | bytes 6291460
  492.8 0.7 copy-start.6
Sparse Core Ops, SparseCore 0:
  273.6 47.8 reduce-scatter.1
  446.1 39.9 all-gather.1

commit v3 on v2

--- a/solution.py
+++ b/solution.py
@@ -14,7 +14,8 @@
 MODES = 32
 EPSILON = 1e-05
 THRESHOLD = 0.05
-ROWS = 4
+ROWS = 8
+SMALL_ROWS = 32
 F32 = jnp.float32
 BF16 = jnp.bfloat16
 BOTH = ("wide", "section")
@@ -180,10 +181,12 @@
     return ref[...].reshape(-1, ref.shape[-1])
 
 
-def picked(step, steps, refs):
+def picked(info, step, steps, refs):
     if len(refs) == 1:
         return flat(refs[0])
-    return jnp.where(step < steps // 2, flat(refs[0]), flat(refs[1]))
+    own, first, second = refs
+    first = jnp.where(info[2] == 1, flat(own), flat(first))
+    return jnp.where(step < steps // 2, first, flat(second))
 
 
 def put_pieces(step, steps, refs, values):
@@ -300,8 +303,12 @@
 
 
 def spectral_backward_kernel(
-    info, own, recv, weight, modes, before, after, table_in, table_out, keep, send, weight_grad, offset_grad, planes, flowing, stacked, summed
+    start, info, own, recv, weight, modes, before, after, table_in, table_out, *refs
 ):
+    if start is None:
+        keep, send, weight_grad, offset_grad, planes, flowing, stacked, summed = refs
+    else:
+        _, keep, send, out, planes, flowing, stacked, summed, weight_grad, offset_grad, blank, sems = refs
     core = info[0]
     sign = jnp.where(core == 1, -1.0, 1.0).astype(F32)
     place_weights(weight, stacked)
@@ -322,16 +329,33 @@
     empty = jnp.zeros((1, flowing.shape[1]), F32)
     totals = lax.fori_loop(0, MODES * MODES // MIX_ROWS, mix, (empty, empty))
     lanes = flowing.shape[1] // 2
+    offset_grad[...] = jnp.zeros_like(offset_grad)
     for j in range(2):
-        offset_grad[j, 0] = totals[j][:, :lanes]
-        offset_grad[j, 1] = totals[j][:, lanes:]
+        offset_grad[2 * j : 2 * j + 1] = totals[j][:, :lanes]
+        offset_grad[2 * j + 1 : 2 * j + 2] = totals[j][:, lanes:]
         weight_grad[j, 0] = summed[j, :lanes, :lanes] + summed[j, lanes:, lanes:]
         weight_grad[j, 1] = summed[j, :lanes, lanes:] - summed[j, lanes:, :lanes]
+    if start is not None:
+        block, other = 2 * core + pl.program_id(0), 2 * (1 - core) + pl.program_id(0)
+        blank[...] = jnp.zeros_like(blank)
+        copies = []
+        for index in range(4):
+            for source, place in ((weight_grad.at[index // 2, index % 2], block), (blank, other)):
+                at = pl.ds(pl.multiple_of(start + (index * BLOCKS + place) * 128, 8), 128)
+                copies.append(pltpu.make_async_copy(source, out.at[at], sems.at[len(copies)]))
+        for source, place in ((offset_grad, block), (blank.at[pl.ds(0, 8)], other)):
+            at = pl.ds(pl.multiple_of(start + 4 * BLOCKS * 128 + place * 8, 8), 8)
+            copies.append(pltpu.make_async_copy(source, out.at[at], sems.at[len(copies)]))
+        for copy in copies:
+            copy.start()
     synthesise(flowing, table_out, sign, planes, keep, send)
-
-
-def first_norm_kernel(steps, info, a, b, gains, biases, keep, send):
-    unit, _ = normalise(picked(pl.program_id(0), steps, (a, b)))
+    if start is not None:
+        for copy in copies:
+            copy.wait()
+
+
+def first_norm_kernel(steps, info, own, a, b, gains, biases, keep, send):
+    unit, _ = normalise(picked(info, pl.program_id(0), steps, (own, a, b)))
     parted(info[0], unit * gains[0:1] + biases[0:1], keep, send)
 
 
@@ -342,7 +366,7 @@
     kept, taken, gains, biases, up, up_offset, down, down_offset = refs[:8]
     refs = refs[8:]
     core = info[0]
-    mixed = picked(step, steps, x_refs) + joined(core, kept, taken)
+    mixed = picked(info, step, steps, x_refs) + joined(core, kept, taken)
     unit, _ = normalise(mixed)
     normed = unit * gains[1:2] + biases[1:2]
     before = exact_dot(normed, up[...], 1, 0) + up_offset[layer : layer + 1]
@@ -370,7 +394,7 @@
     return [values[:, at : at + 128] for at in range(0, values.shape[1], 128)]
 
 
-def ffn_backward_kernel(steps, fused, by_member, info, *refs):
+def ffn_backward_kernel(steps, fused, info, *refs):
     step = pl.program_id(0)
     core = info[0]
     refs = list(refs)
@@ -380,10 +404,12 @@
         grad, late_gain, late_bias = first_norm_backward(core, flat(x), du_kept, du_sent, dh_kept, dh_taken, next_gains)
         refs = refs[12:]
     else:
-        grad = picked(step, steps, refs[6:8])
-        refs = refs[8:]
+        grad = picked(info, step, steps, refs[6:9])
+        refs = refs[9:]
     keep, send, *packed, up_grad, down_grad, small = refs
-    kept_grads, sent_grads = packed if by_member else (packed[0].at[0], packed[0].at[1])
+    if not fused:
+        out, lined, sem, up_grad, down_grad, small = packed + [up_grad, down_grad, small]
+    kept_grads, sent_grads = packed if fused else (lined.at[0], lined.at[1])
 
     @pl.when(step == 0)
     def _():
@@ -412,15 +438,21 @@
         width = up_grad.shape[0]
         parts = zip(lanes_first(up_grad[...]), lanes_first(down_grad[...]), lanes_first(small[...]))
         for index, (a, b, c) in enumerate(parts):
-            kept_grads[index, :width] = jnp.where(core == 0, a, b) if by_member else a
-            sent_grads[index, :width] = jnp.where(core == 0, b, a) if by_member else b
-            kept_grads[index, width:] = c
-            sent_grads[index, width:] = c
-
-
-def input_grad_kernel(steps, info, a, b, du_kept, du_sent, dh_kept, dh_taken, gains, first_out, second_out, small):
+            kept_grads[index, :width] = jnp.where(core == 0, a, b) if fused else a
+            sent_grads[index, :width] = jnp.where(core == 0, b, a) if fused else b
+            for grads in (kept_grads, sent_grads):
+                grads[index, width : width + 8] = c
+                grads[index, width + 8 :] = jnp.zeros((SMALL_ROWS - 8, 128), F32)
+        if not fused:
+            lines = out.at[pl.ds(0, lined.size // 128)].reshape(lined.shape)
+            copy = pltpu.make_async_copy(lined, lines, sem)
+            copy.start()
+            copy.wait()
+
+
+def input_grad_kernel(steps, info, own, a, b, du_kept, du_sent, dh_kept, dh_taken, gains, first_out, second_out, small):
     step = pl.program_id(0)
-    x = picked(step, steps, (a, b))
+    x = picked(info, step, steps, (own, a, b))
     result, gain_sum, bias_sum = first_norm_backward(info[0], x, du_kept, du_sent, dh_kept, dh_taken, gains)
 
     @pl.when(step == 0)
@@ -432,7 +464,7 @@
     put_pieces(step, steps, (first_out, second_out), result)
 
 
-def call(kernel, grid, in_specs, out_specs, out_shapes, scratch, flops, moved, name, vmem=56):
+def call(kernel, grid, in_specs, out_specs, out_shapes, scratch, flops, moved, name, vmem=56, aliases=None):
     return pl.pallas_call(
         kernel,
         grid_spec=pltpu.PrefetchScalarGridSpec(
@@ -443,6 +475,7 @@
             scratch_shapes=scratch,
         ),
         out_shape=out_shapes,
+        input_output_aliases=aliases or {},
         compiler_params=pltpu.CompilerParams(vmem_limit_bytes=vmem * 2**20),
         cost_estimate=pl.CostEstimate(flops=int(flops), bytes_accessed=int(moved), transcendentals=0),
         name=name,
@@ -466,6 +499,11 @@
         self.wide_row = pl.BlockSpec((ROWS, GRID, hidden), local)
         self.half_row = pl.BlockSpec((ROWS, GRID, half), canonical)
         self.first = pl.BlockSpec((ROWS, GRID, width), lambda j, s: (jnp.minimum(j, per_piece - 1), 0, 0))
+        self.pieces = [
+            pl.BlockSpec((None, ROWS, GRID, width), lambda j, s: (s[1], jnp.minimum(j, per_piece - 1) * s[2], 0, 0)),
+            pl.BlockSpec((ROWS, GRID, width), lambda j, s: (jnp.minimum(j, per_piece - 1) * (1 - s[2]), 0, 0)),
+            pl.BlockSpec((ROWS, GRID, width), lambda j, s: (jnp.maximum(j - per_piece, 0), 0, 0)),
+        ]
         self.second = pl.BlockSpec((ROWS, GRID, width), lambda j, s: (jnp.maximum(j - per_piece, 0), 0, 0))
         self.half_shape = jax.ShapeDtypeStruct((2 * quarter, GRID, half), F32)
         self.row_shape = jax.ShapeDtypeStruct((2 * quarter, GRID, width), F32)
@@ -482,18 +520,18 @@
         return pl.BlockSpec(shape, lambda j, s: (0,) * len(shape))
 
 
-def first_norm(plan, info, a, b, gains, biases):
+def first_norm(plan, info, pieces, gains, biases):
     return call(
         functools.partial(first_norm_kernel, plan.steps),
         plan.steps,
-        [plan.first, plan.second, plan.norm(0), plan.norm(0)],
+        [*plan.pieces, plan.norm(0), plan.norm(0)],
         [plan.half_row, plan.half_row],
         [plan.half_shape, plan.half_shape],
         [],
         0,
         4 * 2**20 * 2,
         "first_norm",
-    )(info, a, b, gains, biases)
+    )(info, *pieces, gains, biases)
 
 
 def spectral_specs(layer, width):
@@ -525,34 +563,48 @@
     )(info, own, recv, weight_all, offset_all, tables[0], tables[3])
 
 
-def spectral_backward(plan, layer, info, own, recv, weight_all, saved, tables):
+def spectral_backward(plan, layer, info, own, recv, weight_all, saved, tables, packed=None, start=None):
     block, cells, weight, offset, table, modes, modes_shape, planes, flowing, stacked = spectral_specs(layer, plan.width)
+    specs = [cells, cells, weight, modes, modes, modes, table, table]
+    out_specs, out_shapes = [cells, cells], [plan.half_shape, plan.half_shape]
+    scratch = [planes, flowing, stacked, pltpu.VMEM((2, 2 * block, 2 * block), F32)]
+    args = [info, own, recv, weight_all, *saved, tables[1], tables[2]]
+    aliases = {}
+    if start is None:
+        out_specs += [
+            pl.BlockSpec((2, 2, None, block, block), lambda b, s: (0, 0, b, 0, 0)),
+            pl.BlockSpec((None, 8, block), lambda b, s: (b, 0, 0)),
+        ]
+        out_shapes += [
+            jax.ShapeDtypeStruct((2, 2, 2, block, block), F32),
+            jax.ShapeDtypeStruct((2, 8, block), F32),
+        ]
+    else:
+        specs.append(pl.BlockSpec(memory_space=pl.ANY))
+        out_specs.append(pl.BlockSpec(memory_space=pl.ANY))
+        out_shapes.append(jax.ShapeDtypeStruct(packed.shape, F32))
+        aliases = {len(args): 2}
+        args.append(packed)
+        scratch += [pltpu.VMEM((2, 2, block, block), F32), pltpu.VMEM((8, block), F32), pltpu.VMEM((block, block), F32)]
+        scratch += [pltpu.SemaphoreType.DMA((10,))]
     return call(
-        spectral_backward_kernel,
+        functools.partial(spectral_backward_kernel, start),
         2,
-        [cells, cells, weight, modes, modes, modes, table, table],
-        [
-            cells,
-            cells,
-            pl.BlockSpec((2, 2, None, block, block), lambda b, s: (0, 0, b, 0, 0)),
-            pl.BlockSpec((2, 2, None, 1, block), lambda b, s: (0, 0, b, 0, 0)),
-        ],
-        [
-            plan.half_shape,
-            plan.half_shape,
-            jax.ShapeDtypeStruct((2, 2, 2, block, block), F32),
-            jax.ShapeDtypeStruct((2, 2, 2, 1, block), F32),
-        ],
-        [planes, flowing, stacked, pltpu.VMEM((2, 2 * block, 2 * block), F32)],
-        3 * 4e9,
-        14 * 2**20,
+        specs,
+        out_specs,
+        out_shapes,
+        scratch,
+        0,
+        0,
         f"spectral_backward_{layer}",
-    )(info, own, recv, weight_all, *saved, tables[1], tables[2])
+        56,
+        aliases,
+    )(*args)
 
 
 def ffn_forward(plan, layer, more, info, x, kept, taken, gains, biases, up, up_offset, down, down_offset):
     width, hidden = plan.width, plan.hidden
-    specs = [plan.first, plan.second] if len(x) == 2 else [plan.row]
+    specs = list(plan.pieces) if len(x) == 3 else [plan.row]
     specs += [plan.half_row, plan.half_row, plan.norm(layer), plan.norm(layer)]
     specs += [plan.matrix(layer, width, hidden), plan.whole(up_offset.shape)]
     specs += [plan.matrix(layer, hidden, width), plan.whole(down_offset.shape)]
@@ -580,11 +632,16 @@
     )(info, *args)
 
 
-def ffn_backward(plan, layer, info, mixed, before, gains, biases, up, down, grads):
+def ffn_backward(plan, layer, info, mixed, before, gains, biases, up, down, grads, rows=None):
     width, hidden = plan.width, plan.hidden
     fused = len(grads) == 5
-    packed = (width // 128, hidden + 8, 128)
-    packed = [packed, packed] if layer == 0 else [(2, *packed)]
+    lined = (width // 128, hidden + SMALL_ROWS, 128)
+    scratch = [pltpu.VMEM(shape, F32) for shape in ((width, hidden), (hidden, width), (8, width))]
+    if fused:
+        packed, packed_specs = [lined, lined], [plan.whole(lined)] * 2
+    else:
+        packed, packed_specs = [(rows, 128)], [pl.BlockSpec(memory_space=pl.ANY)]
+        scratch = [pltpu.VMEM((2, *lined), F32), pltpu.SemaphoreType.DMA] + scratch
     specs = [plan.row, plan.wide_row, plan.norm(layer), plan.norm(layer)]
     specs += [plan.matrix(layer, width, hidden), plan.matrix(layer, hidden, width)]
     args = [mixed, before, gains, biases, up, down, *grads]
@@ -592,40 +649,40 @@
         specs += [plan.row] + [plan.half_row] * 4 + [plan.norm(layer + 1)]
         args += [gains]
     else:
-        specs += [plan.first, plan.second]
+        specs += plan.pieces
     return call(
-        functools.partial(ffn_backward_kernel, plan.steps, fused, layer == 0),
+        functools.partial(ffn_backward_kernel, plan.steps, fused),
         plan.steps,
         specs,
         [
             plan.half_row,
             plan.half_row,
-            *[plan.whole(shape) for shape in packed],
+            *packed_specs,
         ],
         [
             plan.half_shape,
             plan.half_shape,
             *[jax.ShapeDtypeStruct(shape, F32) for shape in packed],
         ],
-        [pltpu.VMEM(shape, F32) for shape in ((width, hidden), (hidden, width), (8, width))],
+        scratch,
         3 * 8 * 2048 * width * hidden,
         24 * 2**20,
         f"ffn_backward_{layer}",
     )(info, *args)
 
 
-def input_gradient(plan, info, a, b, du, dh, gains):
+def input_gradient(plan, info, pieces, du, dh, gains):
     return call(
         functools.partial(input_grad_kernel, plan.steps),
         plan.steps,
-        [plan.first, plan.second] + [plan.half_row] * 4 + [plan.norm(0)],
+        plan.pieces + [plan.half_row] * 4 + [plan.norm(0)],
         [plan.first, plan.second, plan.whole((8, plan.width))],
         [plan.piece_shape, plan.piece_shape, jax.ShapeDtypeStruct((8, plan.width), F32)],
         [],
         0,
         16 * 2**20,
         "input_gradient",
-    )(info, a, b, *du, *dh, gains)
+    )(info, *pieces, *du, *dh, gains)
 
 
 def item_routes(wide, section):
@@ -635,7 +692,9 @@
         for w in range(wide):
             c = w % 2
             for z in range(section):
-                pairs.append((w * section + z, (w - c + z // 2) * section + 2 * c + (z % 2 ^ flip)))
+                target = (w - c + z // 2) * section + 2 * c + (z % 2 ^ flip)
+                if target != w * section + z:
+                    pairs.append((w * section + z, target))
         routes.append(pairs)
     return routes
 
@@ -681,35 +740,38 @@
     return lax.ppermute(piece, BOTH, route)
 
 
-def join_kernel(steps, info, first, second, *refs):
-    step = pl.program_id(0)
-    from_first = (step // steps) == info[1]
-    refs[-1][...] = jnp.where(from_first, first[...], second[...])
-
-
-def join(info, first, second, after=()):
+def join_kernel(sources, info, *refs):
+    values = refs[0][...]
+    if sources == 2:
+        values = jnp.where(info[2] == 1, values, refs[1][...])
+    refs[-1][...] = values
+
+
+def join(info, own, first, second, after=()):
     rows, *cell = first.shape
-    steps = rows // ROWS
     anywhere = pl.BlockSpec(memory_space=pl.ANY)
-
-    def piece(flip):
-        def place(j, s):
-            return (jnp.where(j // steps == s[1] ^ flip, j % steps, (1 - j // steps) * (steps - 1)), 0, 0)
-
-        return pl.BlockSpec((ROWS, *cell), place)
-
-    return call(
-        functools.partial(join_kernel, steps),
-        2 * steps,
-        [piece(0), piece(1)] + [anywhere] * len(after),
-        pl.BlockSpec((None, ROWS, *cell), lambda j, s: (j // steps, j % steps, 0, 0)),
-        jax.ShapeDtypeStruct((2, rows, *cell), F32),
-        [],
-        0,
-        0,
-        "join",
-        16,
-    )(info, first, second, *after)
+    shape = jax.ShapeDtypeStruct((2, rows, *cell), F32)
+
+    def part(flip, sources, specs, others):
+        return call(
+            functools.partial(join_kernel, len(sources)),
+            rows // ROWS,
+            specs + [anywhere] * len(others),
+            pl.BlockSpec((None, ROWS, *cell), lambda j, s: (s[1] ^ flip, j, 0, 0)),
+            shape,
+            [],
+            0,
+            0,
+            f"join_{flip}",
+            16,
+            {1 + len(sources): 0} if flip else None,
+        )(info, *sources, *others)
+
+    mine = pl.BlockSpec((ROWS, *cell), lambda j, s: (j * s[2], 0, 0))
+    sent = pl.BlockSpec((ROWS, *cell), lambda j, s: (j * (1 - s[2]), 0, 0))
+    row = pl.BlockSpec((ROWS, *cell), lambda j, s: (j, 0, 0))
+    half = part(0, [own, first], [mine, sent], list(after))
+    return part(1, [second], [row], [half])
 
 
 def as_one(function, *args):
@@ -771,32 +833,55 @@
     return values
 
 
+def turned(steps):
+    return steps, steps[1:] + steps[:1]
+
+
+def sum_spread_halves(values, steps):
+    halves = jnp.split(values, 2)
+    for pair in zip(*turned(steps)):
+        halves = [sum_spread(half, *step) for half, step in zip(halves, pair)]
+    return jnp.concatenate(halves)
+
+
+def collect_halves(values, steps):
+    halves = jnp.split(values, 2)
+    for pair in list(zip(*turned(steps)))[::-1]:
+        halves = [collect(half, *step) for half, step in zip(halves, pair)]
+    return jnp.concatenate(halves)
+
+
 def packed_rows(parts, unit):
     rows = [part.reshape(-1, 128) for part in parts]
     missing = -sum(row.shape[0] for row in rows) % unit
     return jnp.concatenate(rows + [jnp.zeros((missing, 128), F32)])
 
 
-def unpack_kernel(cuts, info, mine, other, second, *outs):
+def unpack_kernel(info, mine, other, second, *outs):
     gain_out, bias_out, mix_out, offset_out, up_out, up_offset_out, down_out, down_offset_out = outs
     core = info[0]
-    low = jnp.where(core == 0, mine[...], other[...])
-    high = jnp.where(core == 0, other[...], mine[...])
+
+    def low_high(start, count):
+        a, b = mine[start : start + count], other[start : start + count]
+        return jnp.where(core == 0, a, b), jnp.where(core == 0, b, a)
+
     width = up_out.shape[1]
-    rows, lanes = width + 8, width // 128
+    rows, lanes = width + SMALL_ROWS, width // 128
     down_at, mix_at = lanes * rows, 2 * lanes * rows
+    first_mix = lanes * rows
+    inner_at = first_mix + 8 * 128 + 16
     for index in range(lanes):
         at = pl.ds(index * 128, 128)
         begin = index * rows
-        up_out[0, :, at] = low[begin : begin + width]
-        down_out[0, :, at] = high[begin : begin + width]
+        up_out[0, :, at], down_out[0, :, at] = low_high(begin, width)
         up_out[1, :, at] = second[begin : begin + width]
         down_out[1, :, at] = second[down_at + begin : down_at + begin + width]
-        small = low[begin + width : begin + rows]
-        late = second[begin + width : begin + rows]
-        inner = [low[row : row + 1] + high[row : row + 1] for row in (cuts[3] + index, cuts[3] + lanes + index)]
-        gain_out[0, 0:1, at] = inner[0]
-        bias_out[0, 0:1, at] = inner[1]
+        small = low_high(begin + width, 8)[0]
+        late = second[begin + width : begin + width + 8]
+        low, high = low_high(inner_at + 8 * index, 8)
+        inner = low + high
+        gain_out[0, 0:1, at] = inner[0:1]
+        bias_out[0, 0:1, at] = inner[1:2]
         gain_out[0, 1:2, at] = small[0:1]
         bias_out[0, 1:2, at] = small[1:2]
         gain_out[1, 0:1, at] = small[4:5]
@@ -807,28 +892,30 @@
         up_offset_out[1:2, at] = late[2:3]
         down_offset_out[0:1, at] = small[3:4]
         down_offset_out[1:2, at] = late[3:4]
-    mix_rows = mix_out[1].size // 128
-    mix_out[1] = second[mix_at : mix_at + mix_rows].reshape(mix_out.shape[1:])
-    for j in range(2):
-        for part in range(2):
-            begin = mix_at + mix_rows + (2 * j + part) * BLOCKS
-            offset_out[1, j, part] = second[begin : begin + BLOCKS]
-            for block in range(2):
-                index = (2 * j + part) * 2 + block
-                begin = cuts[1] + index * 128
-                mix_out[0, j, part, block] = low[begin : begin + 128]
-                mix_out[0, j, part, 2 + block] = high[begin : begin + 128]
-                begin = cuts[2] + index
-                offset_out[0, j, part, block : block + 1] = low[begin : begin + 1]
-                offset_out[0, j, part, 2 + block : 3 + block] = high[begin : begin + 1]
-
-
-def unpack(info, cuts, args, shapes):
+    for block in range(BLOCKS):
+        late = second[mix_at + (4 * BLOCKS) * 128 + 8 * block : mix_at + (4 * BLOCKS) * 128 + 8 * block + 8]
+        for j in range(2):
+            for part in range(2):
+                begin = mix_at + ((2 * j + part) * BLOCKS + block) * 128
+                mix_out[1, j, part, block] = second[begin : begin + 128]
+                offset_out[1, j, part, block : block + 1] = late[2 * j + part : 2 * j + part + 1]
+    for block in range(2):
+        offsets = low_high(first_mix + 8 * 128 + 8 * block, 8)
+        for j in range(2):
+            for part in range(2):
+                weights = low_high(first_mix + ((2 * j + part) * 2 + block) * 128, 128)
+                for half in range(2):
+                    at = 2 * half + block
+                    mix_out[0, j, part, at] = weights[half]
+                    offset_out[0, j, part, at : at + 1] = offsets[half][2 * j + part : 2 * j + part + 1]
+
+
+def unpack(info, args, shapes):
     def whole(shape):
         return pl.BlockSpec(shape, lambda j, s: (0,) * len(shape))
 
     return call(
-        functools.partial(unpack_kernel, cuts),
+        unpack_kernel,
         1,
         [whole(arg.shape) for arg in args],
         [whole(shape) for shape in shapes],
@@ -839,11 +926,6 @@
         "unpack",
         40,
     )(info, *args)
-
-
-def whole_blocks(core, part):
-    empty = jnp.zeros_like(part)
-    return jnp.where(core == 0, jnp.concatenate([part, empty], 2), jnp.concatenate([empty, part], 2))
 
 
 def on_device(
@@ -862,8 +944,8 @@
     plan = Plan(inputs.shape[1], width, hidden)
     routes = item_routes(lax.axis_size("wide"), lax.axis_size("section"))
     core = lax.axis_index("wide") % 2
-    parity = lax.axis_index("section") % 2
-    info = jnp.stack([core, parity]).astype(jnp.int32)
+    section = lax.axis_index("section")
+    info = jnp.stack([core, section % 2, section // 2 == core]).astype(jnp.int32)
     plain, weighted = column_tables()
     tables = [jnp.asarray(split_table(t)) for t in (plain, weighted, plain.T, weighted.T)]
 
@@ -871,70 +953,78 @@
     ffn_args = (norm_gain, norm_bias, up_weight, up_bias, down_weight, down_bias)
     back_args = (norm_gain, norm_bias, up_weight, down_weight)
 
-    def forward(xa, xb):
-        keep, send = first_norm(plan, info, xa, xb, norm_gain, norm_bias)
+    devices = lax.axis_size("wide") * lax.axis_size("section")
+    members = spread_steps("wide", 1, 2)
+    sections = spread_steps("section", 0, 2)
+    matrix_rows = 2 * (width // 128) * (hidden + SMALL_ROWS)
+    second_rows = matrix_rows + 4 * BLOCKS * 128 + 8 * BLOCKS
+    second_rows += -second_rows % (8 * devices)
+
+    def forward(x):
+        keep, send = first_norm(plan, info, x, norm_gain, norm_bias)
         keep, send, *saved0 = spectral_forward(plan, 0, info, keep, swap(send), mix_weight, mix_bias, tables)
-        u0, a0, x1, keep, send = ffn_forward(plan, 0, True, info, (xa, xb), keep, swap(send), *ffn_args)
+        u0, a0, x1, keep, send = ffn_forward(plan, 0, True, info, x, keep, swap(send), *ffn_args)
         keep, send, *saved1 = spectral_forward(plan, 1, info, keep, swap(send), mix_weight, mix_bias, tables)
         u1, a1, va, vb = ffn_forward(plan, 1, False, info, (x1,), keep, swap(send), *ffn_args)
         return (va, vb), (saved0, u0, a0, x1, saved1, u1, a1)
 
-    def backward(xa, xb, ga, gb, saved):
+    def backward(x, grads, saved):
         saved0, u0, a0, x1, saved1, u1, a1 = saved
-        keep, send, matrices = ffn_backward(plan, 1, info, u1, a1, *back_args, (ga, gb))
-        dh_keep, dh_send, mix, offsets = spectral_backward(plan, 1, info, keep, swap(send), mix_weight, saved1, tables)
+        keep, send, packed = ffn_backward(plan, 1, info, u1, a1, *back_args, grads, second_rows)
+        dh_keep, dh_send, packed = spectral_backward(
+            plan, 1, info, keep, swap(send), mix_weight, saved1, tables, packed, matrix_rows
+        )
         late = (x1, keep, send, dh_keep, swap(dh_send))
-        mixing = [whole_blocks(core, part).reshape(-1, 128) for part in (mix, offsets)]
-        second = packed_rows([matrices, *mixing], lax.axis_size("wide") * lax.axis_size("section") * 8)
-        second = lax.psum_scatter(second, "wide", scatter_dimension=0, tiled=True)
-        return *as_one(backward_first, xa, xb, late, (saved0, u0, a0)), second
-
-    def backward_first(xa, xb, late, saved):
+        second = lax.psum_scatter(packed, "wide", scatter_dimension=0, tiled=True)
+        return *as_one(backward_first, x, late, (saved0, u0, a0)), second
+
+    def backward_first(x, late, saved):
         saved0, u0, a0 = saved
-        keep, send, *matrices = ffn_backward(plan, 0, info, u0, a0, *back_args, late)
+        keep, send, kept, sent = ffn_backward(plan, 0, info, u0, a0, *back_args, late)
         dh_keep, dh_send, mix, offsets = spectral_backward(plan, 0, info, keep, swap(send), mix_weight, saved0, tables)
         last = ((keep, send), (dh_keep, swap(dh_send)))
-        dxa, dxb, inner = input_gradient(plan, info, xa, xb, *last, norm_gain)
-        return (dxa, dxb), (matrices, mix, offsets, inner)
-
-    members = spread_steps("wide", 1, 4)
-    sections = spread_steps("section", 0, 2)
-
-    def reduce_gradients(matrices, mix, offsets, inner, second):
-        mine = matrices[0] + swap(matrices[1])
-        parts = [mine, mix, offsets, inner.reshape(8, -1, 128)]
-        unit = lax.axis_size("wide") // 2 * lax.axis_size("section") * 8
-        first = sum_spread_all(packed_rows(parts, unit), members)
-        both = sum_spread_all(jnp.stack([first, second], axis=1).reshape(-1, 2, 128), sections)
-        both = collect_all(both, sections)
-        return both[:, 0], both[:, 1]
-
-    def share_first(first, outputs):
-        summed = collect_all(first, members)
-        return join(info, *outputs), summed, swap(summed)
-
-    def share_gradients(first, second, outputs):
+        dxa, dxb, inner = input_gradient(plan, info, x, *last, norm_gain)
+        return (dxa, dxb), (kept, sent, mix, offsets, inner)
+
+    def reduce_first(kept, sent, mix, offsets, inner, outputs):
+        inner = inner.reshape(8, -1, 128).transpose(1, 0, 2)
+        first = packed_rows([kept + swap(sent), mix, offsets, inner], 8 * devices)
+        first = sum_spread_all(sum_spread_halves(first, members), sections[:1])
+        outputs = join(info, *outputs)
+        [first] = passed([first], [outputs])
+        first = sum_spread_all(first, sections[1:])
+        return collect_all(first, sections), outputs
+
+    def reduce_gradients(local, second, outputs):
+        second = lax.psum(second, "section")
+        return *as_one(reduce_first, *local, outputs), second
+
+    def share_first(first):
+        summed = collect_halves(first, members)
+        return summed, swap(summed)
+
+    def share_gradients(first, second):
         second = lax.all_gather(second, "wide", axis=0, tiled=True)
-        return *as_one(share_first, first, outputs), second
-
-    xa = send_piece(pick(info, inputs, 0), routes[0])
-    xb = send_piece(pick(info, inputs, 1), routes[1])
+        return *as_one(share_first, first), second
+
+    def send_both(pieces, routes):
+        return [send_piece(piece, route) for piece, route in zip(pieces, routes)]
+
+    x = (inputs, *send_both((pick(info, inputs, 0), pick(info, inputs, 1)), routes))
     picked_grads = pick(info, out_grad, 0), pick(info, out_grad, 1)
-    ga, gb = [send_piece(piece, route) for piece, route in zip(passed(picked_grads, (xa, xb)), routes)]
-    results, saved = as_one(forward, xa, xb)
-    outputs = [send_piece(piece, route) for piece, route in zip(passed(results, (ga, gb)), back_routes)]
-    (dxa, dxb), local, second = as_one(backward, xa, xb, ga, gb, saved)
-    dxa = send_piece(*passed([dxa], outputs), back_routes[0])
-    first, second = as_one(reduce_gradients, *local, second)
-    dxb = send_piece(*passed([dxb], [dxa, first]), back_routes[1])
-    outputs, mine, other, second = as_one(share_gradients, first, second, outputs)
-
-    sizes = [part.size // 128 for part in (local[0][0], local[1], local[2])]
-    cuts = [0, sizes[0], sizes[0] + sizes[1], sum(sizes)]
-    args = [mine, other, second]
+    grads = (out_grad, *send_both(passed(picked_grads, x[1:]), routes))
+    results, saved = as_one(forward, x)
+    results = passed(results, grads[1:])
+    outputs = (results[0], *send_both(results, back_routes))
+    (dxa, dxb), local, second = as_one(backward, x, grads, saved)
+    [dxa] = passed([dxa], outputs[1:])
+    returned = send_piece(dxa, back_routes[0])
+    first, outputs, second = as_one(reduce_gradients, local, second, outputs)
+    dxb = send_piece(*passed([dxb], [returned, first]), back_routes[1])
+    mine, other, second = as_one(share_gradients, first, second)
     shapes = [a.shape for a in (norm_gain, norm_bias, mix_weight, mix_bias, up_weight, up_bias, down_weight, down_bias)]
-    gradients = unpack(info, cuts, args, shapes)
-    return (outputs, join(info, dxa, dxb, gradients[:1]), *gradients)
+    gradients = unpack(info, [mine, other, second], shapes)
+    return (outputs, join(info, dxa, returned, dxb), *gradients)
 
 
 def solution(mesh):

time: 508 us -> 474 us (0.933)
  waiting for transfers between devices: 179 us -> 165 us
  other arithmetic: 13.8 us -> 6.69 us
    ppermute x8, starting transfers between devices: 42.7 us -> 11.2 us  [send_piece(): return lax.ppermute(piece, BOTH, route)]
    ppermute x10, starting transfers between devices: 38.5 us -> 60.2 us  [swap(): lax.ppermute(values, 'wide', [(i, i ^ 1) for i in range(lax.axis_size('wi...]
    ppermute x5 -> x6, waiting for transfers between devices: 39.9 us -> 29.8 us  [collect(): lax.ppermute(values, axis, partners(axis, bit, offset))]
    ppermute x5 -> x6, waiting for transfers between devices: 53.5 us -> 44.7 us  [sum_spread(): total = total + lax.ppermute(part, axis, partners(axis, bit, offset))]
    concatenate x1 -> x2, other arithmetic: 6.94 us -> 1.34 us  [the longest x1 1.31 us: collect_halves(): return jnp.concatenate(halves)]
    pallas_call x9 -> x11, Pallas kernels: 122 us -> 120 us  [the longest x2 53.6 us: ffn_backward(): call(functools.partial(ffn_backward_kernel, plan.steps, fused), plan.step...]
  transfers between devices with their start and end apart: 30 -> 33, of which waited for: 20 -> 24; matrix products, arithmetic and copies ran while one was open for 4% -> 4% of each run, Pallas kernels for 36% -> 38%
where the time goes in v3:
time: 474 us; the launch traced here: 473 us
  Pallas kernels  184 us (39%)
  waiting for transfers between devices  165 us (35%)
  starting transfers between devices  84.5 us (18%)
  local copies, waits for them, and re-layouts  19 us (4%)
  between operations  13.9 us (3%)
  other arithmetic  6.69 us (1%)
    ppermute x10, starting transfers between devices, swap(): lax.ppermute(values, 'wide', [(i, i ^ 1) for i in range(lax.axis_size('wi...  60.2 us
    pallas_call x2, Pallas kernels, ffn_backward(): call(functools.partial(ffn_backward_kernel, plan.steps, fused), plan.step...  53.6 us
    ppermute x6, waiting for transfers between devices, sum_spread(): total = total + lax.ppermute(part, axis, partners(axis, bit, offset))  44.7 us
    ppermute x8, waiting for transfers between devices, send_piece(): return lax.ppermute(piece, BOTH, route)  41.9 us
    ppermute x10, waiting for transfers between devices, swap(): lax.ppermute(values, 'wide', [(i, i ^ 1) for i in range(lax.axis_size('wi...  39.2 us
    pallas_call x2, Pallas kernels, spectral_backward(): call(functools.partial(spectral_backward_kernel, start), 2, specs, out_sp...  32.7 us
    pallas_call x2, Pallas kernels, spectral_forward(): call(spectral_forward_kernel, 2, [cells, cells, weight, offset, table, ta...  30.3 us
    ppermute x6, waiting for transfers between devices, collect(): lax.ppermute(values, axis, partners(axis, bit, offset))  29.8 us
  transfers between devices with their start and end apart: 33, of which 24 were waited for; matrix products, arithmetic and copies ran while one was open for 4% of the time, Pallas kernels for 38%

profile of v3, /device:TPU:0, one launch (start us, length us, event | category | flops | bytes accessed | tf_op | source)
XLA Modules:
  0.0 472.8 jit_solution(8415069958769091183)
XLA Ops:
  7.3 2.5 pick.4
  11.4 3.1 collective-permute-start.23
  15.3 1.4 copy-done.2
  17.4 1.4 copy-done.3
  18.8 41.8 %collective-permute-done.23.refs_3_ = f32[16,64,512]{2,1,0:T(8,128)} collective-permute-done((f32[16,64,512]{2,1,0:T(8,128)S(1)}, f32[16,64,512]{2,1,0:T(8,128)}, u32[]{:S(2)}, u32[]{:S(2)}) %collective-permute-start.23) | collective-permute-done | bytes 2097184 | tf_op jit(solution)/shard_map/ppermute | solution.py:740
  60.6 2.0 collective-permute-start.24
  62.6 1.7 collective-permute-start.25
  64.3 133.6 %conditional.7 = (f32[16,64,512]{2,1,0:T(8,128)}, f32[16,64,512]{2,1,0:T(8,128)}, f32[2,1024,256]{2,1,0:T(8,128)}, f32[2,1024,256]{2,1,0:T(8,128)}, f32[2,1024,2...) conditional(s32[]{:T(128)} %convert_element_type.16, () %tuple.66, ...), branch_computations={%region_0.1_spmd, %region_1.2_spmd} | conditional | flops 24884901888 | bytes 171966848 | solution.py:781
  64.3 6.1 %first_norm.1 = (f32[32,64,256]{2,1,0:T(8,128)}, f32[32,64,256]{2,1,0:T(8,128)}) custom-call(s32[3]{0:T(128)S(1)} %get-tuple-element.163.info, f32[2,16,64,512]{3,2,1,0:T(8,128)} %get-tuple-element.164.own.refs_0_, f32[16,64,512]{2,1,0:T(8,128)S(1)} %get-tuple-element.165.a.refs_1_, f32[16,64,512]{2,1,0:T(8,128)} %get-tuple-element.166.b.refs_2_, ...), custom_call_target="tpu_custom_call" | custom-call | bytes 8388608 | tf_op jit(solution)/shard_map/cond/branch_1_fun/first_norm/pallas_call | solution.py:524
  70.5 48.0 %collective-permute-start = (f32[32,64,256]{2,1,0:T(8,128)}, f32[32,64,256]{2,1,0:T(8,128)S(1)}, u32[]{:S(2)}, u32[]{:S(2)}) collective-permute-start(f32[32,64,256]{2,1,0:T(8,128)} %get-tuple-element.170), channel_id=1, source_target_pairs={{0,4},{4,0},{8,12},{12,8},{16,20},{20,16},{24,28},{28,24},{1,5},{5... | collective-permute-start | bytes 6291464 | tf_op jit(solution)/shard_map/cond/branch_1_fun/ppermute | solution.py:785
  118.4 4.0 collective-permute-done.recv
  123.8 15.1 %spectral_forward_0.1 = (f32[32,64,256]{2,1,0:T(8,128)}, f32[32,64,256]{2,1,0:T(8,128)}, f32[2,1024,256]{2,1,0:T(8,128)}, f32[2,1024,256]{2,1,0:T(8,128)}, f32[2,1024,256]{2,1,0:T(8,128)}) custom-call(s32[3]{0:T(128)S(1)} %get-tuple-element.163.info, f32[32,64,256]{2,1,0:T(8,128)} %get-tuple-element.169.own, f32[32,64,256]{2,1,0:T(8,128)} %copy-done.19, ...), custom_call_target="tpu_custom_call" | custom-call | flops 6000000000 | bytes 14680064 | tf_op jit(solution)/shard_map/cond/branch_1_fun/spectral_forward_0/pallas_call | solution.py:553
  139.3 4.1 collective-permute-done.1.refs_4_
  143.4 15.2 %ffn_forward_0.1 = (f32[32,64,512]{2,1,0:T(8,128)}, f32[32,64,512]{2,1,0:T(8,128)}, f32[32,64,512]{2,1,0:T(8,128)}, f32[32,64,256]{2,1,0:T(8,128)}, f32[32,64,256]{2,1,0:T(8,128)}) custom-call(s32[3]{0:T(128)S(1)} %get-tuple-element.163.info, f32[2,16,64,512]{3,2,1,0:T(8,128)S(1)} %copy-done.5, f32[16,64,512]{2,1,0:T(8,128)S(1)} %get-tuple-element.165.a.refs_1_, ...), custom_call_target="tpu_custom_call" | custom-call | flops 6442450944 | bytes 25165824 | tf_op jit(solution)/shard_map/cond/branch_1_fun/ffn_forward_0/pallas_call | solution.py:622
  158.9 4.0 collective-permute-done.2.recv
  164.2 15.2 %spectral_forward_1.1 = (f32[32,64,256]{2,1,0:T(8,128)}, f32[32,64,256]{2,1,0:T(8,128)}, f32[2,1024,256]{2,1,0:T(8,128)}, f32[2,1024,256]{2,1,0:T(8,128)}, f32[2,1024,256]{2,1,0:T(8,128)}) custom-call(s32[3]{0:T(128)S(1)} %get-tuple-element.163.info, f32[32,64,256]{2,1,0:T(8,128)} %get-tuple-element.182.own, f32[32,64,256]{2,1,0:T(8,128)} %copy-done.18, ...), custom_call_target="tpu_custom_call" | custom-call | flops 6000000000 | bytes 14680064 | tf_op jit(solution)/shard_map/cond/branch_1_fun/spectral_forward_1/pallas_call | solution.py:553
  179.8 4.1 collective-permute-done.3.refs_2_
  183.9 14.0 %ffn_forward_1.1 = (f32[32,64,512]{2,1,0:T(8,128)}, f32[32,64,512]{2,1,0:T(8,128)}, f32[16,64,512]{2,1,0:T(8,128)}, f32[16,64,512]{2,1,0:T(8,128)}) custom-call(s32[3]{0:T(128)S(1)} %get-tuple-element.163.info, f32[32,64,512]{2,1,0:T(8,128)} %get-tuple-element.441.refs_0_, f32[32,64,256]{2,1,0:T(8,128)} %get-tuple-element.184.refs_1_, ...), custom_call_target="tpu_custom_call" | custom-call | flops 6442450944 | bytes 25165824 | tf_op jit(solution)/shard_map/cond/branch_1_fun/ffn_forward_1/pallas_call | solution.py:622
  198.0 2.1 collective-permute-start.26
  200.3 122.2 %conditional.8 = (f32[16,64,512]{2,1,0:T(8,128)}, f32[16,64,512]{2,1,0:T(8,128)}, f32[4,544,128]{2,1,0:T(8,128)}, f32[4,544,128]{2,1,0:T(8,128)}, f32[2,2,2,128,...) conditional(s32[]{:T(128)} %convert_element_type.16, () %tuple.65, ...), branch_computations={%region_2.3_spmd, %region_3.7_spmd} | conditional | flops 25769803776 | bytes 154370736 | solution.py:781
  200.4 25.0 %ffn_backward_1.1 = (f32[32,64,256]{2,1,0:T(8,128)S(1)}, f32[32,64,256]{2,1,0:T(8,128)}, f32[6656,128]{1,0:T(8,128)}) custom-call(s32[3]{0:T(128)S(1)} %get-tuple-element.230.info, f32[32,64,512]{2,1,0:T(8,128)} %get-tuple-element.238.refs_0_, f32[32,64,512]{2,1,0:T(8,128)} %get-tuple-element.239.refs_1_, f32[2,2,512]{2,1,0:T(2,128)S(1)} %get-tuple-element.233.refs_2_, ...), custom_call_target="tpu_custom_call" | custom-call | flops 12884901888 | bytes 25165824 | tf_op jit(solution)/shard_map/cond/branch_1_fun/ffn_backward_1/pallas_call | solution.py:653
  225.4 8.0 %collective-permute-start.6 = (f32[32,64,256]{2,1,0:T(8,128)}, f32[32,64,256]{2,1,0:T(8,128)}, u32[]{:S(2)}, u32[]{:S(2)}) collective-permute-start(f32[32,64,256]{2,1,0:T(8,128)} %get-tuple-element.244), channel_id=1, source_target_pairs={{0,4},{4,0},{8,12},{12,8},{16,20},{20,16},{24,28},{28,24},{1,5},{5... | collective-permute-start | bytes 6291464 | tf_op jit(solution)/shard_map/cond/branch_1_fun/ppermute | solution.py:785
  233.4 4.1 collective-permute-done.6.recv
  237.5 16.1 %spectral_backward_1.1 = (f32[32,64,256]{2,1,0:T(8,128)}, f32[32,64,256]{2,1,0:T(8,128)}, f32[6656,128]{1,0:T(8,128)}) custom-call(s32[3]{0:T(128)S(1)} %get-tuple-element.230.info, f32[32,64,256]{2,1,0:T(8,128)S(1)} %get-tuple-element.243.own, f32[32,64,256]{2,1,0:T(8,128)} %collective-permute-done.6.recv, ...), custom_call_target="tpu_custom_call", output_to_operand_aliasing={{2}: (9, {})} | custom-call | tf_op jit(solution)/shard_map/cond/branch_1_fun/spectral_backward_1/pallas_call | solution.py:590
  254.2 4.1 collective-permute-done.7
  258.3 64.3 %conditional = (f32[16,64,512]{2,1,0:T(8,128)}, f32[16,64,512]{2,1,0:T(8,128)}, f32[4,544,128]{2,1,0:T(8,128)}, f32[4,544,128]{2,1,0:T(8,128)}, f32[2,2,2,128,12...) conditional(s32[]{:T(128)} %convert_element_type.3, () %tuple.40, (s32[3]{0:T(128)S(1)}, ...), branch_computations={%region_4.4_spmd, %region_5.5_spmd} | conditional | flops 12884901888 | bytes 83886272 | solution.py:781
  258.3 28.6 %ffn_backward_0.1 = (f32[32,64,256]{2,1,0:T(8,128)}, f32[32,64,256]{2,1,0:T(8,128)}, f32[4,544,128]{2,1,0:T(8,128)}, f32[4,544,128]{2,1,0:T(8,128)}) custom-call(s32[3]{0:T(128)S(1)} %get-tuple-element.198.info, f32[32,64,512]{2,1,0:T(8,128)} %get-tuple-element.202.refs_0_, f32[32,64,512]{2,1,0:T(8,128)} %get-tuple-element.203.refs_1_, ...), custom_call_target="tpu_custom_call" | custom-call | flops 12884901888 | bytes 25165824 | tf_op jit(solution)/shard_map/cond/branch_1_fun/cond/branch_1_fun/ffn_backward_0/pallas_call | solution.py:653
  287.5 4.0 collective-permute-done.4.recv
  291.5 1.3 copy-done.11
  292.8 16.5 %spectral_backward_0.1 = (f32[32,64,256]{2,1,0:T(8,128)}, f32[32,64,256]{2,1,0:T(8,128)}, f32[2,2,2,128,128]{4,3,2,1,0:T(8,128)}, f32[2,8,128]{2,1,0:T(8,128)}) custom-call(s32[3]{0:T(128)S(1)} %get-tuple-element.198.info, f32[32,64,256]{2,1,0:T(8,128)} %get-tuple-element.213.own.du_kept, f32[32,64,256]{2,1,0:T(8,128)} %copy-done.11, ...), custom_call_target="tpu_custom_call" | custom-call | tf_op jit(solution)/shard_map/cond/branch_1_fun/cond/branch_1_fun/spectral_backward_0/pallas_call | solution.py:590
  309.8 4.1 collective-permute-done.5.dh_taken
  313.9 8.7 %input_gradient.1 = (f32[16,64,512]{2,1,0:T(8,128)}, f32[16,64,512]{2,1,0:T(8,128)}, f32[8,512]{1,0:T(8,128)}) custom-call(s32[3]{0:T(128)S(1)} %get-tuple-element.198.info, f32[2,16,64,512]{3,2,1,0:T(8,128)S(1)} %copy-done.6, f32[16,64,512]{2,1,0:T(8,128)S(1)} %get-tuple-element.200.a, f32[16,64,512]{2,1,0:T(8,128)} %get-tuple-element.201.b, ...), custom_call_target="tpu_custom_call" | custom-call | bytes 16777216 | tf_op jit(solution)/shard_map/cond/branch_1_fun/cond/branch_1_fun/input_gradient/pallas_call | solution.py:675
  323.4 89.7 %conditional.9 = (f32[832,128]{1,0:T(8,128)}, f32[2,16,64,512]{3,2,1,0:T(8,128)}, f32[832,128]{1,0:T(8,128)}) conditional(s32[]{:T(128)} %convert_element_type.16, () %tuple.64, (f32[4,544,128]{2,1,0:T(8,128)}, f32[4,544,128]{2,1,0:T(8,128)}, f32[2,2,2,128,128]{4,3,2,1,0:T(8,128)}, f32[2,8,128]{2,1,0:T(8,128)}, f32[8,512]{1,0:T(8,128)}, ...), branch_computations={%region_7.8_spmd, %region_8.12_spmd} | conditional | flops 890966 | bytes 38856152 | solution.py:781
  324.2 88.9 %conditional.1 = (f32[832,128]{1,0:T(8,128)}, f32[2,16,64,512]{3,2,1,0:T(8,128)}) conditional(s32[]{:T(128)} %convert_element_type.5, () %tuple.46, (f32[4,544,128]{2,1,0:T(8,128)}, f32[4,544,128]{2,1,0:T(8,128)}, f32[2,2,2,128,128]{4,3,2,1,0:T(8,128)}, f32[2,8,128]{2,1,0:T(8,128)}, f32[8,512]{1,0:T(8,128)}, /*index=5*/s32[3]{0:T(128)S(1)}, ...), branch_computations={%region_9.9_spmd, %region_10.10_spmd} | conditional | flops 784465 | bytes 36300064 | solution.py:781
  324.2 1.6 collective-permute-start.8
  325.8 2.6 collective-permute-done.8
  328.3 1.4 add.84
  329.9 1.6 collective-permute-start.9
  335.7 1.5 collective-permute-start.11
  337.3 4.9 %collective-permute-done.9 = f32[832,128]{1,0:T(8,128)} collective-permute-done((f32[832,128]{1,0:T(8,128)S(1)}, f32[832,128]{1,0:T(8,128)}, u32[]{:S(2)}, u32[]{:S(2)}) %collective-permute-start.9) | collective-permute-done | bytes 426016 | tf_op jit(solution)/shard_map/cond/branch_1_fun/cond/branch_1_fun/ppermute | solution.py:807
  343.2 1.6 collective-permute-start.10
  344.8 3.9 collective-permute-done.11
  350.5 1.8 collective-permute-done.10
  352.3 3.5 collective-permute-done.12
  355.9 1.4 collective-permute-start.13
  357.3 3.5 join_0.2.refs_1_
  360.8 3.2 join_1.2.refs_1_
  364.0 19.4 %collective-permute-done.13 = f32[416,128]{1,0:T(8,128)S(1)} collective-permute-done((f32[416,128]{1,0:T(8,128)S(1)}, f32[416,128]{1,0:T(8,128)S(1)}, u32[]{:S(2)}, u32[]{:S(2)}) %collective-permute-start.13) | collective-permute-done | bytes 213024 | tf_op jit(solution)/shard_map/cond/branch_1_fun/cond/branch_1_fun/ppermute | solution.py:807
  385.2 11.3 %collective-permute-done.14 = f32[208,128]{1,0:T(8,128)S(1)} collective-permute-done((f32[208,128]{1,0:T(8,128)S(1)}, f32[208,128]{1,0:T(8,128)S(1)}, u32[]{:S(2)}, u32[]{:S(2)}) %collective-permute-start.14) | collective-permute-done | bytes 106528 | tf_op jit(solution)/shard_map/cond/branch_1_fun/cond/branch_1_fun/ppermute | solution.py:807
  397.5 7.7 %collective-permute-done.15 = f32[208,128]{1,0:T(8,128)S(1)} collective-permute-done((f32[208,128]{1,0:T(8,128)S(1)}, f32[208,128]{1,0:T(8,128)S(1)}, u32[]{:S(2)}, u32[]{:S(2)}) %collective-permute-start.15) | collective-permute-done | bytes 106528 | tf_op jit(solution)/shard_map/cond/branch_1_fun/cond/branch_1_fun/ppermute | solution.py:815
  406.8 5.6 %collective-permute-done.16 = f32[416,128]{1,0:T(8,128)S(1)} collective-permute-done((f32[416,128]{1,0:T(8,128)S(1)}, f32[416,128]{1,0:T(8,128)S(1)}, u32[]{:S(2)}, u32[]{:S(2)}) %collective-permute-start.16) | collective-permute-done | bytes 213024 | tf_op jit(solution)/shard_map/cond/branch_1_fun/cond/branch_1_fun/ppermute | solution.py:815
  414.7 39.6 %conditional.10 = (f32[3328,128]{1,0:T(8,128)}, f32[3328,128]{1,0:T(8,128)}, f32[6656,128]{1,0:T(8,128)}) conditional(s32[]{:T(128)} %convert_element_type.16, () %tuple.70, (f32[832,128]{1,0:T(8,128)}, f32[832,128]{1,0:T(8,128)}) %tuple.71), branch_computations={%region_12.13_spmd, %region_13.16_spmd} | conditional | flops 426030 | bytes 35357480 | solution.py:781
  415.4 31.2 %conditional.2 = (f32[3328,128]{1,0:T(8,128)}, f32[3328,128]{1,0:T(8,128)}) conditional(s32[]{:T(128)} %convert_element_type.8, () %tuple.52, f32[832,128]{1,0:T(8,128)} %get-tuple-element.289), branch_computations={%region_14.14_spmd, %region_15.15_spmd} | conditional | flops 426025 | bytes 23855802 | solution.py:781
  416.5 1.5 collective-permute-start.17
  418.0 1.5 collective-permute-start.19
  421.5 2.3 collective-permute-done.17
  423.9 1.7 collective-permute-start.18
  425.7 1.4 collective-permute-start.20
  427.2 13.9 %collective-permute-done.18 = f32[832,128]{1,0:T(8,128)S(1)} collective-permute-done((f32[832,128]{1,0:T(8,128)S(1)}, f32[832,128]{1,0:T(8,128)S(1)}, u32[]{:S(2)}, u32[]{:S(2)}) %collective-permute-start.18) | collective-permute-done | bytes 426016 | tf_op jit(solution)/shard_map/cond/branch_1_fun/cond/branch_1_fun/ppermute | solution.py:815
  442.7 3.9 collective-permute-done.21
  446.6 7.7 %all-gather.2.cloned.1.call-done = f32[6656,128]{1,0:T(8,128)} async-done(((f32[832,128]{1,0:T(8,128)}), f32[6656,128]{1,0:T(8,128)}) %all-gather.2.cloned.1.call-update) | async-done | bytes 3407888 | tf_op jit(solution)/shard_map/cond/branch_1_fun/all_gather | solution.py:1007
  454.3 6.8 %unpack.1 = (f32[2,2,512]{2,1,0:T(2,128)}, f32[2,2,512]{2,1,0:T(2,128)}, f32[2,2,2,4,128,128]{5,4,3,2,1,0:T(8,128)}, f32[2,2,2,4,128]{4,3,2,1,0:T(4,128)}, f32[2...) custom-call(s32[3]{0:T(128)S(1)} %pad_add_fusion.info, ...), custom_call_target="tpu_custom_call" | custom-call | tf_op jit(solution)/shard_map/unpack/pallas_call | solution.py:917
  461.1 3.2 join_0.3.refs_1_
  464.3 1.9 join_1.3
  (123 shorter events, 30.2 us)
Async XLA Ops:
  7.3 3.4 copy-start.4
  9.7 4.8 %copy-start.7 = (f32[2,16,64,512]{3,2,1,0:T(8,128)S(1)}, f32[2,16,64,512]{3,2,1,0:T(8,128)}, u32[]{:S(2)}) copy-start(f32[2,16,64,512]{3,2,1,0:T(8,128)} %source.7) | copy-start | bytes 12582916
  9.8 9.0 %collective-permute-start.22 = (f32[16,64,512]{2,1,0:T(8,128)S(1)}, f32[16,64,512]{2,1,0:T(8,128)S(1)}, u32[]{:S(2)}, u32[]{:S(2)}) collective-permute-start(f32[16,64,512]{2,1,0:T(8,128)S(1)} %pick.4), channel_id=1, source_target_pairs={{2,4},{3,5},{4,2},{5,3},{10,12},{11,13},{12,10},{13,11},{18,20},{1... | collective-permute-start | bytes 6291464 | tf_op jit(solution)/shard_map/ppermute | solution.py:740
  11.4 49.2 %collective-permute-start.23 = (f32[16,64,512]{2,1,0:T(8,128)S(1)}, f32[16,64,512]{2,1,0:T(8,128)}, u32[]{:S(2)}, u32[]{:S(2)}) collective-permute-start(f32[16,64,512]{2,1,0:T(8,128)S(1)} %pick.5), channel_id=1, source_target_pairs={{0,1},{1,0},{2,5},{3,4},{4,3},{5,2},{6,7},{7,6},{8,9},{9,8},{10,13... | collective-permute-start | bytes 6291464 | tf_op jit(solution)/shard_map/ppermute | solution.py:740
  15.3 1.4 copy-start.2
  17.4 1.4 copy-start.3
  18.8 45.5 %copy-start.14 = (f32[2,2,512]{2,1,0:T(2,128)S(1)}, f32[2,2,512]{2,1,0:T(2,128)}, u32[]{:S(2)}) copy-start(f32[2,2,512]{2,1,0:T(2,128)} %param.29) | copy-start | bytes 24580
  18.8 45.5 %copy-start.15 = (f32[2,2,512]{2,1,0:T(2,128)S(1)}, f32[2,2,512]{2,1,0:T(2,128)}, u32[]{:S(2)}) copy-start(f32[2,2,512]{2,1,0:T(2,128)} %param.30) | copy-start | bytes 24580
  18.8 45.5 %copy-start.20 = (f32[2,2,2,4,128]{4,3,2,1,0:T(4,128)S(1)}, f32[2,2,2,4,128]{4,3,2,1,0:T(4,128)}, u32[]{:S(2)}) copy-start(f32[2,2,2,4,128]{4,3,2,1,0:T(4,128)} %param.32) | copy-start | bytes 49156
  18.8 45.5 %copy-start.21 = (f32[2,512]{1,0:T(2,128)S(1)}, f32[2,512]{1,0:T(2,128)}, u32[]{:S(2)}) copy-start(f32[2,512]{1,0:T(2,128)} %param.34) | copy-start | bytes 12292
  18.8 45.5 %copy-start.22 = (f32[2,512]{1,0:T(2,128)S(1)}, f32[2,512]{1,0:T(2,128)}, u32[]{:S(2)}) copy-start(f32[2,512]{1,0:T(2,128)} %param.36) | copy-start | bytes 12292
  60.6 137.3 %collective-permute-start.24 = (f32[16,64,512]{2,1,0:T(8,128)}, f32[16,64,512]{2,1,0:T(8,128)}, u32[]{:S(2)}, u32[]{:S(2)}) collective-permute-start(f32[16,64,512]{2,1,0:T(8,128)} %get-tuple-element.344), channel_id=1, source_target_pairs={{2,4},{3,5},{4,2},{5,3},{10,12},{11,13},{12,10},{13,11},{18,20},{1... | collective-permute-start | bytes 6291464 | tf_op jit(solution)/shard_map/ppermute | solution.py:740
  62.6 135.3 %collective-permute-start.25 = (f32[16,64,512]{2,1,0:T(8,128)}, f32[16,64,512]{2,1,0:T(8,128)}, u32[]{:S(2)}, u32[]{:S(2)}) collective-permute-start(f32[16,64,512]{2,1,0:T(8,128)} %get-tuple-element.345), channel_id=1, source_target_pairs={{0,1},{1,0},{2,5},{3,4},{4,3},{5,2},{6,7},{7,6},{8,9},{9,8},{10,13... | collective-permute-start | bytes 6291464 | tf_op jit(solution)/shard_map/ppermute | solution.py:740
  70.5 52.0 %collective-permute-start = (f32[32,64,256]{2,1,0:T(8,128)}, f32[32,64,256]{2,1,0:T(8,128)S(1)}, u32[]{:S(2)}, u32[]{:S(2)}) collective-permute-start(f32[32,64,256]{2,1,0:T(8,128)} %get-tuple-element.170), channel_id=1, source_target_pairs={{0,4},{4,0},{8,12},{12,8},{16,20},{20,16},{24,28},{28,24},{1,5},{5... | collective-permute-start | bytes 6291464 | tf_op jit(solution)/shard_map/cond/branch_1_fun/ppermute | solution.py:785
  122.4 1.3 copy-start.19
  123.8 19.6 %copy-start.5 = (f32[2,16,64,512]{3,2,1,0:T(8,128)S(1)}, f32[2,16,64,512]{3,2,1,0:T(8,128)}, u32[]{:S(2)}) copy-start(f32[2,16,64,512]{3,2,1,0:T(8,128)} %get-tuple-element.164.own.refs_0_) | copy-start | bytes 12582916 | tf_op jit(solution)/shard_map/cond
  138.9 4.5 collective-permute-start.1
  158.5 4.4 collective-permute-start.2
  162.9 1.3 copy-start.18
  164.2 19.7 %copy-start.16 = (f32[2,512,512]{2,1,0:T(8,128)S(1)}, f32[2,512,512]{2,1,0:T(8,128)}, u32[]{:S(2)}) copy-start(f32[2,512,512]{2,1,0:T(8,128)} %get-tuple-element.177.refs_7_.refs_5_) | copy-start | bytes 6291460 | tf_op jit(solution)/shard_map/cond
  164.2 19.7 %copy-start.17 = (f32[2,512,512]{2,1,0:T(8,128)S(1)}, f32[2,512,512]{2,1,0:T(8,128)}, u32[]{:S(2)}) copy-start(f32[2,512,512]{2,1,0:T(8,128)} %get-tuple-element.179.refs_9_.refs_7_) | copy-start | bytes 6291460 | tf_op jit(solution)/shard_map/cond
  179.4 4.5 collective-permute-start.3
  198.0 124.6 %collective-permute-start.26 = (f32[16,64,512]{2,1,0:T(8,128)}, f32[16,64,512]{2,1,0:T(8,128)}, u32[]{:S(2)}, u32[]{:S(2)}) collective-permute-start(f32[16,64,512]{2,1,0:T(8,128)} %get-tuple-element.362), channel_id=1, source_target_pairs={{4,2},{5,3},{2,4},{3,5},{12,10},{13,11},{10,12},{11,13},{20,18},{2... | collective-permute-start | bytes 6291464 | tf_op jit(solution)/shard_map/ppermute | solution.py:740
  200.0 122.6 %collective-permute-start.27 = (f32[16,64,512]{2,1,0:T(8,128)}, f32[16,64,512]{2,1,0:T(8,128)}, u32[]{:S(2)}, u32[]{:S(2)}) collective-permute-start(f32[16,64,512]{2,1,0:T(8,128)} %get-tuple-element.363), channel_id=1, source_target_pairs={{1,0},{0,1},{5,2},{4,3},{3,4},{2,5},{7,6},{6,7},{9,8},{8,9},{13,10... | collective-permute-start | bytes 6291464 | tf_op jit(solution)/shard_map/ppermute | solution.py:740
  200.3 122.2 %reduce-scatter.2.cloned.1.call-start = ((), (), s32[]{:S(2)}) async-start(), calls=%async_computation.1 | async-start | bytes 3833856 | tf_op jit(solution)/shard_map/cond/branch_1_fun/reduce_scatter | solution.py:978
  200.3 37.2 %copy-start.8 = (f32[2,2,2,4,128,128]{5,4,3,2,1,0:T(8,128)S(1)}, f32[2,2,2,4,128,128]{5,4,3,2,1,0:T(8,128)}, u32[]{:S(2)}) copy-start(f32[2,2,2,4,128,128]{5,4,3,2,1,0:T(8,128)} %get-tuple-element.245.weight) | copy-start | bytes 6291460 | tf_op jit(solution)/shard_map/cond
  200.3 37.2 %copy-start.12 = (bf16[64,256]{1,0:T(8,128)(2,1)S(1)}, bf16[64,256]{1,0:T(8,128)(2,1)}, u32[]{:S(2)}) copy-start(bf16[64,256]{1,0:T(8,128)(2,1)} %constant.235.clone.1.table_in) | copy-start | bytes 98308 | tf_op jit(solution)/shard_map/cond
  200.3 37.2 %copy-start.13 = (bf16[64,256]{1,0:T(8,128)(2,1)S(1)}, bf16[64,256]{1,0:T(8,128)(2,1)}, u32[]{:S(2)}) copy-start(bf16[64,256]{1,0:T(8,128)(2,1)} %constant.236.clone.1.table_out) | copy-start | bytes 98308 | tf_op jit(solution)/shard_map/cond
  225.4 28.3 %copy-start.10 = (f32[32,64,256]{2,1,0:T(8,128)}, f32[32,64,256]{2,1,0:T(8,128)S(1)}, u32[]{:S(2)}) copy-start(f32[32,64,256]{2,1,0:T(8,128)S(1)} %get-tuple-element.243.own) | copy-start | bytes 6291460 | tf_op jit(solution)/shard_map/cond
  225.4 12.1 %collective-permute-start.6 = (f32[32,64,256]{2,1,0:T(8,128)}, f32[32,64,256]{2,1,0:T(8,128)}, u32[]{:S(2)}, u32[]{:S(2)}) collective-permute-start(f32[32,64,256]{2,1,0:T(8,128)} %get-tuple-element.244), channel_id=1, source_target_pairs={{0,4},{4,0},{8,12},{12,8},{16,20},{20,16},{24,28},{28,24},{1,5},{5... | collective-permute-start | bytes 6291464 | tf_op jit(solution)/shard_map/cond/branch_1_fun/ppermute | solution.py:785
  253.7 4.6 collective-permute-start.7
  286.9 4.6 collective-permute-start.4
  291.5 1.3 copy-start.11
  292.8 21.1 %copy-start.6 = (f32[2,16,64,512]{3,2,1,0:T(8,128)S(1)}, f32[2,16,64,512]{3,2,1,0:T(8,128)}, u32[]{:S(2)}) copy-start(f32[2,16,64,512]{3,2,1,0:T(8,128)} %get-tuple-element.199.own) | copy-start | bytes 12582916 | tf_op jit(solution)/shard_map/cond/branch_1_fun/cond
  309.3 4.6 collective-permute-start.5
  322.6 90.5 %collective-permute-start.28 = (f32[16,64,512]{2,1,0:T(8,128)}, f32[16,64,512]{2,1,0:T(8,128)S(1)}, u32[]{:S(2)}, u32[]{:S(2)}) collective-permute-start(f32[16,64,512]{2,1,0:T(8,128)} %passed.8.refs_0_), channel_id=1, source_target_pairs={{4,2},{5,3},{2,4},{3,5},{12,10},{13,11},{10,12},{11,13},{20,18},{2... | collective-permute-start | bytes 6291464 | tf_op jit(solution)/shard_map/ppermute | solution.py:740
  323.4 89.7 %all-reduce.2.cloned.1.call-start = ((), (), s32[]{:S(2)}) async-start(), calls=%async_computation.2 | async-start | bytes 851968 | tf_op jit(solution)/shard_map/cond/branch_1_fun/psum | solution.py:999
  324.2 4.2 collective-permute-start.8
  329.9 12.3 %collective-permute-start.9 = (f32[832,128]{1,0:T(8,128)S(1)}, f32[832,128]{1,0:T(8,128)}, u32[]{:S(2)}, u32[]{:S(2)}) collective-permute-start(f32[832,128]{1,0:T(8,128)S(1)} %dynamic-slice_bitcast_fusion.1), channel_id=1, source_target_pairs={{0,8},{4,12},{8,0},{12,4},{16,24},{20,28},{24,16},{28,20},{1,9},{5... | collective-permute-start | bytes 1277960 | tf_op jit(solution)/shard_map/cond/branch_1_fun/cond/branch_1_fun/ppermute | solution.py:807
  334.0 0.9 copy-start.9
  335.7 13.0 %collective-permute-start.11 = (f32[832,128]{1,0:T(8,128)}, f32[832,128]{1,0:T(8,128)}, u32[]{:S(2)}, u32[]{:S(2)}) collective-permute-start(f32[832,128]{1,0:T(8,128)} %dynamic-slice_bitcast_fusion), channel_id=1, source_target_pairs={{0,16},{4,20},{8,24},{12,28},{16,0},{20,4},{24,8},{28,12},{1,17},{... | collective-permute-start | bytes 1277960 | tf_op jit(solution)/shard_map/cond/branch_1_fun/cond/branch_1_fun/ppermute | solution.py:807
  343.2 9.0 %collective-permute-start.10 = (f32[416,128]{1,0:T(8,128)S(1)}, f32[416,128]{1,0:T(8,128)S(1)}, u32[]{:S(2)}, u32[]{:S(2)}) collective-permute-start(f32[416,128]{1,0:T(8,128)S(1)} %dynamic-slice_bitcast_fusion.4), channel_id=1, source_target_pairs={{0,16},{4,20},{8,24},{12,28},{16,0},{20,4},{24,8},{28,12},{1,17},{... | collective-permute-start | bytes 638984 | tf_op jit(solution)/shard_map/cond/branch_1_fun/cond/branch_1_fun/ppermute | solution.py:807
  349.9 5.9 %collective-permute-start.12 = (f32[416,128]{1,0:T(8,128)S(1)}, f32[416,128]{1,0:T(8,128)S(1)}, u32[]{:S(2)}, u32[]{:S(2)}) collective-permute-start(f32[416,128]{1,0:T(8,128)S(1)} %dynamic-slice_bitcast_fusion.3), channel_id=1, source_target_pairs={{0,8},{4,12},{8,0},{12,4},{16,24},{20,28},{24,16},{28,20},{1,9},{5... | collective-permute-start | bytes 638984 | tf_op jit(solution)/shard_map/cond/branch_1_fun/cond/branch_1_fun/ppermute | solution.py:807
  355.9 27.4 %collective-permute-start.13 = (f32[416,128]{1,0:T(8,128)S(1)}, f32[416,128]{1,0:T(8,128)S(1)}, u32[]{:S(2)}, u32[]{:S(2)}) collective-permute-start(f32[416,128]{1,0:T(8,128)S(1)} %dynamic-slice_bitcast_fusion.2), channel_id=1, source_target_pairs={{0,1},{1,0},{2,3},{3,2},{4,5},{5,4},{6,7},{7,6},{8,9},{9,8},{10,11... | collective-permute-start | bytes 638984 | tf_op jit(solution)/shard_map/cond/branch_1_fun/cond/branch_1_fun/ppermute | solution.py:807
  384.9 11.5 %collective-permute-start.14 = (f32[208,128]{1,0:T(8,128)S(1)}, f32[208,128]{1,0:T(8,128)S(1)}, u32[]{:S(2)}, u32[]{:S(2)}) collective-permute-start(f32[208,128]{1,0:T(8,128)S(1)} %dynamic-slice_bitcast_fusion.5), channel_id=1, source_target_pairs={{0,2},{1,3},{2,0},{3,1},{4,6},{5,7},{6,4},{7,5},{8,10},{9,11},{10,... | collective-permute-start | bytes 319496 | tf_op jit(solution)/shard_map/cond/branch_1_fun/cond/branch_1_fun/ppermute | solution.py:807
  397.4 7.8 %collective-permute-start.15 = (f32[208,128]{1,0:T(8,128)S(1)}, f32[208,128]{1,0:T(8,128)S(1)}, u32[]{:S(2)}, u32[]{:S(2)}) collective-permute-start(f32[208,128]{1,0:T(8,128)S(1)} %get-tuple-element.396), channel_id=1, source_target_pairs={{0,2},{1,3},{2,0},{3,1},{4,6},{5,7},{6,4},{7,5},{8,10},{9,11},{10,... | collective-permute-start | bytes 319496 | tf_op jit(solution)/shard_map/cond/branch_1_fun/cond/branch_1_fun/ppermute | solution.py:815
  405.2 7.1 %collective-permute-start.16 = (f32[416,128]{1,0:T(8,128)S(1)}, f32[416,128]{1,0:T(8,128)S(1)}, u32[]{:S(2)}, u32[]{:S(2)}) collective-permute-start(f32[416,128]{1,0:T(8,128)S(1)} %bitcast.97), channel_id=1, source_target_pairs={{0,1},{1,0},{2,3},{3,2},{4,5},{5,4},{6,7},{7,6},{8,9},{9,8},{10,11... | collective-permute-start | bytes 638984 | tf_op jit(solution)/shard_map/cond/branch_1_fun/cond/branch_1_fun/ppermute | solution.py:815
  413.1 1.3 copy-start
  414.4 49.9 %collective-permute-start.29 = (f32[16,64,512]{2,1,0:T(8,128)}, f32[16,64,512]{2,1,0:T(8,128)S(1)}, u32[]{:S(2)}, u32[]{:S(2)}) collective-permute-start(f32[16,64,512]{2,1,0:T(8,128)} %passed.9), channel_id=1, source_target_pairs={{1,0},{0,1},{5,2},{4,3},{3,4},{2,5},{7,6},{6,7},{9,8},{8,9},{13,10... | collective-permute-start | bytes 6291464 | tf_op jit(solution)/shard_map/ppermute | solution.py:740
  414.7 39.6 %all-gather.2.cloned.1.call-start = ((), (), s32[]{:S(2)}) async-start(), calls=%async_computation.3 | async-start | bytes 3833856 | tf_op jit(solution)/shard_map/cond/branch_1_fun/all_gather | solution.py:1007
  416.5 7.4 %collective-permute-start.17 = (f32[416,128]{1,0:T(8,128)S(1)}, f32[416,128]{1,0:T(8,128)S(1)}, u32[]{:S(2)}, u32[]{:S(2)}) collective-permute-start(f32[416,128]{1,0:T(8,128)S(1)} %get-tuple-element.397), channel_id=1, source_target_pairs={{0,16},{4,20},{8,24},{12,28},{16,0},{20,4},{24,8},{28,12},{1,17},{... | collective-permute-start | bytes 638984 | tf_op jit(solution)/shard_map/cond/branch_1_fun/cond/branch_1_fun/ppermute | solution.py:815
  418.0 7.7 %collective-permute-start.19 = (f32[416,128]{1,0:T(8,128)S(1)}, f32[416,128]{1,0:T(8,128)S(1)}, u32[]{:S(2)}, u32[]{:S(2)}) collective-permute-start(f32[416,128]{1,0:T(8,128)S(1)} %get-tuple-element.398), channel_id=1, source_target_pairs={{0,8},{4,12},{8,0},{12,4},{16,24},{20,28},{24,16},{28,20},{1,9},{5... | collective-permute-start | bytes 638984 | tf_op jit(solution)/shard_map/cond/branch_1_fun/cond/branch_1_fun/ppermute | solution.py:815
  423.9 17.2 %collective-permute-start.18 = (f32[832,128]{1,0:T(8,128)S(1)}, f32[832,128]{1,0:T(8,128)S(1)}, u32[]{:S(2)}, u32[]{:S(2)}) collective-permute-start(f32[832,128]{1,0:T(8,128)S(1)} %bitcast.87), channel_id=1, source_target_pairs={{0,8},{4,12},{8,0},{12,4},{16,24},{20,28},{24,16},{28,20},{1,9},{5... | collective-permute-start | bytes 1277960 | tf_op jit(solution)/shard_map/cond/branch_1_fun/cond/branch_1_fun/ppermute | solution.py:815
  425.7 15.7 %collective-permute-start.20 = (f32[832,128]{1,0:T(8,128)S(1)}, f32[832,128]{1,0:T(8,128)S(1)}, u32[]{:S(2)}, u32[]{:S(2)}) collective-permute-start(f32[832,128]{1,0:T(8,128)S(1)} %bitcast.89), channel_id=1, source_target_pairs={{0,16},{4,20},{8,24},{12,28},{16,0},{20,4},{24,8},{28,12},{1,17},{... | collective-permute-start | bytes 1277960 | tf_op jit(solution)/shard_map/cond/branch_1_fun/cond/branch_1_fun/ppermute | solution.py:815
  442.7 3.9 collective-permute-start.21
  454.3 6.8 %copy-start.1 = (f32[16,64,512]{2,1,0:T(8,128)S(1)}, f32[16,64,512]{2,1,0:T(8,128)}, u32[]{:S(2)}) copy-start(f32[16,64,512]{2,1,0:T(8,128)} %copy-done) | copy-start | bytes 6291460
Sparse Core Ops, SparseCore 0:
  253.8 46.1 reduce-scatter.1
  326.7 73.8 all-reduce.1
  417.4 36.8 all-gather.1

commit v4 on v3

--- a/solution.py
+++ b/solution.py
@@ -394,7 +394,7 @@
     return [values[:, at : at + 128] for at in range(0, values.shape[1], 128)]
 
 
-def ffn_backward_kernel(steps, fused, info, *refs):
+def ffn_backward_kernel(steps, fused, part, info, *refs):
     step = pl.program_id(0)
     core = info[0]
     refs = list(refs)
@@ -404,18 +404,20 @@
         grad, late_gain, late_bias = first_norm_backward(core, flat(x), du_kept, du_sent, dh_kept, dh_taken, next_gains)
         refs = refs[12:]
     else:
-        grad = picked(info, step, steps, refs[6:9])
-        refs = refs[9:]
-    keep, send, *packed, up_grad, down_grad, small = refs
-    if not fused:
-        out, lined, sem, up_grad, down_grad, small = packed + [up_grad, down_grad, small]
-    kept_grads, sent_grads = packed if fused else (lined.at[0], lined.at[1])
+        grad = flat(refs[6]) if part else jnp.where(info[2] == 1, flat(refs[6]), flat(refs[7]))
+        refs = refs[7:] if part else refs[8:]
+    if fused:
+        keep, send, kept_grads, sent_grads, up_grad, down_grad, small = refs
+    elif part == 0:
+        keep, send, up_grad, down_grad, small = refs
+    else:
+        *started, _, _, keep, send, out, lined, sem, up_grad, down_grad, small = refs
+        kept_grads, sent_grads = lined.at[0], lined.at[1]
 
     @pl.when(step == 0)
     def _():
-        up_grad[...] = jnp.zeros_like(up_grad)
-        down_grad[...] = jnp.zeros_like(down_grad)
-        small[...] = jnp.zeros_like(small)
+        for index, total in enumerate((up_grad, down_grad, small)):
+            total[...] = started[index][...] if part else jnp.zeros_like(total)
 
     unit, scale = normalise(flat(mixed))
     normed = unit * gains[1:2] + biases[1:2]
@@ -432,6 +434,8 @@
         small[4:5] += late_gain
         small[5:6] += late_bias
     parted(core, grad + norm_backward(outer, unit, scale, gains[1:2]), keep, send)
+    if part == 0 and not fused:
+        return
 
     @pl.when(step == steps - 1)
     def _():
@@ -464,7 +468,7 @@
     put_pieces(step, steps, (first_out, second_out), result)
 
 
-def call(kernel, grid, in_specs, out_specs, out_shapes, scratch, flops, moved, name, vmem=56, aliases=None):
+def call(kernel, grid, in_specs, out_specs, out_shapes, scratch, flops, moved, name, vmem=30, aliases=None):
     return pl.pallas_call(
         kernel,
         grid_spec=pltpu.PrefetchScalarGridSpec(
@@ -597,7 +601,7 @@
         0,
         0,
         f"spectral_backward_{layer}",
-        56,
+        30,
         aliases,
     )(*args)
 
@@ -632,43 +636,52 @@
     )(info, *args)
 
 
-def ffn_backward(plan, layer, info, mixed, before, gains, biases, up, down, grads, rows=None):
+def ffn_backward(plan, layer, info, mixed, before, gains, biases, up, down, grads, part=0, started=(), rows=None):
     width, hidden = plan.width, plan.hidden
-    fused = len(grads) == 5
-    lined = (width // 128, hidden + SMALL_ROWS, 128)
-    scratch = [pltpu.VMEM(shape, F32) for shape in ((width, hidden), (hidden, width), (8, width))]
-    if fused:
-        packed, packed_specs = [lined, lined], [plan.whole(lined)] * 2
-    else:
-        packed, packed_specs = [(rows, 128)], [pl.BlockSpec(memory_space=pl.ANY)]
-        scratch = [pltpu.VMEM((2, *lined), F32), pltpu.SemaphoreType.DMA] + scratch
-    specs = [plan.row, plan.wide_row, plan.norm(layer), plan.norm(layer)]
+    fused = layer == 0
+    steps = plan.steps if fused else plan.steps // 2
+    start = part * steps
+    anywhere = pl.BlockSpec(memory_space=pl.ANY)
+
+    def shifted_rows(spec, lanes):
+        return pl.BlockSpec((ROWS, GRID, lanes), lambda j, s: spec.index_map(j + start, s))
+
+    specs = [shifted_rows(plan.row, width), shifted_rows(plan.wide_row, hidden), plan.norm(layer), plan.norm(layer)]
     specs += [plan.matrix(layer, width, hidden), plan.matrix(layer, hidden, width)]
-    args = [mixed, before, gains, biases, up, down, *grads]
+    args = [info, mixed, before, gains, biases, up, down, *grads]
     if fused:
         specs += [plan.row] + [plan.half_row] * 4 + [plan.norm(layer + 1)]
         args += [gains]
     else:
-        specs += plan.pieces
+        specs += [plan.row] if part else plan.pieces[:2]
+    lined = (width // 128, hidden + SMALL_ROWS, 128)
+    totals = ((width, hidden), (hidden, width), (8, width))
+    scratch = [pltpu.VMEM(shape, F32) for shape in totals]
+    aliases = None
+    if fused:
+        packed, packed_specs = [lined, lined], [plan.whole(lined)] * 2
+    elif part == 0:
+        packed, packed_specs, scratch = totals, [plan.whole(shape) for shape in totals], []
+    else:
+        packed, packed_specs = [(rows, 128)], [anywhere]
+        scratch = [pltpu.VMEM((2, *lined), F32), pltpu.SemaphoreType.DMA] + scratch
+        keep, send, *begun = started
+        specs += [plan.whole(shape) for shape in totals] + [anywhere] * 2
+        args += [*begun, keep, send]
+        aliases = {len(args) - 2: 0, len(args) - 1: 1}
     return call(
-        functools.partial(ffn_backward_kernel, plan.steps, fused),
-        plan.steps,
+        functools.partial(ffn_backward_kernel, steps, fused, part),
+        steps,
         specs,
-        [
-            plan.half_row,
-            plan.half_row,
-            *packed_specs,
-        ],
-        [
-            plan.half_shape,
-            plan.half_shape,
-            *[jax.ShapeDtypeStruct(shape, F32) for shape in packed],
-        ],
+        [shifted_rows(plan.half_row, width // 2)] * 2 + packed_specs,
+        [plan.half_shape, plan.half_shape] + [jax.ShapeDtypeStruct(shape, F32) for shape in packed],
         scratch,
         3 * 8 * 2048 * width * hidden,
         24 * 2**20,
-        f"ffn_backward_{layer}",
-    )(info, *args)
+        f"ffn_backward_{layer}_{part}",
+        30,
+        aliases,
+    )(*args)
 
 
 def input_gradient(plan, info, pieces, du, dh, gains):
@@ -968,9 +981,9 @@
         u1, a1, va, vb = ffn_forward(plan, 1, False, info, (x1,), keep, swap(send), *ffn_args)
         return (va, vb), (saved0, u0, a0, x1, saved1, u1, a1)
 
-    def backward(x, grads, saved):
+    def backward(x, grads, started, saved):
         saved0, u0, a0, x1, saved1, u1, a1 = saved
-        keep, send, packed = ffn_backward(plan, 1, info, u1, a1, *back_args, grads, second_rows)
+        keep, send, packed = ffn_backward(plan, 1, info, u1, a1, *back_args, grads, 1, started, second_rows)
         dh_keep, dh_send, packed = spectral_backward(
             plan, 1, info, keep, swap(send), mix_weight, saved1, tables, packed, matrix_rows
         )
@@ -1014,9 +1027,10 @@
     picked_grads = pick(info, out_grad, 0), pick(info, out_grad, 1)
     grads = (out_grad, *send_both(passed(picked_grads, x[1:]), routes))
     results, saved = as_one(forward, x)
-    results = passed(results, grads[1:])
+    started = ffn_backward(plan, 1, info, *saved[-2:], *back_args, grads[:2])
+    results = passed(results, [grads[2], started[-1]])
     outputs = (results[0], *send_both(results, back_routes))
-    (dxa, dxb), local, second = as_one(backward, x, grads, saved)
+    (dxa, dxb), local, second = as_one(backward, x, grads[2:], started, saved)
     [dxa] = passed([dxa], outputs[1:])
     returned = send_piece(dxa, back_routes[0])
     first, outputs, second = as_one(reduce_gradients, local, second, outputs)

time: 474 us -> 458 us (0.966)
  Pallas kernels: 184 us -> 172 us
    pallas_call x2 -> x3, Pallas kernels: 53.6 us -> 56.1 us  [ffn_backward(): call(functools.partial(ffn_backward_kernel, steps, fused, part), steps, s...]
  transfers between devices with their start and end apart: 33 -> 33, of which waited for: 24 -> 23; matrix products, arithmetic and copies ran while one was open for 4% -> 4% of each run, Pallas kernels for 38% -> 37%
where the time goes in v4:
time: 458 us; the launch traced here: 457 us
  Pallas kernels  172 us (38%)
  waiting for transfers between devices  164 us (36%)
  starting transfers between devices  80.6 us (18%)
  local copies, waits for them, and re-layouts  19.4 us (4%)
  between operations  13.9 us (3%)
  other arithmetic  6.72 us (1%)
    ppermute x10, starting transfers between devices, swap(): lax.ppermute(values, 'wide', [(i, i ^ 1) for i in range(lax.axis_size('wi...  57.9 us
    pallas_call x3, Pallas kernels, ffn_backward(): call(functools.partial(ffn_backward_kernel, steps, fused, part), steps, s...  56.1 us
    ppermute x6, waiting for transfers between devices, sum_spread(): total = total + lax.ppermute(part, axis, partners(axis, bit, offset))  49 us
    ppermute x8, waiting for transfers between devices, send_piece(): return lax.ppermute(piece, BOTH, route)  42.6 us
    ppermute x10, waiting for transfers between devices, swap(): lax.ppermute(values, 'wide', [(i, i ^ 1) for i in range(lax.axis_size('wi...  37.3 us
    pallas_call x2, Pallas kernels, spectral_backward(): call(functools.partial(spectral_backward_kernel, start), 2, specs, out_sp...  28.3 us
    ppermute x6, waiting for transfers between devices, collect(): lax.ppermute(values, axis, partners(axis, bit, offset))  26.5 us
    pallas_call x2, Pallas kernels, spectral_forward(): call(spectral_forward_kernel, 2, [cells, cells, weight, offset, table, ta...  26.4 us
  transfers between devices with their start and end apart: 33, of which 23 were waited for; matrix products, arithmetic and copies ran while one was open for 4% of the time, Pallas kernels for 37%

profile of v4, /device:TPU:0, one launch (start us, length us, event | category | flops | bytes accessed | tf_op | source)
XLA Modules:
  0.0 457.0 jit_solution(6025063116347268556)
XLA Ops:
  7.3 2.5 pick.4
  11.4 3.1 collective-permute-start.23
  16.6 1.4 copy-done.5
  18.0 42.6 %collective-permute-done.23.refs_3_ = f32[16,64,512]{2,1,0:T(8,128)} collective-permute-done((f32[16,64,512]{2,1,0:T(8,128)S(1)}, f32[16,64,512]{2,1,0:T(8,128)}, u32[]{:S(2)}, u32[]{:S(2)}) %collective-permute-start.23) | collective-permute-done | bytes 2097184 | tf_op jit(solution)/shard_map/ppermute | solution.py:753
  61.4 1.8 collective-permute-start.24
  63.2 122.9 %conditional.7 = (f32[16,64,512]{2,1,0:T(8,128)}, f32[16,64,512]{2,1,0:T(8,128)}, f32[2,1024,256]{2,1,0:T(8,128)}, f32[2,1024,256]{2,1,0:T(8,128)}, f32[2,1024,2...) conditional(s32[]{:T(128)} %convert_element_type.16, () %tuple.66, ...), branch_computations={%region_0.1_spmd, %region_1.2_spmd} | conditional | flops 24884901888 | bytes 172229056 | solution.py:794
  63.2 5.1 %first_norm.1 = (f32[32,64,256]{2,1,0:T(8,128)S(1)}, f32[32,64,256]{2,1,0:T(8,128)S(1)}) custom-call(s32[3]{0:T(128)S(1)} %get-tuple-element.169.info, f32[2,16,64,512]{3,2,1,0:T(8,128)} %get-tuple-element.170.own.refs_0_, f32[16,64,512]{2,1,0:T(8,128)} %get-tuple-element.171.a.refs_1_, f32[16,64,512]{2,1,0:T(8,128)} %get-tuple-element.172.b.refs_2_, ...), custom_call_target="tpu_custom_call" | custom-call | bytes 8388608 | tf_op jit(solution)/shard_map/cond/branch_1_fun/first_norm/pallas_call | solution.py:528
  68.4 49.2 %collective-permute-start = (f32[32,64,256]{2,1,0:T(8,128)S(1)}, f32[32,64,256]{2,1,0:T(8,128)S(1)}, u32[]{:S(2)}, u32[]{:S(2)}) collective-permute-start(f32[32,64,256]{2,1,0:T(8,128)S(1)} %get-tuple-element.176), channel_id=1, source_target_pairs={{0,4},{4,0},{8,12},{12,8},{16,20},{20,16},{24,28},{28,24},{1,5},{5... | collective-permute-start | bytes 6291464 | tf_op jit(solution)/shard_map/cond/branch_1_fun/ppermute | solution.py:798
  117.5 3.8 collective-permute-done.recv
  121.4 13.2 %spectral_forward_0.1 = (f32[32,64,256]{2,1,0:T(8,128)S(1)}, f32[32,64,256]{2,1,0:T(8,128)S(1)}, f32[2,1024,256]{2,1,0:T(8,128)}, f32[2,1024,256]{2,1,0:T(8,128)}, f32[2,1024,256]{2,1,0:T(8,128)}) custom-call(s32[3]{0:T(128)S(1)} %get-tuple-element.169.info, f32[32,64,256]{2,1,0:T(8,128)S(1)} %get-tuple-element.175.own, ...), custom_call_target="tpu_custom_call" | custom-call | flops 6000000000 | bytes 14680064 | tf_op jit(solution)/shard_map/cond/branch_1_fun/spectral_forward_0/pallas_call | solution.py:557
  135.0 3.8 collective-permute-done.1.refs_4_
  138.8 13.1 %ffn_forward_0.1 = (f32[32,64,512]{2,1,0:T(8,128)}, f32[32,64,512]{2,1,0:T(8,128)}, f32[32,64,512]{2,1,0:T(8,128)}, f32[32,64,256]{2,1,0:T(8,128)S(1)}, f32[32,64,256]{2,1,0:T(8,128)S(1)}) custom-call(s32[3]{0:T(128)S(1)} %get-tuple-element.169.info, f32[2,16,64,512]{3,2,1,0:T(8,128)S(1)} %copy-done.9, f32[16,64,512]{2,1,0:T(8,128)S(1)} %copy-done.12, ...), custom_call_target="tpu_custom_call" | custom-call | flops 6442450944 | bytes 25165824 | tf_op jit(solution)/shard_map/cond/branch_1_fun/ffn_forward_0/pallas_call | solution.py:626
  152.3 3.8 collective-permute-done.2.recv
  156.0 13.2 %spectral_forward_1.1 = (f32[32,64,256]{2,1,0:T(8,128)S(1)}, f32[32,64,256]{2,1,0:T(8,128)S(1)}, f32[2,1024,256]{2,1,0:T(8,128)}, f32[2,1024,256]{2,1,0:T(8,128)}, f32[2,1024,256]{2,1,0:T(8,128)}) custom-call(s32[3]{0:T(128)S(1)} %get-tuple-element.169.info, f32[32,64,256]{2,1,0:T(8,128)S(1)} %get-tuple-element.188.own, ...), custom_call_target="tpu_custom_call" | custom-call | flops 6000000000 | bytes 14680064 | tf_op jit(solution)/shard_map/cond/branch_1_fun/spectral_forward_1/pallas_call | solution.py:557
  169.6 3.8 collective-permute-done.3.refs_2_
  173.4 12.7 %ffn_forward_1.1 = (f32[32,64,512]{2,1,0:T(8,128)S(1)}, f32[32,64,512]{2,1,0:T(8,128)S(1)}, f32[16,64,512]{2,1,0:T(8,128)}, f32[16,64,512]{2,1,0:T(8,128)}) custom-call(s32[3]{0:T(128)S(1)} %get-tuple-element.169.info, f32[32,64,512]{2,1,0:T(8,128)} %get-tuple-element.460.refs_0_, f32[32,64,256]{2,1,0:T(8,128)S(1)} %get-tuple-element.190.refs_1_, ...), custom_call_target="tpu_custom_call" | custom-call | flops 6442450944 | bytes 25165824 | tf_op jit(solution)/shard_map/cond/branch_1_fun/ffn_forward_1/pallas_call | solution.py:626
  186.1 5.1 %copy-done.1 = f32[2,16,64,512]{3,2,1,0:T(8,128)S(1)} copy-done((f32[2,16,64,512]{3,2,1,0:T(8,128)S(1)}, f32[2,16,64,512]{3,2,1,0:T(8,128)}, u32[]{:S(2)}) %copy-start.1) | copy-done | bytes 4194328
  191.2 12.4 %ffn_backward_1_0.1 = (f32[32,64,256]{2,1,0:T(8,128)}, f32[32,64,256]{2,1,0:T(8,128)}, f32[512,512]{1,0:T(8,128)S(1)}, f32[512,512]{1,0:T(8,128)}, f32[8,512]{1,0:T(8,128)S(1)}) custom-call(s32[3]{0:T(128)S(1)} %pad_add_fusion.info, f32[32,64,512]{2,1,0:T(8,128)S(1)} %get-tuple-element.356.refs_0_, f32[32,64,512]{2,1,0:T(8,128)S(1)} %get-tuple-element.357.refs_1_, ...), custom_call_target="tpu_custom_call" | custom-call | flops 12884901888 | bytes 25165824 | tf_op jit(solution)/shard_map/ffn_backward_1_0/pallas_call | solution.py:672
  203.7 2.2 collective-permute-start.26
  206.1 99.4 %conditional.8 = (f32[16,64,512]{2,1,0:T(8,128)}, f32[16,64,512]{2,1,0:T(8,128)}, f32[4,544,128]{2,1,0:T(8,128)}, f32[4,544,128]{2,1,0:T(8,128)}, f32[2,2,2,128,...) conditional(s32[]{:T(128)} %convert_element_type.16, () %tuple.65, ...), branch_computations={%region_2.3_spmd, %region_3.7_spmd} | conditional | flops 25769803776 | bytes 213091216 | solution.py:794
  206.2 15.3 %ffn_backward_1_1.1 = (f32[32,64,256]{2,1,0:T(8,128)S(1)}, f32[32,64,256]{2,1,0:T(8,128)}, f32[6656,128]{1,0:T(8,128)}) custom-call(s32[3]{0:T(128)S(1)} %get-tuple-element.236.info, f32[32,64,512]{2,1,0:T(8,128)} %get-tuple-element.244.refs_0_, f32[32,64,512]{2,1,0:T(8,128)} %get-tuple-element.245.refs_1_, ...), custom_call_target="tpu_custom_call", output_to_operand_aliasing={{0}: (11, {}), {1}: (12, {})} | custom-call | flops 12884901888 | bytes 25165824 | tf_op jit(solution)/shard_map/cond/branch_1_fun/ffn_backward_1_1/pallas_call | solution.py:672
  221.5 3.4 collective-permute-start.6
  224.9 4.0 collective-permute-done.6.recv
  228.9 14.6 %spectral_backward_1.1 = (f32[32,64,256]{2,1,0:T(8,128)}, f32[32,64,256]{2,1,0:T(8,128)S(1)}, f32[6656,128]{1,0:T(8,128)}) custom-call(s32[3]{0:T(128)S(1)} %get-tuple-element.236.info, f32[32,64,256]{2,1,0:T(8,128)} %copy-done.27, f32[32,64,256]{2,1,0:T(8,128)S(1)} %collective-permute-done.6.recv, ...), custom_call_target="tpu_custom_call", output_to_operand_aliasing={{2}: (9, {})} | custom-call | tf_op jit(solution)/shard_map/cond/branch_1_fun/spectral_backward_1/pallas_call | solution.py:594
  244.0 3.9 collective-permute-done.7
  247.9 57.6 %conditional = (f32[16,64,512]{2,1,0:T(8,128)}, f32[16,64,512]{2,1,0:T(8,128)}, f32[4,544,128]{2,1,0:T(8,128)}, f32[4,544,128]{2,1,0:T(8,128)}, f32[2,2,2,128,12...) conditional(s32[]{:T(128)} %convert_element_type.3, () %tuple.40, (s32[3]{0:T(128)S(1)}, ...), branch_computations={%region_4.4_spmd, %region_5.5_spmd} | conditional | flops 12884901888 | bytes 117440824 | solution.py:794
  248.0 28.4 %ffn_backward_0_0.1 = (f32[32,64,256]{2,1,0:T(8,128)S(1)}, f32[32,64,256]{2,1,0:T(8,128)S(1)}, f32[4,544,128]{2,1,0:T(8,128)}, f32[4,544,128]{2,1,0:T(8,128)}) custom-call(s32[3]{0:T(128)S(1)} %get-tuple-element.204.info, f32[32,64,512]{2,1,0:T(8,128)} %get-tuple-element.208.refs_0_, f32[32,64,512]{2,1,0:T(8,128)} %get-tuple-element.209.refs_1_, ...), custom_call_target="tpu_custom_call" | custom-call | flops 12884901888 | bytes 25165824 | tf_op jit(solution)/shard_map/cond/branch_1_fun/cond/branch_1_fun/ffn_backward_0_0/pallas_call | solution.py:672
  276.7 3.8 collective-permute-done.4.recv
  280.5 13.6 %spectral_backward_0.1 = (f32[32,64,256]{2,1,0:T(8,128)S(1)}, f32[32,64,256]{2,1,0:T(8,128)S(1)}, f32[2,2,2,128,128]{4,3,2,1,0:T(8,128)}, f32[2,8,128]{2,1,0:T(8,128)}) custom-call(s32[3]{0:T(128)S(1)} %get-tuple-element.204.info, f32[32,64,256]{2,1,0:T(8,128)S(1)} %get-tuple-element.219.own.du_kept, f32[32,64,256]{2,1,0:T(8,128)S(1)} %collective-permute-done.4.recv, ...), custom_call_target="tpu_custom_call" | custom-call | tf_op jit(solution)/shard_map/cond/branch_1_fun/cond/branch_1_fun/spectral_backward_0/pallas_call | solution.py:594
  294.5 3.8 collective-permute-done.5.dh_taken
  298.3 7.2 %input_gradient.1 = (f32[16,64,512]{2,1,0:T(8,128)}, f32[16,64,512]{2,1,0:T(8,128)}, f32[8,512]{1,0:T(8,128)}) custom-call(s32[3]{0:T(128)S(1)} %get-tuple-element.204.info, f32[2,16,64,512]{3,2,1,0:T(8,128)S(1)} %copy-done.10, f32[16,64,512]{2,1,0:T(8,128)S(1)} %copy-done.13, f32[16,64,512]{2,1,0:T(8,128)} %get-tuple-element.207.b, ...), custom_call_target="tpu_custom_call" | custom-call | bytes 16777216 | tf_op jit(solution)/shard_map/cond/branch_1_fun/cond/branch_1_fun/input_gradient/pallas_call | solution.py:688
  306.3 91.8 %conditional.9 = (f32[832,128]{1,0:T(8,128)}, f32[2,16,64,512]{3,2,1,0:T(8,128)}, f32[832,128]{1,0:T(8,128)}) conditional(s32[]{:T(128)} %convert_element_type.16, () %tuple.64, (f32[4,544,128]{2,1,0:T(8,128)}, f32[4,544,128]{2,1,0:T(8,128)}, f32[2,2,2,128,128]{4,3,2,1,0:T(8,128)}, f32[2,8,128]{2,1,0:T(8,128)}, f32[8,512]{1,0:T(8,128)}, ...), branch_computations={%region_7.8_spmd, %region_8.12_spmd} | conditional | flops 890966 | bytes 38856152 | solution.py:794
  307.1 91.0 %conditional.1 = (f32[832,128]{1,0:T(8,128)}, f32[2,16,64,512]{3,2,1,0:T(8,128)}) conditional(s32[]{:T(128)} %convert_element_type.5, () %tuple.46, (f32[4,544,128]{2,1,0:T(8,128)}, f32[4,544,128]{2,1,0:T(8,128)}, f32[2,2,2,128,128]{4,3,2,1,0:T(8,128)}, f32[2,8,128]{2,1,0:T(8,128)}, f32[8,512]{1,0:T(8,128)}, /*index=5*/s32[3]{0:T(128)S(1)}, ...), branch_computations={%region_9.9_spmd, %region_10.10_spmd} | conditional | flops 784465 | bytes 36300064 | solution.py:794
  307.1 3.2 collective-permute-start.8
  310.3 2.6 collective-permute-done.8
  312.8 1.4 add.84
  314.4 1.6 collective-permute-start.9
  320.3 1.5 collective-permute-start.11
  321.8 4.9 %collective-permute-done.9 = f32[832,128]{1,0:T(8,128)} collective-permute-done((f32[832,128]{1,0:T(8,128)S(1)}, f32[832,128]{1,0:T(8,128)}, u32[]{:S(2)}, u32[]{:S(2)}) %collective-permute-start.9) | collective-permute-done | bytes 426016 | tf_op jit(solution)/shard_map/cond/branch_1_fun/cond/branch_1_fun/ppermute | solution.py:820
  327.8 1.6 collective-permute-start.10
  329.3 3.9 collective-permute-done.11
  335.0 1.8 collective-permute-done.10
  336.8 3.5 collective-permute-done.12
  340.6 3.5 join_0.2.refs_1_
  344.1 3.2 join_1.2.refs_1_
  347.3 20.8 %collective-permute-done.13 = f32[416,128]{1,0:T(8,128)S(1)} collective-permute-done((f32[416,128]{1,0:T(8,128)S(1)}, f32[416,128]{1,0:T(8,128)S(1)}, u32[]{:S(2)}, u32[]{:S(2)}) %collective-permute-start.13) | collective-permute-done | bytes 213024 | tf_op jit(solution)/shard_map/cond/branch_1_fun/cond/branch_1_fun/ppermute | solution.py:820
  369.7 14.1 %collective-permute-done.14 = f32[208,128]{1,0:T(8,128)S(1)} collective-permute-done((f32[208,128]{1,0:T(8,128)S(1)}, f32[208,128]{1,0:T(8,128)S(1)}, u32[]{:S(2)}, u32[]{:S(2)}) %collective-permute-start.14) | collective-permute-done | bytes 106528 | tf_op jit(solution)/shard_map/cond/branch_1_fun/cond/branch_1_fun/ppermute | solution.py:820
  384.8 6.0 %collective-permute-done.15 = f32[208,128]{1,0:T(8,128)S(1)} collective-permute-done((f32[208,128]{1,0:T(8,128)S(1)}, f32[208,128]{1,0:T(8,128)S(1)}, u32[]{:S(2)}, u32[]{:S(2)}) %collective-permute-start.15) | collective-permute-done | bytes 106528 | tf_op jit(solution)/shard_map/cond/branch_1_fun/cond/branch_1_fun/ppermute | solution.py:828
  392.4 5.0 %collective-permute-done.16 = f32[416,128]{1,0:T(8,128)S(1)} collective-permute-done((f32[416,128]{1,0:T(8,128)S(1)}, f32[416,128]{1,0:T(8,128)S(1)}, u32[]{:S(2)}, u32[]{:S(2)}) %collective-permute-start.16) | collective-permute-done | bytes 213024 | tf_op jit(solution)/shard_map/cond/branch_1_fun/cond/branch_1_fun/ppermute | solution.py:828
  399.7 38.7 %conditional.10 = (f32[3328,128]{1,0:T(8,128)}, f32[3328,128]{1,0:T(8,128)}, f32[6656,128]{1,0:T(8,128)}) conditional(s32[]{:T(128)} %convert_element_type.16, () %tuple.70, (f32[832,128]{1,0:T(8,128)}, f32[832,128]{1,0:T(8,128)}) %tuple.71), branch_computations={%region_12.13_spmd, %region_13.16_spmd} | conditional | flops 426030 | bytes 35357480 | solution.py:794
  400.5 31.3 %conditional.2 = (f32[3328,128]{1,0:T(8,128)}, f32[3328,128]{1,0:T(8,128)}) conditional(s32[]{:T(128)} %convert_element_type.8, () %tuple.52, f32[832,128]{1,0:T(8,128)} %get-tuple-element.298), branch_computations={%region_14.14_spmd, %region_15.15_spmd} | conditional | flops 426025 | bytes 23855802 | solution.py:794
  401.5 1.7 collective-permute-start.17
  403.2 1.9 collective-permute-start.19
  407.1 1.9 collective-permute-done.17
  408.9 2.1 collective-permute-start.18
  411.1 1.5 collective-permute-start.20
  412.8 12.1 %collective-permute-done.18 = f32[832,128]{1,0:T(8,128)S(1)} collective-permute-done((f32[832,128]{1,0:T(8,128)S(1)}, f32[832,128]{1,0:T(8,128)S(1)}, u32[]{:S(2)}, u32[]{:S(2)}) %collective-permute-start.18) | collective-permute-done | bytes 426016 | tf_op jit(solution)/shard_map/cond/branch_1_fun/cond/branch_1_fun/ppermute | solution.py:828
  424.9 1.5 collective-permute-done.20
  426.4 1.4 pad_maximum_fusion.1
  427.8 3.9 collective-permute-done.21
  431.7 6.8 %all-gather.2.cloned.1.call-done = f32[6656,128]{1,0:T(8,128)} async-done(((f32[832,128]{1,0:T(8,128)}), f32[6656,128]{1,0:T(8,128)}) %all-gather.2.cloned.1.call-update) | async-done | bytes 3407888 | tf_op jit(solution)/shard_map/cond/branch_1_fun/all_gather | solution.py:1020
  438.5 6.8 %unpack.1 = (f32[2,2,512]{2,1,0:T(2,128)}, f32[2,2,512]{2,1,0:T(2,128)}, f32[2,2,2,4,128,128]{5,4,3,2,1,0:T(8,128)}, f32[2,2,2,4,128]{4,3,2,1,0:T(4,128)}, f32[2...) custom-call(s32[3]{0:T(128)S(1)} %pad_add_fusion.info, ...), custom_call_target="tpu_custom_call" | custom-call | tf_op jit(solution)/shard_map/unpack/pallas_call | solution.py:930
  445.3 3.2 join_0.3.refs_1_
  448.5 1.9 join_1.3
  (152 shorter events, 26.7 us)
Async XLA Ops:
  9.7 4.8 %copy-start = (f32[2,16,64,512]{3,2,1,0:T(8,128)S(1)}, f32[2,16,64,512]{3,2,1,0:T(8,128)}, u32[]{:S(2)}) copy-start(f32[2,16,64,512]{3,2,1,0:T(8,128)} %refs_6_.1) | copy-start | bytes 12582916
  9.8 8.2 %collective-permute-start.22 = (f32[16,64,512]{2,1,0:T(8,128)S(1)}, f32[16,64,512]{2,1,0:T(8,128)S(1)}, u32[]{:S(2)}, u32[]{:S(2)}) collective-permute-start(f32[16,64,512]{2,1,0:T(8,128)S(1)} %pick.4), channel_id=1, source_target_pairs={{2,4},{3,5},{4,2},{5,3},{10,12},{11,13},{12,10},{13,11},{18,20},{1... | collective-permute-start | bytes 6291464 | tf_op jit(solution)/shard_map/ppermute | solution.py:753
  11.4 49.2 %collective-permute-start.23 = (f32[16,64,512]{2,1,0:T(8,128)S(1)}, f32[16,64,512]{2,1,0:T(8,128)}, u32[]{:S(2)}, u32[]{:S(2)}) collective-permute-start(f32[16,64,512]{2,1,0:T(8,128)S(1)} %pick.5), channel_id=1, source_target_pairs={{0,1},{1,0},{2,5},{3,4},{4,3},{5,2},{6,7},{7,6},{8,9},{9,8},{10,13... | collective-permute-start | bytes 6291464 | tf_op jit(solution)/shard_map/ppermute | solution.py:753
  17.9 45.2 %copy-start.30 = (f32[2,2,512]{2,1,0:T(2,128)S(1)}, f32[2,2,512]{2,1,0:T(2,128)}, u32[]{:S(2)}) copy-start(f32[2,2,512]{2,1,0:T(2,128)} %refs_2_.1) | copy-start | bytes 24580
  17.9 45.2 %copy-start.31 = (f32[2,2,512]{2,1,0:T(2,128)S(1)}, f32[2,2,512]{2,1,0:T(2,128)}, u32[]{:S(2)}) copy-start(f32[2,2,512]{2,1,0:T(2,128)} %refs_3_.1) | copy-start | bytes 24580
  18.0 45.2 %copy-start.34 = (f32[2,2,2,4,128]{4,3,2,1,0:T(4,128)S(1)}, f32[2,2,2,4,128]{4,3,2,1,0:T(4,128)}, u32[]{:S(2)}) copy-start(f32[2,2,2,4,128]{4,3,2,1,0:T(4,128)} %param.32) | copy-start | bytes 49156
  18.0 45.2 %copy-start.35 = (f32[2,512]{1,0:T(2,128)S(1)}, f32[2,512]{1,0:T(2,128)}, u32[]{:S(2)}) copy-start(f32[2,512]{1,0:T(2,128)} %param.34) | copy-start | bytes 12292
  18.0 45.2 %copy-start.36 = (f32[2,512]{1,0:T(2,128)S(1)}, f32[2,512]{1,0:T(2,128)}, u32[]{:S(2)}) copy-start(f32[2,512]{1,0:T(2,128)} %param.36) | copy-start | bytes 12292
  18.0 42.6 %copy-start.11 = (f32[16,64,512]{2,1,0:T(8,128)}, f32[16,64,512]{2,1,0:T(8,128)S(1)}, u32[]{:S(2)}) copy-start(f32[16,64,512]{2,1,0:T(8,128)S(1)} %collective-permute-done.22.refs_2_) | copy-start | bytes 6291460
  60.6 125.5 %collective-permute-start.25 = (f32[16,64,512]{2,1,0:T(8,128)}, f32[16,64,512]{2,1,0:T(8,128)S(1)}, u32[]{:S(2)}, u32[]{:S(2)}) collective-permute-start(f32[16,64,512]{2,1,0:T(8,128)} %get-tuple-element.359), channel_id=1, source_target_pairs={{2,4},{3,5},{4,2},{5,3},{10,12},{11,13},{12,10},{13,11},{18,20},{1... | collective-permute-start | bytes 6291464 | tf_op jit(solution)/shard_map/ppermute | solution.py:753
  61.4 142.3 %collective-permute-start.24 = (f32[16,64,512]{2,1,0:T(8,128)}, f32[16,64,512]{2,1,0:T(8,128)}, u32[]{:S(2)}, u32[]{:S(2)}) collective-permute-start(f32[16,64,512]{2,1,0:T(8,128)} %get-tuple-element.358), channel_id=1, source_target_pairs={{0,1},{1,0},{2,5},{3,4},{4,3},{5,2},{6,7},{7,6},{8,9},{9,8},{10,13... | collective-permute-start | bytes 6291464 | tf_op jit(solution)/shard_map/ppermute | solution.py:753
  63.2 58.1 %copy-start.6 = (bf16[64,256]{1,0:T(8,128)(2,1)S(1)}, bf16[64,256]{1,0:T(8,128)(2,1)}, u32[]{:S(2)}) copy-start(bf16[64,256]{1,0:T(8,128)(2,1)} %constant.234.clone.1.table_in) | copy-start | bytes 98308 | tf_op jit(solution)/shard_map/cond
  63.2 58.1 %copy-start.7 = (bf16[64,256]{1,0:T(8,128)(2,1)S(1)}, bf16[64,256]{1,0:T(8,128)(2,1)}, u32[]{:S(2)}) copy-start(bf16[64,256]{1,0:T(8,128)(2,1)} %constant.237.clone.1.table_out) | copy-start | bytes 98308 | tf_op jit(solution)/shard_map/cond
  63.2 58.1 %copy-start.14 = (f32[2,2,2,4,128,128]{5,4,3,2,1,0:T(8,128)S(1)}, f32[2,2,2,4,128,128]{5,4,3,2,1,0:T(8,128)}, u32[]{:S(2)}) copy-start(f32[2,2,2,4,128,128]{5,4,3,2,1,0:T(8,128)} %get-tuple-element.177.weight) | copy-start | bytes 6291460 | tf_op jit(solution)/shard_map/cond
  68.4 53.0 %collective-permute-start = (f32[32,64,256]{2,1,0:T(8,128)S(1)}, f32[32,64,256]{2,1,0:T(8,128)S(1)}, u32[]{:S(2)}, u32[]{:S(2)}) collective-permute-start(f32[32,64,256]{2,1,0:T(8,128)S(1)} %get-tuple-element.176), channel_id=1, source_target_pairs={{0,4},{4,0},{8,12},{12,8},{16,20},{20,16},{24,28},{28,24},{1,5},{5... | collective-permute-start | bytes 6291464 | tf_op jit(solution)/shard_map/cond/branch_1_fun/ppermute | solution.py:798
  121.3 17.4 %copy-start.9 = (f32[2,16,64,512]{3,2,1,0:T(8,128)S(1)}, f32[2,16,64,512]{3,2,1,0:T(8,128)}, u32[]{:S(2)}) copy-start(f32[2,16,64,512]{3,2,1,0:T(8,128)} %get-tuple-element.170.own.refs_0_) | copy-start | bytes 12582916 | tf_op jit(solution)/shard_map/cond
  121.3 17.4 %copy-start.12 = (f32[16,64,512]{2,1,0:T(8,128)S(1)}, f32[16,64,512]{2,1,0:T(8,128)}, u32[]{:S(2)}) copy-start(f32[16,64,512]{2,1,0:T(8,128)} %get-tuple-element.171.a.refs_1_) | copy-start | bytes 6291460 | tf_op jit(solution)/shard_map/cond
  121.3 17.4 %copy-start.32 = (f32[2,512,512]{2,1,0:T(8,128)S(1)}, f32[2,512,512]{2,1,0:T(8,128)}, u32[]{:S(2)}) copy-start(f32[2,512,512]{2,1,0:T(8,128)} %get-tuple-element.183.refs_7_.refs_5_) | copy-start | bytes 6291460 | tf_op jit(solution)/shard_map/cond
  121.4 17.4 %copy-start.33 = (f32[2,512,512]{2,1,0:T(8,128)S(1)}, f32[2,512,512]{2,1,0:T(8,128)}, u32[]{:S(2)}) copy-start(f32[2,512,512]{2,1,0:T(8,128)} %get-tuple-element.185.refs_9_.refs_7_) | copy-start | bytes 6291460 | tf_op jit(solution)/shard_map/cond
  134.6 4.2 collective-permute-start.1
  151.9 4.2 collective-permute-start.2
  169.2 4.2 collective-permute-start.3
  186.1 17.5 %copy-start.23 = (f32[32,64,512]{2,1,0:T(8,128)}, f32[32,64,512]{2,1,0:T(8,128)S(1)}, u32[]{:S(2)}) copy-start(f32[32,64,512]{2,1,0:T(8,128)S(1)} %get-tuple-element.356.refs_0_) | copy-start | bytes 12582916
  186.1 17.5 %copy-start.24 = (f32[32,64,512]{2,1,0:T(8,128)}, f32[32,64,512]{2,1,0:T(8,128)S(1)}, u32[]{:S(2)}) copy-start(f32[32,64,512]{2,1,0:T(8,128)S(1)} %get-tuple-element.357.refs_1_) | copy-start | bytes 12582916
  186.1 5.1 %copy-start.1 = (f32[2,16,64,512]{3,2,1,0:T(8,128)S(1)}, f32[2,16,64,512]{3,2,1,0:T(8,128)}, u32[]{:S(2)}) copy-start(f32[2,16,64,512]{3,2,1,0:T(8,128)} %refs_6_.1) | copy-start | bytes 12582916
  203.7 101.8 %collective-permute-start.26 = (f32[16,64,512]{2,1,0:T(8,128)}, f32[16,64,512]{2,1,0:T(8,128)}, u32[]{:S(2)}, u32[]{:S(2)}) collective-permute-start(f32[16,64,512]{2,1,0:T(8,128)} %get-tuple-element.381), channel_id=1, source_target_pairs={{4,2},{5,3},{2,4},{3,5},{12,10},{13,11},{10,12},{11,13},{20,18},{2... | collective-permute-start | bytes 6291464 | tf_op jit(solution)/shard_map/ppermute | solution.py:753
  205.9 99.6 %collective-permute-start.27 = (f32[16,64,512]{2,1,0:T(8,128)}, f32[16,64,512]{2,1,0:T(8,128)}, u32[]{:S(2)}, u32[]{:S(2)}) collective-permute-start(f32[16,64,512]{2,1,0:T(8,128)} %get-tuple-element.382), channel_id=1, source_target_pairs={{1,0},{0,1},{5,2},{4,3},{3,4},{2,5},{7,6},{6,7},{9,8},{8,9},{13,10... | collective-permute-start | bytes 6291464 | tf_op jit(solution)/shard_map/ppermute | solution.py:753
  206.1 99.4 %reduce-scatter.2.cloned.1.call-start = ((), (), s32[]{:S(2)}) async-start(), calls=%async_computation.1 | async-start | bytes 3833856 | tf_op jit(solution)/shard_map/cond/branch_1_fun/reduce_scatter | solution.py:991
  206.1 22.8 %copy-start.15 = (f32[2,2,2,4,128,128]{5,4,3,2,1,0:T(8,128)S(1)}, f32[2,2,2,4,128,128]{5,4,3,2,1,0:T(8,128)}, u32[]{:S(2)}) copy-start(f32[2,2,2,4,128,128]{5,4,3,2,1,0:T(8,128)} %get-tuple-element.254.weight) | copy-start | bytes 6291460 | tf_op jit(solution)/shard_map/cond
  206.1 22.8 %copy-start.20 = (f32[2,1024,256]{2,1,0:T(8,128)S(1)}, f32[2,1024,256]{2,1,0:T(8,128)}, u32[]{:S(2)}) copy-start(f32[2,1024,256]{2,1,0:T(8,128)} %get-tuple-element.255.modes) | copy-start | bytes 6291460 | tf_op jit(solution)/shard_map/cond
  206.1 22.8 %copy-start.21 = (f32[2,1024,256]{2,1,0:T(8,128)S(1)}, f32[2,1024,256]{2,1,0:T(8,128)}, u32[]{:S(2)}) copy-start(f32[2,1024,256]{2,1,0:T(8,128)} %get-tuple-element.256.before) | copy-start | bytes 6291460 | tf_op jit(solution)/shard_map/cond
  206.1 22.8 %copy-start.22 = (f32[2,1024,256]{2,1,0:T(8,128)S(1)}, f32[2,1024,256]{2,1,0:T(8,128)}, u32[]{:S(2)}) copy-start(f32[2,1024,256]{2,1,0:T(8,128)} %get-tuple-element.257.after) | copy-start | bytes 6291460 | tf_op jit(solution)/shard_map/cond
  206.1 22.8 %copy-start.28 = (bf16[64,256]{1,0:T(8,128)(2,1)S(1)}, bf16[64,256]{1,0:T(8,128)(2,1)}, u32[]{:S(2)}) copy-start(bf16[64,256]{1,0:T(8,128)(2,1)} %constant.235.clone.1.table_in) | copy-start | bytes 98308 | tf_op jit(solution)/shard_map/cond
  206.1 22.8 %copy-start.29 = (bf16[64,256]{1,0:T(8,128)(2,1)S(1)}, bf16[64,256]{1,0:T(8,128)(2,1)}, u32[]{:S(2)}) copy-start(bf16[64,256]{1,0:T(8,128)(2,1)} %constant.236.clone.1.table_out) | copy-start | bytes 98308 | tf_op jit(solution)/shard_map/cond
  221.5 7.4 %copy-start.27 = (f32[32,64,256]{2,1,0:T(8,128)}, f32[32,64,256]{2,1,0:T(8,128)S(1)}, u32[]{:S(2)}) copy-start(f32[32,64,256]{2,1,0:T(8,128)S(1)} %get-tuple-element.252.own) | copy-start | bytes 6291460 | tf_op jit(solution)/shard_map/cond
  221.5 7.4 %collective-permute-start.6 = (f32[32,64,256]{2,1,0:T(8,128)}, f32[32,64,256]{2,1,0:T(8,128)S(1)}, u32[]{:S(2)}, u32[]{:S(2)}) collective-permute-start(f32[32,64,256]{2,1,0:T(8,128)} %get-tuple-element.253), channel_id=1, source_target_pairs={{0,4},{4,0},{8,12},{12,8},{16,20},{20,16},{24,28},{28,24},{1,5},{5... | collective-permute-start | bytes 6291464 | tf_op jit(solution)/shard_map/cond/branch_1_fun/ppermute | solution.py:798
  243.6 4.4 collective-permute-start.7
  247.9 32.5 %copy-start.16 = (f32[2,2,2,4,128,128]{5,4,3,2,1,0:T(8,128)S(1)}, f32[2,2,2,4,128,128]{5,4,3,2,1,0:T(8,128)}, u32[]{:S(2)}) copy-start(f32[2,2,2,4,128,128]{5,4,3,2,1,0:T(8,128)} %get-tuple-element.221.weight) | copy-start | bytes 6291460 | tf_op jit(solution)/shard_map/cond/branch_1_fun/cond
  247.9 32.5 %copy-start.17 = (f32[2,1024,256]{2,1,0:T(8,128)S(1)}, f32[2,1024,256]{2,1,0:T(8,128)}, u32[]{:S(2)}) copy-start(f32[2,1024,256]{2,1,0:T(8,128)} %get-tuple-element.222.modes) | copy-start | bytes 6291460 | tf_op jit(solution)/shard_map/cond/branch_1_fun/cond
  247.9 32.5 %copy-start.18 = (f32[2,1024,256]{2,1,0:T(8,128)S(1)}, f32[2,1024,256]{2,1,0:T(8,128)}, u32[]{:S(2)}) copy-start(f32[2,1024,256]{2,1,0:T(8,128)} %get-tuple-element.223.before) | copy-start | bytes 6291460 | tf_op jit(solution)/shard_map/cond/branch_1_fun/cond
  247.9 32.6 %copy-start.19 = (f32[2,1024,256]{2,1,0:T(8,128)S(1)}, f32[2,1024,256]{2,1,0:T(8,128)}, u32[]{:S(2)}) copy-start(f32[2,1024,256]{2,1,0:T(8,128)} %get-tuple-element.224.after) | copy-start | bytes 6291460 | tf_op jit(solution)/shard_map/cond/branch_1_fun/cond
  276.3 4.2 collective-permute-start.4
  280.5 17.8 %copy-start.10 = (f32[2,16,64,512]{3,2,1,0:T(8,128)S(1)}, f32[2,16,64,512]{3,2,1,0:T(8,128)}, u32[]{:S(2)}) copy-start(f32[2,16,64,512]{3,2,1,0:T(8,128)} %get-tuple-element.205.own) | copy-start | bytes 12582916 | tf_op jit(solution)/shard_map/cond/branch_1_fun/cond
  280.5 17.8 %copy-start.13 = (f32[16,64,512]{2,1,0:T(8,128)S(1)}, f32[16,64,512]{2,1,0:T(8,128)}, u32[]{:S(2)}) copy-start(f32[16,64,512]{2,1,0:T(8,128)} %get-tuple-element.206.a) | copy-start | bytes 6291460 | tf_op jit(solution)/shard_map/cond/branch_1_fun/cond
  294.2 4.2 collective-permute-start.5
  305.5 92.6 %collective-permute-start.28 = (f32[16,64,512]{2,1,0:T(8,128)}, f32[16,64,512]{2,1,0:T(8,128)S(1)}, u32[]{:S(2)}, u32[]{:S(2)}) collective-permute-start(f32[16,64,512]{2,1,0:T(8,128)} %passed.8.refs_0_), channel_id=1, source_target_pairs={{4,2},{5,3},{2,4},{3,5},{12,10},{13,11},{10,12},{11,13},{20,18},{2... | collective-permute-start | bytes 6291464 | tf_op jit(solution)/shard_map/ppermute | solution.py:753
  306.3 91.8 %all-reduce.2.cloned.1.call-start = ((), (), s32[]{:S(2)}) async-start(), calls=%async_computation.2 | async-start | bytes 851968 | tf_op jit(solution)/shard_map/cond/branch_1_fun/psum | solution.py:1012
  307.1 5.7 %collective-permute-start.8 = (f32[4,544,128]{2,1,0:T(8,128)}, f32[4,544,128]{2,1,0:T(8,128)S(1)}, u32[]{:S(2)}, u32[]{:S(2)}) collective-permute-start(f32[4,544,128]{2,1,0:T(8,128)} %get-tuple-element.278), channel_id=1, source_target_pairs={{0,4},{4,0},{8,12},{12,8},{16,20},{20,16},{24,28},{28,24},{1,5},{5... | collective-permute-start | bytes 3342344 | tf_op jit(solution)/shard_map/cond/branch_1_fun/cond/branch_1_fun/ppermute | solution.py:798
  314.4 12.3 %collective-permute-start.9 = (f32[832,128]{1,0:T(8,128)S(1)}, f32[832,128]{1,0:T(8,128)}, u32[]{:S(2)}, u32[]{:S(2)}) collective-permute-start(f32[832,128]{1,0:T(8,128)S(1)} %dynamic-slice_bitcast_fusion.1), channel_id=1, source_target_pairs={{0,8},{4,12},{8,0},{12,4},{16,24},{20,28},{24,16},{28,20},{1,9},{5... | collective-permute-start | bytes 1277960 | tf_op jit(solution)/shard_map/cond/branch_1_fun/cond/branch_1_fun/ppermute | solution.py:820
  320.3 13.0 %collective-permute-start.11 = (f32[832,128]{1,0:T(8,128)}, f32[832,128]{1,0:T(8,128)}, u32[]{:S(2)}, u32[]{:S(2)}) collective-permute-start(f32[832,128]{1,0:T(8,128)} %dynamic-slice_bitcast_fusion), channel_id=1, source_target_pairs={{0,16},{4,20},{8,24},{12,28},{16,0},{20,4},{24,8},{28,12},{1,17},{... | collective-permute-start | bytes 1277960 | tf_op jit(solution)/shard_map/cond/branch_1_fun/cond/branch_1_fun/ppermute | solution.py:820
  327.8 9.1 %collective-permute-start.10 = (f32[416,128]{1,0:T(8,128)S(1)}, f32[416,128]{1,0:T(8,128)S(1)}, u32[]{:S(2)}, u32[]{:S(2)}) collective-permute-start(f32[416,128]{1,0:T(8,128)S(1)} %dynamic-slice_bitcast_fusion.4), channel_id=1, source_target_pairs={{0,16},{4,20},{8,24},{12,28},{16,0},{20,4},{24,8},{28,12},{1,17},{... | collective-permute-start | bytes 638984 | tf_op jit(solution)/shard_map/cond/branch_1_fun/cond/branch_1_fun/ppermute | solution.py:820
  334.5 5.9 %collective-permute-start.12 = (f32[416,128]{1,0:T(8,128)S(1)}, f32[416,128]{1,0:T(8,128)S(1)}, u32[]{:S(2)}, u32[]{:S(2)}) collective-permute-start(f32[416,128]{1,0:T(8,128)S(1)} %dynamic-slice_bitcast_fusion.3), channel_id=1, source_target_pairs={{0,8},{4,12},{8,0},{12,4},{16,24},{20,28},{24,16},{28,20},{1,9},{5... | collective-permute-start | bytes 638984 | tf_op jit(solution)/shard_map/cond/branch_1_fun/cond/branch_1_fun/ppermute | solution.py:820
  340.5 27.6 %collective-permute-start.13 = (f32[416,128]{1,0:T(8,128)S(1)}, f32[416,128]{1,0:T(8,128)S(1)}, u32[]{:S(2)}, u32[]{:S(2)}) collective-permute-start(f32[416,128]{1,0:T(8,128)S(1)} %dynamic-slice_bitcast_fusion.2), channel_id=1, source_target_pairs={{0,1},{1,0},{2,3},{3,2},{4,5},{5,4},{6,7},{7,6},{8,9},{9,8},{10,11... | collective-permute-start | bytes 638984 | tf_op jit(solution)/shard_map/cond/branch_1_fun/cond/branch_1_fun/ppermute | solution.py:820
  369.7 14.1 %collective-permute-start.14 = (f32[208,128]{1,0:T(8,128)S(1)}, f32[208,128]{1,0:T(8,128)S(1)}, u32[]{:S(2)}, u32[]{:S(2)}) collective-permute-start(f32[208,128]{1,0:T(8,128)S(1)} %dynamic-slice_bitcast_fusion.5), channel_id=1, source_target_pairs={{0,2},{1,3},{2,0},{3,1},{4,6},{5,7},{6,4},{7,5},{8,10},{9,11},{10,... | collective-permute-start | bytes 319496 | tf_op jit(solution)/shard_map/cond/branch_1_fun/cond/branch_1_fun/ppermute | solution.py:820
  384.8 6.0 %collective-permute-start.15 = (f32[208,128]{1,0:T(8,128)S(1)}, f32[208,128]{1,0:T(8,128)S(1)}, u32[]{:S(2)}, u32[]{:S(2)}) collective-permute-start(f32[208,128]{1,0:T(8,128)S(1)} %get-tuple-element.415), channel_id=1, source_target_pairs={{0,2},{1,3},{2,0},{3,1},{4,6},{5,7},{6,4},{7,5},{8,10},{9,11},{10,... | collective-permute-start | bytes 319496 | tf_op jit(solution)/shard_map/cond/branch_1_fun/cond/branch_1_fun/ppermute | solution.py:828
  390.8 6.6 %collective-permute-start.16 = (f32[416,128]{1,0:T(8,128)S(1)}, f32[416,128]{1,0:T(8,128)S(1)}, u32[]{:S(2)}, u32[]{:S(2)}) collective-permute-start(f32[416,128]{1,0:T(8,128)S(1)} %bitcast.97), channel_id=1, source_target_pairs={{0,1},{1,0},{2,3},{3,2},{4,5},{5,4},{6,7},{7,6},{8,9},{9,8},{10,11... | collective-permute-start | bytes 638984 | tf_op jit(solution)/shard_map/cond/branch_1_fun/cond/branch_1_fun/ppermute | solution.py:828
  399.5 49.0 %collective-permute-start.29 = (f32[16,64,512]{2,1,0:T(8,128)}, f32[16,64,512]{2,1,0:T(8,128)S(1)}, u32[]{:S(2)}, u32[]{:S(2)}) collective-permute-start(f32[16,64,512]{2,1,0:T(8,128)} %passed.9), channel_id=1, source_target_pairs={{1,0},{0,1},{5,2},{4,3},{3,4},{2,5},{7,6},{6,7},{9,8},{8,9},{13,10... | collective-permute-start | bytes 6291464 | tf_op jit(solution)/shard_map/ppermute | solution.py:753
  399.7 38.7 %all-gather.2.cloned.1.call-start = ((), (), s32[]{:S(2)}) async-start(), calls=%async_computation.3 | async-start | bytes 3833856 | tf_op jit(solution)/shard_map/cond/branch_1_fun/all_gather | solution.py:1020
  401.5 7.4 %collective-permute-start.17 = (f32[416,128]{1,0:T(8,128)S(1)}, f32[416,128]{1,0:T(8,128)S(1)}, u32[]{:S(2)}, u32[]{:S(2)}) collective-permute-start(f32[416,128]{1,0:T(8,128)S(1)} %get-tuple-element.416), channel_id=1, source_target_pairs={{0,16},{4,20},{8,24},{12,28},{16,0},{20,4},{24,8},{28,12},{1,17},{... | collective-permute-start | bytes 638984 | tf_op jit(solution)/shard_map/cond/branch_1_fun/cond/branch_1_fun/ppermute | solution.py:828
  403.2 7.8 %collective-permute-start.19 = (f32[416,128]{1,0:T(8,128)S(1)}, f32[416,128]{1,0:T(8,128)S(1)}, u32[]{:S(2)}, u32[]{:S(2)}) collective-permute-start(f32[416,128]{1,0:T(8,128)S(1)} %get-tuple-element.417), channel_id=1, source_target_pairs={{0,8},{4,12},{8,0},{12,4},{16,24},{20,28},{24,16},{28,20},{1,9},{5... | collective-permute-start | bytes 638984 | tf_op jit(solution)/shard_map/cond/branch_1_fun/cond/branch_1_fun/ppermute | solution.py:828
  408.9 16.0 %collective-permute-start.18 = (f32[832,128]{1,0:T(8,128)S(1)}, f32[832,128]{1,0:T(8,128)S(1)}, u32[]{:S(2)}, u32[]{:S(2)}) collective-permute-start(f32[832,128]{1,0:T(8,128)S(1)} %bitcast.87), channel_id=1, source_target_pairs={{0,8},{4,12},{8,0},{12,4},{16,24},{20,28},{24,16},{28,20},{1,9},{5... | collective-permute-start | bytes 1277960 | tf_op jit(solution)/shard_map/cond/branch_1_fun/cond/branch_1_fun/ppermute | solution.py:828
  411.1 15.4 %collective-permute-start.20 = (f32[832,128]{1,0:T(8,128)S(1)}, f32[832,128]{1,0:T(8,128)S(1)}, u32[]{:S(2)}, u32[]{:S(2)}) collective-permute-start(f32[832,128]{1,0:T(8,128)S(1)} %bitcast.89), channel_id=1, source_target_pairs={{0,16},{4,20},{8,24},{12,28},{16,0},{20,4},{24,8},{28,12},{1,17},{... | collective-permute-start | bytes 1277960 | tf_op jit(solution)/shard_map/cond/branch_1_fun/cond/branch_1_fun/ppermute | solution.py:828
  427.8 3.9 collective-permute-start.21
  438.5 6.8 %copy-start.3 = (f32[16,64,512]{2,1,0:T(8,128)S(1)}, f32[16,64,512]{2,1,0:T(8,128)}, u32[]{:S(2)}) copy-start(f32[16,64,512]{2,1,0:T(8,128)} %copy-done.2) | copy-start | bytes 6291460
  (6 other events, 10.7 us)
Sparse Core Ops, SparseCore 0:
  243.7 47.1 reduce-scatter.1
  309.7 76.4 all-reduce.1
  402.5 35.9 all-gather.1

commit v5 on v4

--- a/solution.py
+++ b/solution.py
@@ -760,31 +760,33 @@
     refs[-1][...] = values
 
 
-def join(info, own, first, second, after=()):
-    rows, *cell = first.shape
+def join_part(info, flip, sources, others):
+    rows, *cell = sources[0].shape
     anywhere = pl.BlockSpec(memory_space=pl.ANY)
-    shape = jax.ShapeDtypeStruct((2, rows, *cell), F32)
-
-    def part(flip, sources, specs, others):
-        return call(
-            functools.partial(join_kernel, len(sources)),
-            rows // ROWS,
-            specs + [anywhere] * len(others),
-            pl.BlockSpec((None, ROWS, *cell), lambda j, s: (s[1] ^ flip, j, 0, 0)),
-            shape,
-            [],
-            0,
-            0,
-            f"join_{flip}",
-            16,
-            {1 + len(sources): 0} if flip else None,
-        )(info, *sources, *others)
-
     mine = pl.BlockSpec((ROWS, *cell), lambda j, s: (j * s[2], 0, 0))
     sent = pl.BlockSpec((ROWS, *cell), lambda j, s: (j * (1 - s[2]), 0, 0))
     row = pl.BlockSpec((ROWS, *cell), lambda j, s: (j, 0, 0))
-    half = part(0, [own, first], [mine, sent], list(after))
-    return part(1, [second], [row], [half])
+    return call(
+        functools.partial(join_kernel, len(sources)),
+        rows // ROWS,
+        ([row] if flip else [mine, sent]) + [anywhere] * len(others),
+        pl.BlockSpec((None, ROWS, *cell), lambda j, s: (s[1] ^ flip, j, 0, 0)),
+        jax.ShapeDtypeStruct((2, rows, *cell), F32),
+        [],
+        0,
+        0,
+        f"join_{flip}",
+        16,
+        {1 + len(sources): 0} if flip else None,
+    )(info, *sources, *others)
+
+
+def join_first(info, own, first):
+    return join_part(info, 0, [own, first], [])
+
+
+def join_second(info, half, second):
+    return join_part(info, 1, [second], [half])
 
 
 def as_one(function, *args):
@@ -1003,7 +1005,7 @@
         inner = inner.reshape(8, -1, 128).transpose(1, 0, 2)
         first = packed_rows([kept + swap(sent), mix, offsets, inner], 8 * devices)
         first = sum_spread_all(sum_spread_halves(first, members), sections[:1])
-        outputs = join(info, *outputs)
+        outputs = join_second(info, join_first(info, *outputs[:2]), outputs[2])
         [first] = passed([first], [outputs])
         first = sum_spread_all(first, sections[1:])
         return collect_all(first, sections), outputs
@@ -1012,13 +1014,14 @@
         second = lax.psum(second, "section")
         return *as_one(reduce_first, *local, outputs), second
 
-    def share_first(first):
+    def share_first(first, own, returned):
+        half = join_first(info, own, returned)
         summed = collect_halves(first, members)
-        return summed, swap(summed)
-
-    def share_gradients(first, second):
+        return summed, swap(summed), half
+
+    def share_gradients(first, second, own, returned):
         second = lax.all_gather(second, "wide", axis=0, tiled=True)
-        return *as_one(share_first, first), second
+        return *as_one(share_first, first, own, returned), second
 
     def send_both(pieces, routes):
         return [send_piece(piece, route) for piece, route in zip(pieces, routes)]
@@ -1035,10 +1038,10 @@
     returned = send_piece(dxa, back_routes[0])
     first, outputs, second = as_one(reduce_gradients, local, second, outputs)
     dxb = send_piece(*passed([dxb], [returned, first]), back_routes[1])
-    mine, other, second = as_one(share_gradients, first, second)
+    mine, other, half, second = as_one(share_gradients, first, second, dxa, returned)
     shapes = [a.shape for a in (norm_gain, norm_bias, mix_weight, mix_bias, up_weight, up_bias, down_weight, down_bias)]
     gradients = unpack(info, [mine, other, second], shapes)
-    return (outputs, join(info, dxa, returned, dxb), *gradients)
+    return (outputs, join_second(info, half, dxb), *gradients)
 
 
 def solution(mesh):

time: 458 us -> 456 us (level)
  transfers between devices with their start and end apart: 33 -> 33, of which waited for: 23 -> 24; matrix products, arithmetic and copies ran while one was open for 4% -> 4% of each run, Pallas kernels for 37% -> 37%
where the time goes in v5:
time: 456 us; the launch traced here: 455 us
  Pallas kernels  172 us (38%)
  waiting for transfers between devices  162 us (36%)
  starting transfers between devices  80.7 us (18%)
  local copies, waits for them, and re-layouts  19.4 us (4%)
  between operations  13.9 us (3%)
  other arithmetic  6.76 us (1%)
    ppermute x10, starting transfers between devices, swap(): lax.ppermute(values, 'wide', [(i, i ^ 1) for i in range(lax.axis_size('wi...  56.7 us
    pallas_call x3, Pallas kernels, ffn_backward(): call(functools.partial(ffn_backward_kernel, steps, fused, part), steps, s...  56.1 us
    ppermute x6, waiting for transfers between devices, sum_spread(): total = total + lax.ppermute(part, axis, partners(axis, bit, offset))  49.4 us
    ppermute x8, waiting for transfers between devices, send_piece(): return lax.ppermute(piece, BOTH, route)  44.3 us
    ppermute x10, waiting for transfers between devices, swap(): lax.ppermute(values, 'wide', [(i, i ^ 1) for i in range(lax.axis_size('wi...  33.7 us
    pallas_call x2, Pallas kernels, spectral_backward(): call(functools.partial(spectral_backward_kernel, start), 2, specs, out_sp...  28.3 us
    ppermute x6, waiting for transfers between devices, collect(): lax.ppermute(values, axis, partners(axis, bit, offset))  26.5 us
    pallas_call x2, Pallas kernels, spectral_forward(): call(spectral_forward_kernel, 2, [cells, cells, weight, offset, table, ta...  26.4 us
  transfers between devices with their start and end apart: 33, of which 24 were waited for; matrix products, arithmetic and copies ran while one was open for 4% of the time, Pallas kernels for 37%

profile of v5, /device:TPU:0, one launch (start us, length us, event | category | flops | bytes accessed | tf_op | source)
XLA Modules:
  0.0 455.4 jit_solution(15513820746717164161)
XLA Ops:
  7.3 2.5 pick.4
  11.4 3.1 collective-permute-start.23
  16.6 1.4 copy-done.3
  19.3 41.3 %collective-permute-done.23.refs_3_ = f32[16,64,512]{2,1,0:T(8,128)} collective-permute-done((f32[16,64,512]{2,1,0:T(8,128)S(1)}, f32[16,64,512]{2,1,0:T(8,128)}, u32[]{:S(2)}, u32[]{:S(2)}) %collective-permute-start.23) | collective-permute-done | bytes 2097184 | tf_op jit(solution)/shard_map/ppermute | solution.py:753
  61.4 1.8 collective-permute-start.24
  63.2 122.9 %conditional.7 = (f32[16,64,512]{2,1,0:T(8,128)}, f32[16,64,512]{2,1,0:T(8,128)}, f32[2,1024,256]{2,1,0:T(8,128)}, f32[2,1024,256]{2,1,0:T(8,128)}, f32[2,1024,2...) conditional(s32[]{:T(128)} %convert_element_type.16, () %tuple.66, ...), branch_computations={%region_0.1_spmd, %region_1.2_spmd} | conditional | flops 24884901888 | bytes 172229056 | solution.py:796
  63.2 5.1 %first_norm.1 = (f32[32,64,256]{2,1,0:T(8,128)S(1)}, f32[32,64,256]{2,1,0:T(8,128)S(1)}) custom-call(s32[3]{0:T(128)S(1)} %get-tuple-element.182.info, f32[2,16,64,512]{3,2,1,0:T(8,128)} %get-tuple-element.183.own.refs_0_, f32[16,64,512]{2,1,0:T(8,128)} %get-tuple-element.184.a.refs_1_, f32[16,64,512]{2,1,0:T(8,128)} %get-tuple-element.185.b.refs_2_, ...), custom_call_target="tpu_custom_call" | custom-call | bytes 8388608 | tf_op jit(solution)/shard_map/cond/branch_1_fun/first_norm/pallas_call | solution.py:528
  68.4 49.2 %collective-permute-start = (f32[32,64,256]{2,1,0:T(8,128)S(1)}, f32[32,64,256]{2,1,0:T(8,128)S(1)}, u32[]{:S(2)}, u32[]{:S(2)}) collective-permute-start(f32[32,64,256]{2,1,0:T(8,128)S(1)} %get-tuple-element.189), channel_id=1, source_target_pairs={{0,4},{4,0},{8,12},{12,8},{16,20},{20,16},{24,28},{28,24},{1,5},{5... | collective-permute-start | bytes 6291464 | tf_op jit(solution)/shard_map/cond/branch_1_fun/ppermute | solution.py:800
  117.5 3.8 collective-permute-done.recv
  121.4 13.2 %spectral_forward_0.1 = (f32[32,64,256]{2,1,0:T(8,128)S(1)}, f32[32,64,256]{2,1,0:T(8,128)S(1)}, f32[2,1024,256]{2,1,0:T(8,128)}, f32[2,1024,256]{2,1,0:T(8,128)}, f32[2,1024,256]{2,1,0:T(8,128)}) custom-call(s32[3]{0:T(128)S(1)} %get-tuple-element.182.info, f32[32,64,256]{2,1,0:T(8,128)S(1)} %get-tuple-element.188.own, ...), custom_call_target="tpu_custom_call" | custom-call | flops 6000000000 | bytes 14680064 | tf_op jit(solution)/shard_map/cond/branch_1_fun/spectral_forward_0/pallas_call | solution.py:557
  135.0 3.8 collective-permute-done.1.refs_4_
  138.8 13.1 %ffn_forward_0.1 = (f32[32,64,512]{2,1,0:T(8,128)}, f32[32,64,512]{2,1,0:T(8,128)}, f32[32,64,512]{2,1,0:T(8,128)}, f32[32,64,256]{2,1,0:T(8,128)S(1)}, f32[32,64,256]{2,1,0:T(8,128)S(1)}) custom-call(s32[3]{0:T(128)S(1)} %get-tuple-element.182.info, f32[2,16,64,512]{3,2,1,0:T(8,128)S(1)} %copy-done.7, f32[16,64,512]{2,1,0:T(8,128)S(1)} %copy-done.11, ...), custom_call_target="tpu_custom_call" | custom-call | flops 6442450944 | bytes 25165824 | tf_op jit(solution)/shard_map/cond/branch_1_fun/ffn_forward_0/pallas_call | solution.py:626
  152.2 3.8 collective-permute-done.2.recv
  156.0 13.2 %spectral_forward_1.1 = (f32[32,64,256]{2,1,0:T(8,128)S(1)}, f32[32,64,256]{2,1,0:T(8,128)S(1)}, f32[2,1024,256]{2,1,0:T(8,128)}, f32[2,1024,256]{2,1,0:T(8,128)}, f32[2,1024,256]{2,1,0:T(8,128)}) custom-call(s32[3]{0:T(128)S(1)} %get-tuple-element.182.info, f32[32,64,256]{2,1,0:T(8,128)S(1)} %get-tuple-element.201.own, ...), custom_call_target="tpu_custom_call" | custom-call | flops 6000000000 | bytes 14680064 | tf_op jit(solution)/shard_map/cond/branch_1_fun/spectral_forward_1/pallas_call | solution.py:557
  169.6 3.8 collective-permute-done.3.refs_2_
  173.4 12.7 %ffn_forward_1.1 = (f32[32,64,512]{2,1,0:T(8,128)S(1)}, f32[32,64,512]{2,1,0:T(8,128)S(1)}, f32[16,64,512]{2,1,0:T(8,128)}, f32[16,64,512]{2,1,0:T(8,128)}) custom-call(s32[3]{0:T(128)S(1)} %get-tuple-element.182.info, f32[32,64,512]{2,1,0:T(8,128)} %get-tuple-element.485.refs_0_, f32[32,64,256]{2,1,0:T(8,128)S(1)} %get-tuple-element.203.refs_1_, ...), custom_call_target="tpu_custom_call" | custom-call | flops 6442450944 | bytes 25165824 | tf_op jit(solution)/shard_map/cond/branch_1_fun/ffn_forward_1/pallas_call | solution.py:626
  186.1 5.1 %copy-done.1 = f32[2,16,64,512]{3,2,1,0:T(8,128)S(1)} copy-done((f32[2,16,64,512]{3,2,1,0:T(8,128)S(1)}, f32[2,16,64,512]{3,2,1,0:T(8,128)}, u32[]{:S(2)}) %copy-start.1) | copy-done | bytes 4194328
  191.2 12.4 %ffn_backward_1_0.1 = (f32[32,64,256]{2,1,0:T(8,128)}, f32[32,64,256]{2,1,0:T(8,128)}, f32[512,512]{1,0:T(8,128)S(1)}, f32[512,512]{1,0:T(8,128)}, f32[8,512]{1,0:T(8,128)S(1)}) custom-call(s32[3]{0:T(128)S(1)} %pad_add_fusion.info, f32[32,64,512]{2,1,0:T(8,128)S(1)} %get-tuple-element.378.refs_0_, f32[32,64,512]{2,1,0:T(8,128)S(1)} %get-tuple-element.379.refs_1_, ...), custom_call_target="tpu_custom_call" | custom-call | flops 12884901888 | bytes 25165824 | tf_op jit(solution)/shard_map/ffn_backward_1_0/pallas_call | solution.py:672
  203.7 2.2 collective-permute-start.26
  206.1 99.4 %conditional.8 = (f32[16,64,512]{2,1,0:T(8,128)}, f32[16,64,512]{2,1,0:T(8,128)}, f32[4,544,128]{2,1,0:T(8,128)}, f32[4,544,128]{2,1,0:T(8,128)}, f32[2,2,2,128,...) conditional(s32[]{:T(128)} %convert_element_type.16, () %tuple.65, ...), branch_computations={%region_2.3_spmd, %region_3.7_spmd} | conditional | flops 25769803776 | bytes 213091216 | solution.py:796
  206.2 15.3 %ffn_backward_1_1.1 = (f32[32,64,256]{2,1,0:T(8,128)S(1)}, f32[32,64,256]{2,1,0:T(8,128)}, f32[6656,128]{1,0:T(8,128)}) custom-call(s32[3]{0:T(128)S(1)} %get-tuple-element.249.info, f32[32,64,512]{2,1,0:T(8,128)} %get-tuple-element.257.refs_0_, f32[32,64,512]{2,1,0:T(8,128)} %get-tuple-element.258.refs_1_, ...), custom_call_target="tpu_custom_call", output_to_operand_aliasing={{0}: (11, {}), {1}: (12, {})} | custom-call | flops 12884901888 | bytes 25165824 | tf_op jit(solution)/shard_map/cond/branch_1_fun/ffn_backward_1_1/pallas_call | solution.py:672
  221.5 3.4 collective-permute-start.6
  224.9 4.0 collective-permute-done.6.recv
  228.9 14.6 %spectral_backward_1.1 = (f32[32,64,256]{2,1,0:T(8,128)}, f32[32,64,256]{2,1,0:T(8,128)S(1)}, f32[6656,128]{1,0:T(8,128)}) custom-call(s32[3]{0:T(128)S(1)} %get-tuple-element.249.info, f32[32,64,256]{2,1,0:T(8,128)} %copy-done.26, f32[32,64,256]{2,1,0:T(8,128)S(1)} %collective-permute-done.6.recv, ...), custom_call_target="tpu_custom_call", output_to_operand_aliasing={{2}: (9, {})} | custom-call | tf_op jit(solution)/shard_map/cond/branch_1_fun/spectral_backward_1/pallas_call | solution.py:594
  244.0 3.9 collective-permute-done.7
  247.9 57.6 %conditional = (f32[16,64,512]{2,1,0:T(8,128)}, f32[16,64,512]{2,1,0:T(8,128)}, f32[4,544,128]{2,1,0:T(8,128)}, f32[4,544,128]{2,1,0:T(8,128)}, f32[2,2,2,128,12...) conditional(s32[]{:T(128)} %convert_element_type.3, () %tuple.39, (s32[3]{0:T(128)S(1)}, ...), branch_computations={%region_4.4_spmd, %region_5.5_spmd} | conditional | flops 12884901888 | bytes 117440824 | solution.py:796
  247.9 28.4 %ffn_backward_0_0.1 = (f32[32,64,256]{2,1,0:T(8,128)S(1)}, f32[32,64,256]{2,1,0:T(8,128)S(1)}, f32[4,544,128]{2,1,0:T(8,128)}, f32[4,544,128]{2,1,0:T(8,128)}) custom-call(s32[3]{0:T(128)S(1)} %get-tuple-element.217.info, f32[32,64,512]{2,1,0:T(8,128)} %get-tuple-element.221.refs_0_, f32[32,64,512]{2,1,0:T(8,128)} %get-tuple-element.222.refs_1_, ...), custom_call_target="tpu_custom_call" | custom-call | flops 12884901888 | bytes 25165824 | tf_op jit(solution)/shard_map/cond/branch_1_fun/cond/branch_1_fun/ffn_backward_0_0/pallas_call | solution.py:672
  276.7 3.8 collective-permute-done.4.recv
  280.5 13.6 %spectral_backward_0.1 = (f32[32,64,256]{2,1,0:T(8,128)S(1)}, f32[32,64,256]{2,1,0:T(8,128)S(1)}, f32[2,2,2,128,128]{4,3,2,1,0:T(8,128)}, f32[2,8,128]{2,1,0:T(8,128)}) custom-call(s32[3]{0:T(128)S(1)} %get-tuple-element.217.info, f32[32,64,256]{2,1,0:T(8,128)S(1)} %get-tuple-element.232.own.du_kept, f32[32,64,256]{2,1,0:T(8,128)S(1)} %collective-permute-done.4.recv, ...), custom_call_target="tpu_custom_call" | custom-call | tf_op jit(solution)/shard_map/cond/branch_1_fun/cond/branch_1_fun/spectral_backward_0/pallas_call | solution.py:594
  294.5 3.8 collective-permute-done.5.dh_taken
  298.3 7.2 %input_gradient.1 = (f32[16,64,512]{2,1,0:T(8,128)}, f32[16,64,512]{2,1,0:T(8,128)}, f32[8,512]{1,0:T(8,128)}) custom-call(s32[3]{0:T(128)S(1)} %get-tuple-element.217.info, f32[2,16,64,512]{3,2,1,0:T(8,128)S(1)} %copy-done.8, f32[16,64,512]{2,1,0:T(8,128)S(1)} %copy-done.12, f32[16,64,512]{2,1,0:T(8,128)} %get-tuple-element.220.b, ...), custom_call_target="tpu_custom_call" | custom-call | bytes 16777216 | tf_op jit(solution)/shard_map/cond/branch_1_fun/cond/branch_1_fun/input_gradient/pallas_call | solution.py:688
  305.5 2.2 collective-permute-start.28
  307.7 90.6 %conditional.9 = (f32[832,128]{1,0:T(8,128)}, f32[2,16,64,512]{3,2,1,0:T(8,128)}, f32[832,128]{1,0:T(8,128)}) conditional(s32[]{:T(128)} %convert_element_type.16, () %tuple.64, (f32[4,544,128]{2,1,0:T(8,128)}, f32[4,544,128]{2,1,0:T(8,128)}, f32[2,2,2,128,128]{4,3,2,1,0:T(8,128)}, f32[2,8,128]{2,1,0:T(8,128)}, f32[8,512]{1,0:T(8,128)}, ...), branch_computations={%region_7.8_spmd, %region_8.12_spmd} | conditional | flops 890966 | bytes 38856152 | solution.py:796
  308.4 89.8 %conditional.1 = (f32[832,128]{1,0:T(8,128)}, f32[2,16,64,512]{3,2,1,0:T(8,128)}) conditional(s32[]{:T(128)} %convert_element_type.5, () %tuple.45, (f32[4,544,128]{2,1,0:T(8,128)}, f32[4,544,128]{2,1,0:T(8,128)}, f32[2,2,2,128,128]{4,3,2,1,0:T(8,128)}, f32[2,8,128]{2,1,0:T(8,128)}, f32[8,512]{1,0:T(8,128)}, /*index=5*/s32[3]{0:T(128)S(1)}, ...), branch_computations={%region_9.9_spmd, %region_10.10_spmd} | conditional | flops 784465 | bytes 36300064 | solution.py:796
  308.5 1.9 collective-permute-start.8
  310.4 2.6 collective-permute-done.8
  314.5 1.6 collective-permute-start.9
  320.4 1.5 collective-permute-start.11
  321.9 4.9 %collective-permute-done.9 = f32[832,128]{1,0:T(8,128)} collective-permute-done((f32[832,128]{1,0:T(8,128)S(1)}, f32[832,128]{1,0:T(8,128)}, u32[]{:S(2)}, u32[]{:S(2)}) %collective-permute-start.9) | collective-permute-done | bytes 426016 | tf_op jit(solution)/shard_map/cond/branch_1_fun/cond/branch_1_fun/ppermute | solution.py:822
  327.9 1.6 collective-permute-start.10
  329.5 3.9 collective-permute-done.11
  335.2 1.8 collective-permute-done.10
  337.0 3.5 collective-permute-done.12
  340.7 3.2 join_0.2.refs_1_
  343.9 3.2 join_1.2.refs_1_
  347.1 21.1 %collective-permute-done.13 = f32[416,128]{1,0:T(8,128)S(1)} collective-permute-done((f32[416,128]{1,0:T(8,128)S(1)}, f32[416,128]{1,0:T(8,128)S(1)}, u32[]{:S(2)}, u32[]{:S(2)}) %collective-permute-start.13) | collective-permute-done | bytes 213024 | tf_op jit(solution)/shard_map/cond/branch_1_fun/cond/branch_1_fun/ppermute | solution.py:822
  369.9 14.1 %collective-permute-done.14 = f32[208,128]{1,0:T(8,128)S(1)} collective-permute-done((f32[208,128]{1,0:T(8,128)S(1)}, f32[208,128]{1,0:T(8,128)S(1)}, u32[]{:S(2)}, u32[]{:S(2)}) %collective-permute-start.14) | collective-permute-done | bytes 106528 | tf_op jit(solution)/shard_map/cond/branch_1_fun/cond/branch_1_fun/ppermute | solution.py:822
  385.0 6.0 %collective-permute-done.15 = f32[208,128]{1,0:T(8,128)S(1)} collective-permute-done((f32[208,128]{1,0:T(8,128)S(1)}, f32[208,128]{1,0:T(8,128)S(1)}, u32[]{:S(2)}, u32[]{:S(2)}) %collective-permute-start.15) | collective-permute-done | bytes 106528 | tf_op jit(solution)/shard_map/cond/branch_1_fun/cond/branch_1_fun/ppermute | solution.py:830
  392.5 5.0 %collective-permute-done.16 = f32[416,128]{1,0:T(8,128)S(1)} collective-permute-done((f32[416,128]{1,0:T(8,128)S(1)}, f32[416,128]{1,0:T(8,128)S(1)}, u32[]{:S(2)}, u32[]{:S(2)}) %collective-permute-start.16) | collective-permute-done | bytes 213024 | tf_op jit(solution)/shard_map/cond/branch_1_fun/cond/branch_1_fun/ppermute | solution.py:830
  398.6 38.7 %conditional.10 = (f32[3328,128]{1,0:T(8,128)}, f32[3328,128]{1,0:T(8,128)}, f32[2,16,64,512]{3,2,1,0:T(8,128)}, f32[6656,128]{1,0:T(8,128)}) conditional(s32[]{:T(128)} %convert_element_type.16, () %tuple.70, (f32[832,128]{1,0:T(8,128)}, s32[3]{0:T(128)S(1)}, f32[16,64,512]{2,1,0:T(8,128)}, f32[16,64,512]{2,1,0:T(8,128)}, ...), branch_computations={%region_12.13_spmd, %region_13.16_spmd} | conditional | flops 426030 | bytes 35357528 | solution.py:796
  399.3 31.3 %conditional.2 = (f32[3328,128]{1,0:T(8,128)}, f32[3328,128]{1,0:T(8,128)}, f32[2,16,64,512]{3,2,1,0:T(8,128)}) conditional(s32[]{:T(128)} %convert_element_type.8, () %tuple.51, (f32[832,128]{1,0:T(8,128)}, s32[3]{0:T(128)S(1)}, f32[16,64,512]{2,1,0:T(8,128)}, f32[16,64,512]{2,1,0:T(8,128)}) %tuple.52), branch_computations={%region_14.14_spmd, %region_15.15_spmd} | conditional | flops 426025 | bytes 23855810 | solution.py:796
  400.4 1.7 collective-permute-start.17
  402.0 1.8 collective-permute-start.19
  405.9 1.9 collective-permute-done.17
  407.8 2.1 collective-permute-start.18
  409.9 1.5 collective-permute-start.20
  411.6 12.1 %collective-permute-done.18 = f32[832,128]{1,0:T(8,128)S(1)} collective-permute-done((f32[832,128]{1,0:T(8,128)S(1)}, f32[832,128]{1,0:T(8,128)S(1)}, u32[]{:S(2)}, u32[]{:S(2)}) %collective-permute-start.18) | collective-permute-done | bytes 426016 | tf_op jit(solution)/shard_map/cond/branch_1_fun/cond/branch_1_fun/ppermute | solution.py:830
  423.8 1.5 collective-permute-done.20
  425.3 1.4 pad_maximum_fusion.1
  426.6 3.5 join_0.3
  430.6 6.7 %all-gather.2.cloned.1.call-done = f32[6656,128]{1,0:T(8,128)} async-done(((f32[832,128]{1,0:T(8,128)}), f32[6656,128]{1,0:T(8,128)}) %all-gather.2.cloned.1.call-update) | async-done | bytes 3407888 | tf_op jit(solution)/shard_map/cond/branch_1_fun/all_gather | solution.py:1023
  437.3 6.7 %unpack.1 = (f32[2,2,512]{2,1,0:T(2,128)}, f32[2,2,512]{2,1,0:T(2,128)}, f32[2,2,2,4,128,128]{5,4,3,2,1,0:T(8,128)}, f32[2,2,2,4,128]{4,3,2,1,0:T(4,128)}, f32[2...) custom-call(s32[3]{0:T(128)S(1)} %pad_add_fusion.info, ...), custom_call_target="tpu_custom_call" | custom-call | tf_op jit(solution)/shard_map/unpack/pallas_call | solution.py:932
  444.0 2.9 collective-permute-done.29.refs_0_
  447.0 1.9 join_1.3
  (150 shorter events, 27.7 us)
Async XLA Ops:
  7.3 3.4 copy-start.6
  9.7 4.8 %copy-start = (f32[2,16,64,512]{3,2,1,0:T(8,128)S(1)}, f32[2,16,64,512]{3,2,1,0:T(8,128)}, u32[]{:S(2)}) copy-start(f32[2,16,64,512]{3,2,1,0:T(8,128)} %refs_6_.1) | copy-start | bytes 12582916
  9.8 8.2 %collective-permute-start.22 = (f32[16,64,512]{2,1,0:T(8,128)S(1)}, f32[16,64,512]{2,1,0:T(8,128)S(1)}, u32[]{:S(2)}, u32[]{:S(2)}) collective-permute-start(f32[16,64,512]{2,1,0:T(8,128)S(1)} %pick.4), channel_id=1, source_target_pairs={{2,4},{3,5},{4,2},{5,3},{10,12},{11,13},{12,10},{13,11},{18,20},{1... | collective-permute-start | bytes 6291464 | tf_op jit(solution)/shard_map/ppermute | solution.py:753
  11.4 49.2 %collective-permute-start.23 = (f32[16,64,512]{2,1,0:T(8,128)S(1)}, f32[16,64,512]{2,1,0:T(8,128)}, u32[]{:S(2)}, u32[]{:S(2)}) collective-permute-start(f32[16,64,512]{2,1,0:T(8,128)S(1)} %pick.5), channel_id=1, source_target_pairs={{0,1},{1,0},{2,5},{3,4},{4,3},{5,2},{6,7},{7,6},{8,9},{9,8},{10,13... | collective-permute-start | bytes 6291464 | tf_op jit(solution)/shard_map/ppermute | solution.py:753
  17.9 45.2 %copy-start.29 = (f32[2,2,512]{2,1,0:T(2,128)S(1)}, f32[2,2,512]{2,1,0:T(2,128)}, u32[]{:S(2)}) copy-start(f32[2,2,512]{2,1,0:T(2,128)} %refs_2_.1) | copy-start | bytes 24580
  17.9 45.2 %copy-start.30 = (f32[2,2,512]{2,1,0:T(2,128)S(1)}, f32[2,2,512]{2,1,0:T(2,128)}, u32[]{:S(2)}) copy-start(f32[2,2,512]{2,1,0:T(2,128)} %refs_3_.1) | copy-start | bytes 24580
  18.0 45.2 %copy-start.33 = (f32[2,2,2,4,128]{4,3,2,1,0:T(4,128)S(1)}, f32[2,2,2,4,128]{4,3,2,1,0:T(4,128)}, u32[]{:S(2)}) copy-start(f32[2,2,2,4,128]{4,3,2,1,0:T(4,128)} %param.32) | copy-start | bytes 49156
  18.0 45.2 %copy-start.34 = (f32[2,512]{1,0:T(2,128)S(1)}, f32[2,512]{1,0:T(2,128)}, u32[]{:S(2)}) copy-start(f32[2,512]{1,0:T(2,128)} %param.34) | copy-start | bytes 12292
  18.0 45.2 %copy-start.35 = (f32[2,512]{1,0:T(2,128)S(1)}, f32[2,512]{1,0:T(2,128)}, u32[]{:S(2)}) copy-start(f32[2,512]{1,0:T(2,128)} %param.36) | copy-start | bytes 12292
  60.6 125.5 %collective-permute-start.25 = (f32[16,64,512]{2,1,0:T(8,128)}, f32[16,64,512]{2,1,0:T(8,128)S(1)}, u32[]{:S(2)}, u32[]{:S(2)}) collective-permute-start(f32[16,64,512]{2,1,0:T(8,128)} %get-tuple-element.381), channel_id=1, source_target_pairs={{2,4},{3,5},{4,2},{5,3},{10,12},{11,13},{12,10},{13,11},{18,20},{1... | collective-permute-start | bytes 6291464 | tf_op jit(solution)/shard_map/ppermute | solution.py:753
  61.4 142.3 %collective-permute-start.24 = (f32[16,64,512]{2,1,0:T(8,128)}, f32[16,64,512]{2,1,0:T(8,128)}, u32[]{:S(2)}, u32[]{:S(2)}) collective-permute-start(f32[16,64,512]{2,1,0:T(8,128)} %get-tuple-element.380), channel_id=1, source_target_pairs={{0,1},{1,0},{2,5},{3,4},{4,3},{5,2},{6,7},{7,6},{8,9},{9,8},{10,13... | collective-permute-start | bytes 6291464 | tf_op jit(solution)/shard_map/ppermute | solution.py:753
  63.2 58.1 %copy-start.4 = (bf16[64,256]{1,0:T(8,128)(2,1)S(1)}, bf16[64,256]{1,0:T(8,128)(2,1)}, u32[]{:S(2)}) copy-start(bf16[64,256]{1,0:T(8,128)(2,1)} %constant.236.clone.1.table_in) | copy-start | bytes 98308 | tf_op jit(solution)/shard_map/cond
  63.2 58.1 %copy-start.5 = (bf16[64,256]{1,0:T(8,128)(2,1)S(1)}, bf16[64,256]{1,0:T(8,128)(2,1)}, u32[]{:S(2)}) copy-start(bf16[64,256]{1,0:T(8,128)(2,1)} %constant.239.clone.1.table_out) | copy-start | bytes 98308 | tf_op jit(solution)/shard_map/cond
  63.2 58.1 %copy-start.13 = (f32[2,2,2,4,128,128]{5,4,3,2,1,0:T(8,128)S(1)}, f32[2,2,2,4,128,128]{5,4,3,2,1,0:T(8,128)}, u32[]{:S(2)}) copy-start(f32[2,2,2,4,128,128]{5,4,3,2,1,0:T(8,128)} %get-tuple-element.190.weight) | copy-start | bytes 6291460 | tf_op jit(solution)/shard_map/cond
  68.4 53.0 %collective-permute-start = (f32[32,64,256]{2,1,0:T(8,128)S(1)}, f32[32,64,256]{2,1,0:T(8,128)S(1)}, u32[]{:S(2)}, u32[]{:S(2)}) collective-permute-start(f32[32,64,256]{2,1,0:T(8,128)S(1)} %get-tuple-element.189), channel_id=1, source_target_pairs={{0,4},{4,0},{8,12},{12,8},{16,20},{20,16},{24,28},{28,24},{1,5},{5... | collective-permute-start | bytes 6291464 | tf_op jit(solution)/shard_map/cond/branch_1_fun/ppermute | solution.py:800
  121.3 17.4 %copy-start.7 = (f32[2,16,64,512]{3,2,1,0:T(8,128)S(1)}, f32[2,16,64,512]{3,2,1,0:T(8,128)}, u32[]{:S(2)}) copy-start(f32[2,16,64,512]{3,2,1,0:T(8,128)} %get-tuple-element.183.own.refs_0_) | copy-start | bytes 12582916 | tf_op jit(solution)/shard_map/cond
  121.3 17.4 %copy-start.11 = (f32[16,64,512]{2,1,0:T(8,128)S(1)}, f32[16,64,512]{2,1,0:T(8,128)}, u32[]{:S(2)}) copy-start(f32[16,64,512]{2,1,0:T(8,128)} %get-tuple-element.184.a.refs_1_) | copy-start | bytes 6291460 | tf_op jit(solution)/shard_map/cond
  121.3 17.4 %copy-start.31 = (f32[2,512,512]{2,1,0:T(8,128)S(1)}, f32[2,512,512]{2,1,0:T(8,128)}, u32[]{:S(2)}) copy-start(f32[2,512,512]{2,1,0:T(8,128)} %get-tuple-element.196.refs_7_.refs_5_) | copy-start | bytes 6291460 | tf_op jit(solution)/shard_map/cond
  121.4 17.4 %copy-start.32 = (f32[2,512,512]{2,1,0:T(8,128)S(1)}, f32[2,512,512]{2,1,0:T(8,128)}, u32[]{:S(2)}) copy-start(f32[2,512,512]{2,1,0:T(8,128)} %get-tuple-element.198.refs_9_.refs_7_) | copy-start | bytes 6291460 | tf_op jit(solution)/shard_map/cond
  134.6 4.2 collective-permute-start.1
  151.9 4.2 collective-permute-start.2
  169.2 4.2 collective-permute-start.3
  186.1 17.5 %copy-start.22 = (f32[32,64,512]{2,1,0:T(8,128)}, f32[32,64,512]{2,1,0:T(8,128)S(1)}, u32[]{:S(2)}) copy-start(f32[32,64,512]{2,1,0:T(8,128)S(1)} %get-tuple-element.378.refs_0_) | copy-start | bytes 12582916
  186.1 17.5 %copy-start.23 = (f32[32,64,512]{2,1,0:T(8,128)}, f32[32,64,512]{2,1,0:T(8,128)S(1)}, u32[]{:S(2)}) copy-start(f32[32,64,512]{2,1,0:T(8,128)S(1)} %get-tuple-element.379.refs_1_) | copy-start | bytes 12582916
  186.1 5.1 %copy-start.1 = (f32[2,16,64,512]{3,2,1,0:T(8,128)S(1)}, f32[2,16,64,512]{3,2,1,0:T(8,128)}, u32[]{:S(2)}) copy-start(f32[2,16,64,512]{3,2,1,0:T(8,128)} %refs_6_.1) | copy-start | bytes 12582916
  203.7 2.4 copy-start.25
  203.7 101.8 %collective-permute-start.26 = (f32[16,64,512]{2,1,0:T(8,128)}, f32[16,64,512]{2,1,0:T(8,128)}, u32[]{:S(2)}, u32[]{:S(2)}) collective-permute-start(f32[16,64,512]{2,1,0:T(8,128)} %get-tuple-element.403), channel_id=1, source_target_pairs={{4,2},{5,3},{2,4},{3,5},{12,10},{13,11},{10,12},{11,13},{20,18},{2... | collective-permute-start | bytes 6291464 | tf_op jit(solution)/shard_map/ppermute | solution.py:753
  205.9 99.6 %collective-permute-start.27 = (f32[16,64,512]{2,1,0:T(8,128)}, f32[16,64,512]{2,1,0:T(8,128)}, u32[]{:S(2)}, u32[]{:S(2)}) collective-permute-start(f32[16,64,512]{2,1,0:T(8,128)} %get-tuple-element.404), channel_id=1, source_target_pairs={{1,0},{0,1},{5,2},{4,3},{3,4},{2,5},{7,6},{6,7},{9,8},{8,9},{13,10... | collective-permute-start | bytes 6291464 | tf_op jit(solution)/shard_map/ppermute | solution.py:753
  206.1 99.4 %reduce-scatter.2.cloned.1.call-start = ((), (), s32[]{:S(2)}) async-start(), calls=%async_computation.1 | async-start | bytes 3833856 | tf_op jit(solution)/shard_map/cond/branch_1_fun/reduce_scatter | solution.py:993
  206.1 22.8 %copy-start.14 = (f32[2,2,2,4,128,128]{5,4,3,2,1,0:T(8,128)S(1)}, f32[2,2,2,4,128,128]{5,4,3,2,1,0:T(8,128)}, u32[]{:S(2)}) copy-start(f32[2,2,2,4,128,128]{5,4,3,2,1,0:T(8,128)} %get-tuple-element.267.weight) | copy-start | bytes 6291460 | tf_op jit(solution)/shard_map/cond
  206.1 22.8 %copy-start.19 = (f32[2,1024,256]{2,1,0:T(8,128)S(1)}, f32[2,1024,256]{2,1,0:T(8,128)}, u32[]{:S(2)}) copy-start(f32[2,1024,256]{2,1,0:T(8,128)} %get-tuple-element.268.modes) | copy-start | bytes 6291460 | tf_op jit(solution)/shard_map/cond
  206.1 22.8 %copy-start.20 = (f32[2,1024,256]{2,1,0:T(8,128)S(1)}, f32[2,1024,256]{2,1,0:T(8,128)}, u32[]{:S(2)}) copy-start(f32[2,1024,256]{2,1,0:T(8,128)} %get-tuple-element.269.before) | copy-start | bytes 6291460 | tf_op jit(solution)/shard_map/cond
  206.1 22.8 %copy-start.21 = (f32[2,1024,256]{2,1,0:T(8,128)S(1)}, f32[2,1024,256]{2,1,0:T(8,128)}, u32[]{:S(2)}) copy-start(f32[2,1024,256]{2,1,0:T(8,128)} %get-tuple-element.270.after) | copy-start | bytes 6291460 | tf_op jit(solution)/shard_map/cond
  206.1 22.8 %copy-start.27 = (bf16[64,256]{1,0:T(8,128)(2,1)S(1)}, bf16[64,256]{1,0:T(8,128)(2,1)}, u32[]{:S(2)}) copy-start(bf16[64,256]{1,0:T(8,128)(2,1)} %constant.237.clone.1.table_in) | copy-start | bytes 98308 | tf_op jit(solution)/shard_map/cond
  206.1 22.7 %copy-start.28 = (bf16[64,256]{1,0:T(8,128)(2,1)S(1)}, bf16[64,256]{1,0:T(8,128)(2,1)}, u32[]{:S(2)}) copy-start(bf16[64,256]{1,0:T(8,128)(2,1)} %constant.238.clone.1.table_out) | copy-start | bytes 98308 | tf_op jit(solution)/shard_map/cond
  221.5 7.4 %copy-start.26 = (f32[32,64,256]{2,1,0:T(8,128)}, f32[32,64,256]{2,1,0:T(8,128)S(1)}, u32[]{:S(2)}) copy-start(f32[32,64,256]{2,1,0:T(8,128)S(1)} %get-tuple-element.265.own) | copy-start | bytes 6291460 | tf_op jit(solution)/shard_map/cond
  221.5 7.4 %collective-permute-start.6 = (f32[32,64,256]{2,1,0:T(8,128)}, f32[32,64,256]{2,1,0:T(8,128)S(1)}, u32[]{:S(2)}, u32[]{:S(2)}) collective-permute-start(f32[32,64,256]{2,1,0:T(8,128)} %get-tuple-element.266), channel_id=1, source_target_pairs={{0,4},{4,0},{8,12},{12,8},{16,20},{20,16},{24,28},{28,24},{1,5},{5... | collective-permute-start | bytes 6291464 | tf_op jit(solution)/shard_map/cond/branch_1_fun/ppermute | solution.py:800
  243.6 4.4 collective-permute-start.7
  247.9 32.5 %copy-start.15 = (f32[2,2,2,4,128,128]{5,4,3,2,1,0:T(8,128)S(1)}, f32[2,2,2,4,128,128]{5,4,3,2,1,0:T(8,128)}, u32[]{:S(2)}) copy-start(f32[2,2,2,4,128,128]{5,4,3,2,1,0:T(8,128)} %get-tuple-element.234.weight) | copy-start | bytes 6291460 | tf_op jit(solution)/shard_map/cond/branch_1_fun/cond
  247.9 32.5 %copy-start.16 = (f32[2,1024,256]{2,1,0:T(8,128)S(1)}, f32[2,1024,256]{2,1,0:T(8,128)}, u32[]{:S(2)}) copy-start(f32[2,1024,256]{2,1,0:T(8,128)} %get-tuple-element.235.modes) | copy-start | bytes 6291460 | tf_op jit(solution)/shard_map/cond/branch_1_fun/cond
  247.9 32.5 %copy-start.17 = (f32[2,1024,256]{2,1,0:T(8,128)S(1)}, f32[2,1024,256]{2,1,0:T(8,128)}, u32[]{:S(2)}) copy-start(f32[2,1024,256]{2,1,0:T(8,128)} %get-tuple-element.236.before) | copy-start | bytes 6291460 | tf_op jit(solution)/shard_map/cond/branch_1_fun/cond
  247.9 32.6 %copy-start.18 = (f32[2,1024,256]{2,1,0:T(8,128)S(1)}, f32[2,1024,256]{2,1,0:T(8,128)}, u32[]{:S(2)}) copy-start(f32[2,1024,256]{2,1,0:T(8,128)} %get-tuple-element.237.after) | copy-start | bytes 6291460 | tf_op jit(solution)/shard_map/cond/branch_1_fun/cond
  276.3 4.2 collective-permute-start.4
  280.5 17.8 %copy-start.8 = (f32[2,16,64,512]{3,2,1,0:T(8,128)S(1)}, f32[2,16,64,512]{3,2,1,0:T(8,128)}, u32[]{:S(2)}) copy-start(f32[2,16,64,512]{3,2,1,0:T(8,128)} %get-tuple-element.218.own) | copy-start | bytes 12582916 | tf_op jit(solution)/shard_map/cond/branch_1_fun/cond
  280.5 17.8 %copy-start.12 = (f32[16,64,512]{2,1,0:T(8,128)S(1)}, f32[16,64,512]{2,1,0:T(8,128)}, u32[]{:S(2)}) copy-start(f32[16,64,512]{2,1,0:T(8,128)} %get-tuple-element.219.a) | copy-start | bytes 6291460 | tf_op jit(solution)/shard_map/cond/branch_1_fun/cond
  294.2 4.2 collective-permute-start.5
  305.5 92.7 %collective-permute-start.28 = (f32[16,64,512]{2,1,0:T(8,128)}, f32[16,64,512]{2,1,0:T(8,128)}, u32[]{:S(2)}, u32[]{:S(2)}) collective-permute-start(f32[16,64,512]{2,1,0:T(8,128)} %passed.8), channel_id=1, source_target_pairs={{4,2},{5,3},{2,4},{3,5},{12,10},{13,11},{10,12},{11,13},{20,18},{2... | collective-permute-start | bytes 6291464 | tf_op jit(solution)/shard_map/ppermute | solution.py:753
  307.7 90.6 %all-reduce.2.cloned.1.call-start = ((), (), s32[]{:S(2)}) async-start(), calls=%async_computation.2 | async-start | bytes 851968 | tf_op jit(solution)/shard_map/cond/branch_1_fun/psum | solution.py:1014
  308.5 4.5 collective-permute-start.8
  314.5 12.3 %collective-permute-start.9 = (f32[832,128]{1,0:T(8,128)S(1)}, f32[832,128]{1,0:T(8,128)}, u32[]{:S(2)}, u32[]{:S(2)}) collective-permute-start(f32[832,128]{1,0:T(8,128)S(1)} %dynamic-slice_bitcast_fusion.1), channel_id=1, source_target_pairs={{0,8},{4,12},{8,0},{12,4},{16,24},{20,28},{24,16},{28,20},{1,9},{5... | collective-permute-start | bytes 1277960 | tf_op jit(solution)/shard_map/cond/branch_1_fun/cond/branch_1_fun/ppermute | solution.py:822
  320.4 13.0 %collective-permute-start.11 = (f32[832,128]{1,0:T(8,128)}, f32[832,128]{1,0:T(8,128)}, u32[]{:S(2)}, u32[]{:S(2)}) collective-permute-start(f32[832,128]{1,0:T(8,128)} %dynamic-slice_bitcast_fusion), channel_id=1, source_target_pairs={{0,16},{4,20},{8,24},{12,28},{16,0},{20,4},{24,8},{28,12},{1,17},{... | collective-permute-start | bytes 1277960 | tf_op jit(solution)/shard_map/cond/branch_1_fun/cond/branch_1_fun/ppermute | solution.py:822
  327.9 9.1 %collective-permute-start.10 = (f32[416,128]{1,0:T(8,128)S(1)}, f32[416,128]{1,0:T(8,128)S(1)}, u32[]{:S(2)}, u32[]{:S(2)}) collective-permute-start(f32[416,128]{1,0:T(8,128)S(1)} %dynamic-slice_bitcast_fusion.4), channel_id=1, source_target_pairs={{0,16},{4,20},{8,24},{12,28},{16,0},{20,4},{24,8},{28,12},{1,17},{... | collective-permute-start | bytes 638984 | tf_op jit(solution)/shard_map/cond/branch_1_fun/cond/branch_1_fun/ppermute | solution.py:822
  334.6 5.9 %collective-permute-start.12 = (f32[416,128]{1,0:T(8,128)S(1)}, f32[416,128]{1,0:T(8,128)S(1)}, u32[]{:S(2)}, u32[]{:S(2)}) collective-permute-start(f32[416,128]{1,0:T(8,128)S(1)} %dynamic-slice_bitcast_fusion.3), channel_id=1, source_target_pairs={{0,8},{4,12},{8,0},{12,4},{16,24},{20,28},{24,16},{28,20},{1,9},{5... | collective-permute-start | bytes 638984 | tf_op jit(solution)/shard_map/cond/branch_1_fun/cond/branch_1_fun/ppermute | solution.py:822
  340.6 27.6 %collective-permute-start.13 = (f32[416,128]{1,0:T(8,128)S(1)}, f32[416,128]{1,0:T(8,128)S(1)}, u32[]{:S(2)}, u32[]{:S(2)}) collective-permute-start(f32[416,128]{1,0:T(8,128)S(1)} %dynamic-slice_bitcast_fusion.2), channel_id=1, source_target_pairs={{0,1},{1,0},{2,3},{3,2},{4,5},{5,4},{6,7},{7,6},{8,9},{9,8},{10,11... | collective-permute-start | bytes 638984 | tf_op jit(solution)/shard_map/cond/branch_1_fun/cond/branch_1_fun/ppermute | solution.py:822
  369.8 14.1 %collective-permute-start.14 = (f32[208,128]{1,0:T(8,128)S(1)}, f32[208,128]{1,0:T(8,128)S(1)}, u32[]{:S(2)}, u32[]{:S(2)}) collective-permute-start(f32[208,128]{1,0:T(8,128)S(1)} %dynamic-slice_bitcast_fusion.5), channel_id=1, source_target_pairs={{0,2},{1,3},{2,0},{3,1},{4,6},{5,7},{6,4},{7,5},{8,10},{9,11},{10,... | collective-permute-start | bytes 319496 | tf_op jit(solution)/shard_map/cond/branch_1_fun/cond/branch_1_fun/ppermute | solution.py:822
  384.9 6.0 %collective-permute-start.15 = (f32[208,128]{1,0:T(8,128)S(1)}, f32[208,128]{1,0:T(8,128)S(1)}, u32[]{:S(2)}, u32[]{:S(2)}) collective-permute-start(f32[208,128]{1,0:T(8,128)S(1)} %get-tuple-element.438), channel_id=1, source_target_pairs={{0,2},{1,3},{2,0},{3,1},{4,6},{5,7},{6,4},{7,5},{8,10},{9,11},{10,... | collective-permute-start | bytes 319496 | tf_op jit(solution)/shard_map/cond/branch_1_fun/cond/branch_1_fun/ppermute | solution.py:830
  391.0 6.6 %collective-permute-start.16 = (f32[416,128]{1,0:T(8,128)S(1)}, f32[416,128]{1,0:T(8,128)S(1)}, u32[]{:S(2)}, u32[]{:S(2)}) collective-permute-start(f32[416,128]{1,0:T(8,128)S(1)} %bitcast.97), channel_id=1, source_target_pairs={{0,1},{1,0},{2,3},{3,2},{4,5},{5,4},{6,7},{7,6},{8,9},{9,8},{10,11... | collective-permute-start | bytes 638984 | tf_op jit(solution)/shard_map/cond/branch_1_fun/cond/branch_1_fun/ppermute | solution.py:830
  398.3 48.7 %collective-permute-start.29 = (f32[16,64,512]{2,1,0:T(8,128)}, f32[16,64,512]{2,1,0:T(8,128)S(1)}, u32[]{:S(2)}, u32[]{:S(2)}) collective-permute-start(f32[16,64,512]{2,1,0:T(8,128)} %passed.9), channel_id=1, source_target_pairs={{1,0},{0,1},{5,2},{4,3},{3,4},{2,5},{7,6},{6,7},{9,8},{8,9},{13,10... | collective-permute-start | bytes 6291464 | tf_op jit(solution)/shard_map/ppermute | solution.py:753
  398.6 38.7 %all-gather.2.cloned.1.call-start = ((), (), s32[]{:S(2)}) async-start(), calls=%async_computation.3 | async-start | bytes 3833856 | tf_op jit(solution)/shard_map/cond/branch_1_fun/all_gather | solution.py:1023
  400.4 7.4 %collective-permute-start.17 = (f32[416,128]{1,0:T(8,128)S(1)}, f32[416,128]{1,0:T(8,128)S(1)}, u32[]{:S(2)}, u32[]{:S(2)}) collective-permute-start(f32[416,128]{1,0:T(8,128)S(1)} %get-tuple-element.439), channel_id=1, source_target_pairs={{0,16},{4,20},{8,24},{12,28},{16,0},{20,4},{24,8},{28,12},{1,17},{... | collective-permute-start | bytes 638984 | tf_op jit(solution)/shard_map/cond/branch_1_fun/cond/branch_1_fun/ppermute | solution.py:830
  402.0 7.8 %collective-permute-start.19 = (f32[416,128]{1,0:T(8,128)S(1)}, f32[416,128]{1,0:T(8,128)S(1)}, u32[]{:S(2)}, u32[]{:S(2)}) collective-permute-start(f32[416,128]{1,0:T(8,128)S(1)} %get-tuple-element.440), channel_id=1, source_target_pairs={{0,8},{4,12},{8,0},{12,4},{16,24},{20,28},{24,16},{28,20},{1,9},{5... | collective-permute-start | bytes 638984 | tf_op jit(solution)/shard_map/cond/branch_1_fun/cond/branch_1_fun/ppermute | solution.py:830
  407.8 16.0 %collective-permute-start.18 = (f32[832,128]{1,0:T(8,128)S(1)}, f32[832,128]{1,0:T(8,128)S(1)}, u32[]{:S(2)}, u32[]{:S(2)}) collective-permute-start(f32[832,128]{1,0:T(8,128)S(1)} %bitcast.87), channel_id=1, source_target_pairs={{0,8},{4,12},{8,0},{12,4},{16,24},{20,28},{24,16},{28,20},{1,9},{5... | collective-permute-start | bytes 1277960 | tf_op jit(solution)/shard_map/cond/branch_1_fun/cond/branch_1_fun/ppermute | solution.py:830
  409.9 15.3 %collective-permute-start.20 = (f32[832,128]{1,0:T(8,128)S(1)}, f32[832,128]{1,0:T(8,128)S(1)}, u32[]{:S(2)}, u32[]{:S(2)}) collective-permute-start(f32[832,128]{1,0:T(8,128)S(1)} %bitcast.89), channel_id=1, source_target_pairs={{0,16},{4,20},{8,24},{12,28},{16,0},{20,4},{24,8},{28,12},{1,17},{... | collective-permute-start | bytes 1277960 | tf_op jit(solution)/shard_map/cond/branch_1_fun/cond/branch_1_fun/ppermute | solution.py:830
  426.6 3.9 collective-permute-start.21
  (5 other events, 7.1 us)
Sparse Core Ops, SparseCore 0:
  243.7 47.1 reduce-scatter.1
  311.0 75.2 all-reduce.1
  401.3 35.9 all-gather.1
